TPU v7x, 32 devices: a whole 2x2x4 slice. The times are simulated.
32 devices in a mesh: cores: 4 (over y, x), strip: 8 (over z, core).
Axes of the slice: x: 2, y: 2, z: 4, core: 2. Of those that a mesh axis runs over, the one named last changes fastest.
Arguments:
- potentials: float32 [64, 256, 2048], P('cores', None, 'strip'), may hold values from -6 to 6
- pair_include: int32 [64, 64], replicated, may hold values 0 or 1
- labels: int32 [256, 2048], P('strip', 'cores'), may hold values from 0 to 127
- conduct_across: float32 [256, 2048], P('strip', 'cores'), may hold values from 0.1 to 10
- conduct_down: float32 [256, 2048], P('strip', 'cores'), may hold values from 0.1 to 10
Outputs:
- current_across: float32 [256, 2048], P('strip', 'cores')
- current_down: float32 [256, 2048], P('strip', 'cores')
Inputs may be any that keep to these rules, and one draw needn't show every extreme that they name: `labels`: a value below 64 names the core area that holds the cell; larger values mark cells outside every core area. `pair_include`: only entries above the diagonal are read.
All inputs are finite; a program needn't handle non-finite values.
Results may differ from a plain program's by a relative error of at most 0.00056.
Values may be sent and summed in bfloat16 or wider, within the bound.
No kernel may reach another device: no remote copies, remote signals or barrier semaphores. Data moves between devices by JAX's collectives and lax.ppermute only.
A program may use at most 64 MiB of HBM per device.

v0:
```python
import math

import jax
import jax.numpy as jnp
from jax import lax
from jax.sharding import PartitionSpec as P


def shifted(shard, axis, by):
    devices = lax.axis_size(axis)
    pairs = [(i, i + by) for i in range(devices) if 0 <= i + by < devices]
    return lax.ppermute(shard, axis, pairs)


def pair_currents(across_fields, down_fields, cell_labels, weights):
    field_count = across_fields.shape[0]
    cell_count = across_fields.shape[1] * across_fields.shape[2]
    flat_across = across_fields.reshape(field_count, cell_count)
    flat_down = down_fields.reshape(field_count, cell_count)
    labels_flat = cell_labels.reshape(cell_count)
    field_ids = jnp.arange(field_count, dtype=jnp.int32)
    other_keep = labels_flat[None, :] != field_ids[:, None]
    stride = math.gcd(field_count, 8)

    def accumulate(number, totals):
        offset = number * stride
        own_across = lax.dynamic_slice_in_dim(flat_across, offset, stride, 0).astype(jnp.float32)
        own_down = lax.dynamic_slice_in_dim(flat_down, offset, stride, 0).astype(jnp.float32)
        own_keep = lax.dynamic_slice_in_dim(other_keep, offset, stride, 0)
        pair_weight = lax.dynamic_slice_in_dim(weights, offset, stride, 0)
        factor = jnp.where(other_keep[None, :, :], pair_weight[:, :, None], 0.0)
        sum_across = jnp.sum(
            factor * jnp.abs(own_across[:, None, :] - flat_across[None, :, :].astype(jnp.float32)),
            axis=1,
        )
        sum_down = jnp.sum(
            factor * jnp.abs(own_down[:, None, :] - flat_down[None, :, :].astype(jnp.float32)),
            axis=1,
        )
        return (
            totals[0] + jnp.sum(jnp.where(own_keep, sum_across, 0.0), axis=0),
            totals[1] + jnp.sum(jnp.where(own_keep, sum_down, 0.0), axis=0),
        )

    empty_sum = jnp.zeros((cell_count,), jnp.float32)
    return lax.fori_loop(0, field_count // stride, accumulate, (empty_sum, empty_sum))


def local(potentials, pair_include, labels, conduct_across, conduct_down):
    strip_count = lax.axis_size("strip")
    field_groups, height, strip_width = potentials.shape
    last_band = lax.axis_index("strip") == strip_count - 1
    arriving = shifted(potentials[:, :, :1], "strip", -1)
    arriving = jnp.where(last_band, potentials[:, :, -1:], arriving)
    beside = jnp.concatenate([potentials[:, :, 1:], arriving], axis=2)
    sideways = (beside - potentials).astype(jnp.bfloat16)
    row_zeros = jnp.zeros((field_groups, 1, strip_width), jnp.float32)
    downward = jnp.concatenate(
        [potentials[:, 1:, :] - potentials[:, :-1, :], row_zeros], axis=1
    ).astype(jnp.bfloat16)
    across_fields, down_fields = (
        lax.all_to_all(
            lax.all_to_all(sideways, "strip", split_axis=1, concat_axis=2, tiled=True),
            "cores",
            split_axis=2,
            concat_axis=0,
            tiled=True,
        ),
        lax.all_to_all(
            lax.all_to_all(downward, "strip", split_axis=1, concat_axis=2, tiled=True),
            "cores",
            split_axis=2,
            concat_axis=0,
            tiled=True,
        ),
    )
    field_count = across_fields.shape[0]
    field_ids = jnp.arange(field_count, dtype=jnp.int32)
    weights = jnp.where(
        field_ids[None, :] > field_ids[:, None], pair_include.astype(jnp.float32), 0.0
    )
    total_across, total_down = pair_currents(across_fields, down_fields, labels, weights)
    scale = 2.0 / (field_count * (field_count - 1))
    row_count, column_count = labels.shape
    return (
        conduct_across * (total_across.reshape(row_count, column_count) * scale),
        conduct_down * (total_down.reshape(row_count, column_count) * scale),
    )


def solution(mesh):
    return jax.shard_map(
        local,
        mesh=mesh,
        in_specs=(
            P("cores", None, "strip"),
            P(),
            P("strip", "cores"),
            P("strip", "cores"),
            P("strip", "cores"),
        ),
        out_specs=(P("strip", "cores"), P("strip", "cores")),
        check_vma=False,
    )
```

profile of v0, /device:TPU:6, one launch (start us, length us, event | category | flops | bytes accessed | tf_op | source)
XLA Modules:
  0.0 339.2 jit_solution(16437005329076285749)
XLA Ops:
  0.6 4.6 %copy.32 = f32[16,256,256]{2,0,1:T(8,128)S(1)} copy(f32[16,256,256]{2,1,0:T(8,128)} %param.7) | data formatting | bytes 8388608 | tf_op args[0]
  8.7 4.9 %all-to-all-start.2 = ((bf16[16,256,256]{2,0,1:T(8,128)(2,1)}), bf16[16,256,256]{2,0,1:T(8,128)(2,1)S(1)}, u32[]{:S(2)}, u32[]{:S(2)}) async-start(bf16[16,256,256]{2,0,1:T(8,128)(2,1)} %concatenate.7), calls=%async_computation.2 | async-start | bytes 4194304 | tf_op jit(solution)/shard_map/all_to_all | solution.py:70
  13.6 4.8 %fusion.4 = (f32[16,256,1]{2,1,0:T(8,128)}, f32[16,256,1]{2,1,0:T(8,128)}) fusion(f32[16,256,256]{2,1,0:T(8,128)} %param.7), kind=kLoop, calls=%fused_computation.21 | loop fusion | bytes 65536 | tf_op jit(solution)/shard_map/slice | solution.py:53
  18.4 2.2 copy.56
  21.9 5.3 %slice.20 = f32[16,256,255]{2,0,1:T(8,128)} slice(f32[16,256,256]{2,0,1:T(8,128)} %copy-done.2), slice={[0:16], [0:256], [1:256]} | slice | bytes 8355840 | tf_op jit(solution)/shard_map/slice | solution.py:55
  27.2 2.2 copy.55
  29.5 2.4 copy.35
  31.9 8.0 %fusion.2 = bf16[16,256,256]{2,0,1:T(8,128)(2,1)} fusion(f32[16,256,1]{2,0,1:T(8,128)} %copy.35, f32[16,256,255]{2,0,1:T(8,128)} %slice.20, f32[16,256,256]{2,1,0:T(8,128)} %param.7), kind=kLoop, calls=%fused_computation.12 | loop fusion | flops 3145728 | bytes 10485760 | tf_op jit(solution)/shard_map/convert_element_type | solution.py:56
  39.8 22.8 %all-to-all-done.2 = bf16[16,256,256]{2,0,1:T(8,128)(2,1)S(1)} async-done(((bf16[16,256,256]{2,0,1:T(8,128)(2,1)}), bf16[16,256,256]{2,0,1:T(8,128)(2,1)S(1)}, u32[]{:S(2)}, u32[]{:S(2)}) %all-to-all-start.2) | async-done | bytes 2097184 | tf_op jit(solution)/shard_map/all_to_all | solution.py:70
  62.6 11.8 %all-to-all-start = ((bf16[16,256,256]{2,0,1:T(8,128)(2,1)}), bf16[16,256,256]{2,0,1:T(8,128)(2,1)}, u32[]{:S(2)}, u32[]{:S(2)}) async-start(bf16[16,256,256]{2,0,1:T(8,128)(2,1)} %fusion.2), calls=%async_computation | async-start | bytes 4194304 | tf_op jit(solution)/shard_map/all_to_all | solution.py:63
  74.5 9.1 %copy.51 = bf16[16,32,8,256]{1,0,3,2:T(8,128)(2,1)} copy(bf16[16,32,8,256]{3,0,1,2:T(8,128)(2,1)S(1)} %bitcast.54) | data formatting | bytes 4194304 | tf_op jit(solution)/shard_map/all_to_all | solution.py:70
  83.6 10.5 %reshape.53 = bf16[4,2,131072]{2,1,0:T(2,128)(2,1)} reshape(bf16[2048,16,32]{2,1,0:T(8,128)(2,1)} %bitcast.50) | data formatting | bytes 4194304
  94.1 29.5 %all-to-all-done = bf16[16,256,256]{2,0,1:T(8,128)(2,1)} async-done(((bf16[16,256,256]{2,0,1:T(8,128)(2,1)}), bf16[16,256,256]{2,0,1:T(8,128)(2,1)}, u32[]{:S(2)}, u32[]{:S(2)}) %all-to-all-start) | async-done | bytes 2097184 | tf_op jit(solution)/shard_map/all_to_all | solution.py:63
  123.6 4.2 %all-to-all-start.3 = ((bf16[4,2,131072]{2,1,0:T(2,128)(2,1)}), bf16[4,2,131072]{2,1,0:T(2,128)(2,1)S(1)}, u32[]{:S(2)}, u32[]{:S(2)}) async-start(bf16[4,2,131072]{2,1,0:T(2,128)(2,1)} %reshape.53), calls=%async_computation.3 | async-start | bytes 4194304 | tf_op jit(solution)/shard_map/all_to_all | solution.py:69
  127.8 12.9 %copy.49 = bf16[16,32,8,256]{1,0,3,2:T(8,128)(2,1)} copy(bf16[16,32,8,256]{3,0,1,2:T(8,128)(2,1)} %bitcast.12) | data formatting | bytes 4194304 | tf_op jit(solution)/shard_map/all_to_all | solution.py:63
  140.7 10.5 %reshape.51 = bf16[4,2,131072]{2,1,0:T(2,128)(2,1)} reshape(bf16[2048,16,32]{2,1,0:T(8,128)(2,1)} %bitcast.51) | data formatting | bytes 4194304
  151.2 5.8 %all-to-all-start.1 = ((bf16[4,2,131072]{2,1,0:T(2,128)(2,1)}), bf16[4,2,131072]{2,1,0:T(2,128)(2,1)}, u32[]{:S(2)}, u32[]{:S(2)}) async-start(bf16[4,2,131072]{2,1,0:T(2,128)(2,1)} %reshape.51), calls=%async_computation.1 | async-start | bytes 4194304 | tf_op jit(solution)/shard_map/all_to_all | solution.py:62
  157.7 5.6 %reshape.54 = bf16[2048,16,32]{2,1,0:T(8,128)(2,1)} reshape(bf16[4,2,131072]{2,1,0:T(2,128)(2,1)S(1)} %all-to-all-done.3) | data formatting | bytes 4194304
  163.3 10.0 %copy.52 = bf16[16,32,4,512]{3,2,1,0:T(4,128)(2,1)} copy(bf16[16,32,4,512]{1,0,3,2:T(8,128)(2,1)} %bitcast.52) | data formatting | bytes 4194304 | tf_op jit(solution)/shard_map/all_to_all | solution.py:69
  175.3 2.6 copy.61
  180.0 7.4 %reshape.52 = bf16[2048,16,32]{2,1,0:T(8,128)(2,1)} reshape(bf16[4,2,131072]{2,1,0:T(2,128)(2,1)} %all-to-all-done.1) | data formatting | bytes 4194304
  187.4 9.9 %copy.50 = bf16[16,32,4,512]{3,2,1,0:T(4,128)(2,1)} copy(bf16[16,32,4,512]{1,0,3,2:T(8,128)(2,1)} %bitcast.53) | data formatting | bytes 4194304 | tf_op jit(solution)/shard_map/all_to_all | solution.py:62
  199.4 2.6 copy.60
  202.0 135.0 %while.16 = (s32[]{:T(128)}, f32[16384]{0:T(1024)S(1)}, f32[16384]{0:T(1024)S(1)}, pred[64,16384]{1,0:T(8,128)(4,1)S(1)}, f32[64,64]{1,0:T(8,128)S(1)}, /*index=...) while((s32[]{:T(128)}, f32[16384]{0:T(1024)S(1)}, ...), condition=%wide.region_5.6_spmd.clone, body=%wide.region_0.5_spmd.clone.sunk | while | flops 76054536 | bytes 35789020 | solution.py:46
  205.8 12.6 %fusion.6 = (f32[8,16384]{1,0:T(8,128)S(1)}, f32[8,16384]{1,0:T(8,128)S(1)}) fusion(f32[64,16384]{1,0:T(8,128)S(1)} %bitcast.42, f32[8,16384]{1,0:T(8,128)S(1)} %get-tuple-element.278, f32[8,64]{1,0:T(8,128)S(1)} %constant_dynamic-slice_fusion.2, pred[64,16384]{1,0:T(8,128)(4,1)S(1)} %get-tuple-element.313, f32[64,16384]{1,0:T(8,128)S(1)} %bitcast.43, ...), kind=kLoop, calls=%fused_computation.3.clone.1 | loop fusion | flops 75235328 | bytes 11536384 | tf_op jit(solution)/shard_map/while/body/eval_jaxpr/reduce_sum | solution.py:36
  222.7 12.6 %fusion.6 = (f32[8,16384]{1,0:T(8,128)S(1)}, f32[8,16384]{1,0:T(8,128)S(1)}) fusion(f32[64,16384]{1,0:T(8,128)S(1)} %bitcast.42, f32[8,16384]{1,0:T(8,128)S(1)} %get-tuple-element.278, f32[8,64]{1,0:T(8,128)S(1)} %constant_dynamic-slice_fusion.2, pred[64,16384]{1,0:T(8,128)(4,1)S(1)} %get-tuple-element.313, f32[64,16384]{1,0:T(8,128)S(1)} %bitcast.43, ...), kind=kLoop, calls=%fused_computation.3.clone.1 | loop fusion | flops 75235328 | bytes 11536384 | tf_op jit(solution)/shard_map/while/body/eval_jaxpr/reduce_sum | solution.py:36
  239.6 12.6 %fusion.6 = (f32[8,16384]{1,0:T(8,128)S(1)}, f32[8,16384]{1,0:T(8,128)S(1)}) fusion(f32[64,16384]{1,0:T(8,128)S(1)} %bitcast.42, f32[8,16384]{1,0:T(8,128)S(1)} %get-tuple-element.278, f32[8,64]{1,0:T(8,128)S(1)} %constant_dynamic-slice_fusion.2, pred[64,16384]{1,0:T(8,128)(4,1)S(1)} %get-tuple-element.313, f32[64,16384]{1,0:T(8,128)S(1)} %bitcast.43, ...), kind=kLoop, calls=%fused_computation.3.clone.1 | loop fusion | flops 75235328 | bytes 11536384 | tf_op jit(solution)/shard_map/while/body/eval_jaxpr/reduce_sum | solution.py:36
  256.5 12.6 %fusion.6 = (f32[8,16384]{1,0:T(8,128)S(1)}, f32[8,16384]{1,0:T(8,128)S(1)}) fusion(f32[64,16384]{1,0:T(8,128)S(1)} %bitcast.42, f32[8,16384]{1,0:T(8,128)S(1)} %get-tuple-element.278, f32[8,64]{1,0:T(8,128)S(1)} %constant_dynamic-slice_fusion.2, pred[64,16384]{1,0:T(8,128)(4,1)S(1)} %get-tuple-element.313, f32[64,16384]{1,0:T(8,128)S(1)} %bitcast.43, ...), kind=kLoop, calls=%fused_computation.3.clone.1 | loop fusion | flops 75235328 | bytes 11536384 | tf_op jit(solution)/shard_map/while/body/eval_jaxpr/reduce_sum | solution.py:36
  273.4 12.6 %fusion.6 = (f32[8,16384]{1,0:T(8,128)S(1)}, f32[8,16384]{1,0:T(8,128)S(1)}) fusion(f32[64,16384]{1,0:T(8,128)S(1)} %bitcast.42, f32[8,16384]{1,0:T(8,128)S(1)} %get-tuple-element.278, f32[8,64]{1,0:T(8,128)S(1)} %constant_dynamic-slice_fusion.2, pred[64,16384]{1,0:T(8,128)(4,1)S(1)} %get-tuple-element.313, f32[64,16384]{1,0:T(8,128)S(1)} %bitcast.43, ...), kind=kLoop, calls=%fused_computation.3.clone.1 | loop fusion | flops 75235328 | bytes 11536384 | tf_op jit(solution)/shard_map/while/body/eval_jaxpr/reduce_sum | solution.py:36
  290.2 12.6 %fusion.6 = (f32[8,16384]{1,0:T(8,128)S(1)}, f32[8,16384]{1,0:T(8,128)S(1)}) fusion(f32[64,16384]{1,0:T(8,128)S(1)} %bitcast.42, f32[8,16384]{1,0:T(8,128)S(1)} %get-tuple-element.278, f32[8,64]{1,0:T(8,128)S(1)} %constant_dynamic-slice_fusion.2, pred[64,16384]{1,0:T(8,128)(4,1)S(1)} %get-tuple-element.313, f32[64,16384]{1,0:T(8,128)S(1)} %bitcast.43, ...), kind=kLoop, calls=%fused_computation.3.clone.1 | loop fusion | flops 75235328 | bytes 11536384 | tf_op jit(solution)/shard_map/while/body/eval_jaxpr/reduce_sum | solution.py:36
  307.1 12.6 %fusion.6 = (f32[8,16384]{1,0:T(8,128)S(1)}, f32[8,16384]{1,0:T(8,128)S(1)}) fusion(f32[64,16384]{1,0:T(8,128)S(1)} %bitcast.42, f32[8,16384]{1,0:T(8,128)S(1)} %get-tuple-element.278, f32[8,64]{1,0:T(8,128)S(1)} %constant_dynamic-slice_fusion.2, pred[64,16384]{1,0:T(8,128)(4,1)S(1)} %get-tuple-element.313, f32[64,16384]{1,0:T(8,128)S(1)} %bitcast.43, ...), kind=kLoop, calls=%fused_computation.3.clone.1 | loop fusion | flops 75235328 | bytes 11536384 | tf_op jit(solution)/shard_map/while/body/eval_jaxpr/reduce_sum | solution.py:36
  324.0 12.6 %fusion.6 = (f32[8,16384]{1,0:T(8,128)S(1)}, f32[8,16384]{1,0:T(8,128)S(1)}) fusion(f32[64,16384]{1,0:T(8,128)S(1)} %bitcast.42, f32[8,16384]{1,0:T(8,128)S(1)} %get-tuple-element.278, f32[8,64]{1,0:T(8,128)S(1)} %constant_dynamic-slice_fusion.2, pred[64,16384]{1,0:T(8,128)(4,1)S(1)} %get-tuple-element.313, f32[64,16384]{1,0:T(8,128)S(1)} %bitcast.43, ...), kind=kLoop, calls=%fused_computation.3.clone.1 | loop fusion | flops 75235328 | bytes 11536384 | tf_op jit(solution)/shard_map/while/body/eval_jaxpr/reduce_sum | solution.py:36
  (101 shorter events, 47.2 us)
Async XLA Ops:
  5.3 1.9 copy-start.2
  8.7 53.9 %all-to-all-start.2 = ((bf16[16,256,256]{2,0,1:T(8,128)(2,1)}), bf16[16,256,256]{2,0,1:T(8,128)(2,1)S(1)}, u32[]{:S(2)}, u32[]{:S(2)}) async-start(bf16[16,256,256]{2,0,1:T(8,128)(2,1)} %concatenate.7), calls=%async_computation.2 | async-start | bytes 4194304 | tf_op jit(solution)/shard_map/all_to_all | solution.py:70
  20.6 8.8 %collective-permute-start = (f32[16,256,1]{1,0,2:T(8,128)S(1)}, f32[16,256,1]{1,0,2:T(8,128)S(1)}, u32[]{:S(2)}, u32[]{:S(2)}) collective-permute-start(f32[16,256,1]{1,0,2:T(8,128)S(1)} %copy.56), channel_id=1, source_target_pairs={{1,0},{2,1},{3,2},{4,3},{5,4},{6,5},{7,6},{9,8},{10,9},{11,10},{12... | collective-permute-start | bytes 49160 | tf_op jit(solution)/shard_map/ppermute | solution.py:12
  62.6 61.0 %all-to-all-start = ((bf16[16,256,256]{2,0,1:T(8,128)(2,1)}), bf16[16,256,256]{2,0,1:T(8,128)(2,1)}, u32[]{:S(2)}, u32[]{:S(2)}) async-start(bf16[16,256,256]{2,0,1:T(8,128)(2,1)} %fusion.2), calls=%async_computation | async-start | bytes 4194304 | tf_op jit(solution)/shard_map/all_to_all | solution.py:63
  94.1 33.7 %copy-start.4 = (s32[32,512]{1,0:T(8,128)S(1)}, s32[32,512]{1,0:T(8,128)}, u32[]{:S(2)}) copy-start(s32[32,512]{1,0:T(8,128)} %param.9) | copy-start | bytes 196612
  123.6 27.6 %all-to-all-start.3 = ((bf16[4,2,131072]{2,1,0:T(2,128)(2,1)}), bf16[4,2,131072]{2,1,0:T(2,128)(2,1)S(1)}, u32[]{:S(2)}, u32[]{:S(2)}) async-start(bf16[4,2,131072]{2,1,0:T(2,128)(2,1)} %reshape.53), calls=%async_computation.3 | async-start | bytes 4194304 | tf_op jit(solution)/shard_map/all_to_all | solution.py:69
  151.2 6.4 %copy-start.5 = (s32[64,64]{1,0:T(8,128)S(1)}, s32[64,64]{1,0:T(8,128)}, u32[]{:S(2)}) copy-start(s32[64,64]{1,0:T(8,128)} %param.8) | copy-start | bytes 49156
  151.2 28.7 %all-to-all-start.1 = ((bf16[4,2,131072]{2,1,0:T(2,128)(2,1)}), bf16[4,2,131072]{2,1,0:T(2,128)(2,1)}, u32[]{:S(2)}, u32[]{:S(2)}) async-start(bf16[4,2,131072]{2,1,0:T(2,128)(2,1)} %reshape.51), calls=%async_computation.1 | async-start | bytes 4194304 | tf_op jit(solution)/shard_map/all_to_all | solution.py:62
  199.4 2.6 copy-start
  202.0 135.1 %copy-start.3 = (f32[32,512]{1,0:T(8,128)S(1)}, f32[32,512]{1,0:T(8,128)}, u32[]{:S(2)}) copy-start(f32[32,512]{1,0:T(8,128)} %param.10) | copy-start | bytes 196612
  202.0 2.6 copy-start.1
  218.8 2.6 copy-start.1
  235.7 2.6 copy-start.1
  252.6 2.6 copy-start.1
  269.5 2.6 copy-start.1
  286.4 2.6 copy-start.1
  303.3 2.6 copy-start.1
  320.1 2.6 copy-start.1
where the time goes:
time: 343 us; the launch traced here: 339 us
  local copies, waits for them, and re-layouts  130 us (38%)
  other arithmetic  125 us (36%)
  waiting for transfers between devices  54.5 us (16%)
  starting transfers between devices  28 us (8%)
    reduce_sum x8, other arithmetic, accumulate(): jnp.sum(factor * jnp.abs(own_down[:, None, :] - flat_down[None, :, :].ast...  101 us
    unnamed x20, local copies, waits for them, and re-layouts  49.6 us
    all_to_all x1, waiting for transfers between devices, local(): lax.all_to_all(sideways, 'strip', split_axis=1, concat_axis=2, tiled=True)  29.5 us
    all_to_all x1, waiting for transfers between devices, local(): lax.all_to_all(downward, 'strip', split_axis=1, concat_axis=2, tiled=True)  22.8 us
    while x32, local copies, waits for them, and re-layouts  20.5 us
    all_to_all x1, local copies, waits for them, and re-layouts, local(): lax.all_to_all(sideways, 'strip', split_axis=1, concat_axis=2, tiled=True)  12.9 us
    all_to_all x2, local copies, waits for them, and re-layouts, local(): lax.all_to_all(lax.all_to_all(downward, 'strip', split_axis=1, concat_axi...  12 us
    all_to_all x2, local copies, waits for them, and re-layouts, local(): lax.all_to_all(lax.all_to_all(sideways, 'strip', split_axis=1, concat_axi...  12 us
  transfers between devices with their start and end apart: 5, of which 3 were waited for; matrix products, arithmetic and copies ran while one was open for 26% of the time, Pallas kernels for 0%

commit v1 on v0

v1 whole, which is shorter than its diff:
```python
import functools

import jax
import jax.numpy as jnp
from jax import lax
from jax.experimental import pallas as pl
from jax.experimental.pallas import tpu as pltpu
from jax.sharding import PartitionSpec as P

PARTNERS = 4
LOW = -64.0
LANES = 128
VMEM = pl.BlockSpec(memory_space=pltpu.VMEM)
SMEM = pl.BlockSpec(memory_space=pltpu.SMEM)
LIMIT = pltpu.CompilerParams(vmem_limit_bytes=32 * 2**20)


def prepare_kernel(include_ref, groups_ref, linear_ref):
    fields = include_ref.shape[0]
    slots = groups_ref.shape[1]
    f32 = jnp.float32

    def dot(a, b, over):
        return lax.dot_general(
            a.astype(jnp.bfloat16),
            b.astype(jnp.bfloat16),
            ((over[:1], over[1:]), ((), ())),
            preferred_element_type=f32,
        )

    row = lax.broadcasted_iota(jnp.int32, (fields, fields), 0)
    column = lax.broadcasted_iota(jnp.int32, (fields, fields), 1)
    upper = jnp.where(column > row, 1.0, 0.0)
    lower = jnp.where(column < row, 1.0, 0.0)
    eye = jnp.where(column == row, 1.0, 0.0)
    included = jnp.where(column > row, include_ref[...], 0).astype(f32)
    place = dot(included, upper, (1, 0))
    both = included + dot(included, eye, (0, 0))
    count = jnp.sum(included, axis=1, keepdims=True)
    degree = jnp.sum(both, axis=1, keepdims=True)
    groups = jnp.floor((count + (PARTNERS - 1)) * (1.0 / PARTNERS))
    start = dot(lower, jnp.broadcast_to(groups, (fields, LANES)), (1, 0))[:, :1]
    total = jnp.sum(groups, axis=0, keepdims=True)
    slot = lax.broadcasted_iota(jnp.int32, (fields, slots), 1).astype(f32)
    ids = lax.broadcasted_iota(jnp.int32, (fields, slots), 0).astype(f32)
    inside = jnp.where((slot >= start) & (slot < start + groups), 1.0, 0.0)
    used = jnp.sum(inside, axis=0, keepdims=True)
    own = jnp.sum(inside * ids, axis=0, keepdims=True)
    first = jnp.sum(inside * (slot - start) * PARTNERS, axis=0, keepdims=True)
    places = dot(jnp.where(included > 0, place, -8.0), inside, (0, 0))
    places = jnp.where(used > 0, places, -8.0)
    groups_ref[...] = jnp.zeros(groups_ref.shape, jnp.int32)
    for u in range(PARTNERS):
        hit = jnp.where(places == first + u, 1.0, 0.0)
        found = jnp.sum(hit, axis=0, keepdims=True)
        partner = jnp.sum(hit * ids, axis=0, keepdims=True)
        absent = jnp.where(used > 0, float(fields), float(fields + 1))
        groups_ref[u : u + 1, :] = jnp.where(found > 0, partner, absent).astype(jnp.int32)
    owner = jnp.where(used > 0, own, float(fields + 1))
    groups_ref[PARTNERS : PARTNERS + 1, :] = owner.astype(jnp.int32)
    groups_ref[PARTNERS + 1 : PARTNERS + 2, :] = jnp.broadcast_to(total, (1, slots)).astype(
        jnp.int32
    )
    lanes = linear_ref.shape[1]
    padding = 2.0 * (groups * PARTNERS - count)
    wide = jnp.concatenate([both, jnp.zeros((fields, lanes - fields), f32)], axis=1)
    row = lax.broadcasted_iota(jnp.int32, (fields, lanes), 0)
    column = lax.broadcasted_iota(jnp.int32, (fields, lanes), 1)
    linear_ref[...] = jnp.where(row == column, 0.0, degree + wide) + padding


def prepare(pair_include):
    fields = pair_include.shape[0]
    most = sum(pl.cdiv(fields - 1 - a, PARTNERS) for a in range(fields))
    slots = pl.cdiv(most + 8, LANES) * LANES
    groups, linear = pl.pallas_call(
        prepare_kernel,
        out_shape=(
            jax.ShapeDtypeStruct((8, slots), jnp.int32),
            jax.ShapeDtypeStruct((fields, LANES), jnp.float32),
        ),
        compiler_params=LIMIT,
        name="prepare",
    )(pair_include)
    return groups.T.reshape(-1), linear


def pairs_kernel(base_ref, groups_ref, *refs, scale, unroll):
    *parts, labels_ref, linear_ref, out_ref, held = refs
    fields = linear_ref.shape[0]
    each = parts[0].shape[0]
    rows, width = out_ref.shape
    labels = labels_ref[...]
    held[fields] = jnp.full((rows, width), LOW, jnp.float32)
    held[fields + 1] = jnp.zeros((rows, width), jnp.float32)
    linear = jnp.zeros((rows, width), jnp.float32)
    for k, part in enumerate(parts):
        for i in range(each):
            field = base_ref[k] + i
            values = jnp.where(labels == field, LOW, part[i].astype(jnp.float32))
            held[field] = values
            table = jnp.broadcast_to(linear_ref[pl.ds(field, 1), :], (rows, LANES))
            factor = jnp.concatenate(
                [
                    jnp.take_along_axis(table, labels[:, at : at + LANES], axis=1)
                    for at in range(0, width, LANES)
                ],
                axis=1,
            )
            linear = linear + factor * values

    def step(number, total):
        for v in range(unroll):
            at = (number * unroll + v) * 8
            own = held[groups_ref[at + PARTNERS]]
            for u in range(PARTNERS):
                total = total + jnp.maximum(own, held[groups_ref[at + u]])
        return total

    steps = (groups_ref[PARTNERS + 1] + (unroll - 1)) // unroll
    total = lax.fori_loop(0, steps, step, jnp.zeros((rows, width), jnp.float32))
    out_ref[...] = (2.0 * total - linear) * scale


def pairs(base, groups, parts, labels, linear):
    fields = linear.shape[0]
    work = fields * fields * labels.size
    return pl.pallas_call(
        functools.partial(pairs_kernel, scale=2.0 / (fields * (fields - 1)), unroll=8),
        in_specs=[SMEM, SMEM] + [VMEM] * (len(parts) + 2),
        out_specs=VMEM,
        out_shape=jax.ShapeDtypeStruct(labels.shape, jnp.float32),
        scratch_shapes=[pltpu.VMEM((fields + 2, *labels.shape), jnp.float32)],
        compiler_params=LIMIT,
        cost_estimate=pl.CostEstimate(flops=work, bytes_accessed=work // 16, transcendentals=0),
        name="pairs",
    )(base, groups, *parts, labels, linear)


def down_kernel(spots_ref, *refs, count, last):
    mains, nexts, outs = refs[:count], refs[count : 2 * count], refs[2 * count :]
    for k in range(count):
        each, rows, width = outs[k].shape
        at_end = spots_ref[k] == last
        row = lax.broadcasted_iota(jnp.int32, (rows, width), 0)
        for i in range(each):
            here = mains[k][i]
            below = jnp.concatenate([here[1:], nexts[k][i, 0:1, :]], axis=0)
            change = jnp.where((row == rows - 1) & at_end, 0.0, below - here)
            outs[k][i] = change.astype(jnp.bfloat16)


def side_kernel(spots_ref, *refs, count):
    mains, besides, outs = refs[:count], refs[count : 2 * count], refs[2 * count :]
    at_end = spots_ref[count] == 1
    for k in range(count):
        each, rows, width = outs[k].shape
        lane = lax.broadcasted_iota(jnp.int32, (rows, width), 1)
        for i in range(each):
            here = mains[k][i]
            right = jnp.where(
                lane == width - 1, besides[k][:, i : i + 1], pltpu.roll(here, width - 1, 1)
            )
            change = jnp.where((lane == width - 1) & at_end, 0.0, right - here)
            outs[k][i] = change.astype(jnp.bfloat16)


def differences(kind, potentials, beside, spots, last_strip, rows):
    each, height, width = potentials.shape
    count = spots.shape[0]

    def main_spec(k):
        return pl.BlockSpec((each, rows, width), lambda i, at: (0, at[k], 0))

    if kind == "down":

        def next_spec(k):
            return pl.BlockSpec(
                (each, 8, width),
                lambda i, at: (0, jnp.minimum((at[k] + 1) * (rows // 8), height // 8 - 1), 0),
            )

        other, specs = potentials, [next_spec(k) for k in range(count)]
        body = functools.partial(down_kernel, count=count, last=height // rows - 1)
    else:

        def beside_spec(k):
            return pl.BlockSpec((rows, LANES), lambda i, at: (at[k], 0))

        other, specs = beside, [beside_spec(k) for k in range(count)]
        body = functools.partial(side_kernel, count=count)
    scalars = jnp.concatenate([spots, last_strip.astype(jnp.int32)[None]])
    return pl.pallas_call(
        body,
        grid_spec=pltpu.PrefetchScalarGridSpec(
            num_scalar_prefetch=1,
            grid=(1,),
            in_specs=[main_spec(k) for k in range(count)] + specs,
            out_specs=[pl.BlockSpec((each, rows, width), lambda i, at: (0, 0, 0))] * count,
        ),
        out_shape=[jax.ShapeDtypeStruct((each, rows, width), jnp.bfloat16)] * count,
        compiler_params=LIMIT,
        cost_estimate=pl.CostEstimate(
            flops=4 * count * each * rows * width,
            bytes_accessed=6 * count * each * rows * width,
            transcendentals=0,
        ),
        name=kind,
    )(scalars, *([potentials] * count), *([other] * count))


def edge_kernel(potentials_ref, out_ref):
    each, rows, _ = potentials_ref.shape
    lane = lax.broadcasted_iota(jnp.int32, (rows, LANES), 1)
    edge = jnp.zeros((rows, LANES), jnp.float32)
    for i in range(each):
        edge = jnp.where(lane == i, potentials_ref[i][:, 0:1], edge)
    out_ref[...] = edge


def first_columns(potentials):
    each, height, _ = potentials.shape
    rows = 64
    return pl.pallas_call(
        edge_kernel,
        grid=(height // rows,),
        in_specs=[pl.BlockSpec((each, rows, LANES), lambda i: (0, i, 0))],
        out_specs=pl.BlockSpec((rows, LANES), lambda i: (i, 0)),
        out_shape=jax.ShapeDtypeStruct((height, LANES), jnp.float32),
        compiler_params=LIMIT,
        name="edge",
    )(potentials)


def finish_kernel(halves_ref, *refs, chunks, width):
    pieces, (across, down, out_across, out_down) = refs[: len(chunks)], refs[len(chunks) :]
    for (kind, turn, first, rows), piece in zip(chunks, pieces):
        conduct, out = (down, out_down) if kind == "down" else (across, out_across)
        lanes = pl.ds(pl.multiple_of(halves_ref[turn] * width, width), width)
        out[first : first + rows, lanes] = conduct[first : first + rows, lanes] * piece[...]


def finish(chunks, halves, pieces, conduct_across, conduct_down):
    shape = jax.ShapeDtypeStruct(conduct_across.shape, jnp.float32)
    return pl.pallas_call(
        functools.partial(finish_kernel, chunks=chunks, width=pieces[0].shape[1]),
        in_specs=[SMEM] + [VMEM] * (len(pieces) + 2),
        out_specs=[VMEM, VMEM],
        out_shape=[shape, shape],
        compiler_params=LIMIT,
        name="finish",
    )(halves, *pieces, conduct_across, conduct_down)


def local(potentials, pair_include, labels, conduct_across, conduct_down):
    groups_of, strips = lax.axis_size("cores"), lax.axis_size("strip")
    core, strip = lax.axis_index("cores"), lax.axis_index("strip")
    each, height, width = potentials.shape
    band_rows = labels.shape[0]
    turns = strips // groups_of
    paired = groups_of & (groups_of - 1) == 0

    def towards(index, k):
        return index ^ k if paired else (index + k) % groups_of

    def source(index, k):
        return index ^ k if paired else (index + groups_of - k) % groups_of

    def moves(turn, home):
        out = []
        for c in range(groups_of):
            for s in range(strips):
                band = c * turns + (s + turn) % turns
                here, there = c * strips + s, (s // turns) * strips + band
                out.append((here, there) if home else (there, here))
        return out

    chunks = [
        (kind, turn, 0, band_rows) for kind in ("down", "side") for turn in range(turns)
    ]
    base = jnp.stack([source(core, k) * each for k in range(groups_of)]).astype(jnp.int32)
    halves = jnp.stack([(strip + turns - t % turns) % turns for t in range(turns)]).astype(
        jnp.int32
    )
    last_strip = strip == strips - 1

    def spots(turn, first, rows):
        band = [towards(core, k) * turns + (strip + turn) % turns for k in range(groups_of)]
        return (jnp.stack(band) * (band_rows // rows) + first // rows).astype(jnp.int32)

    def exchange(kind, turn, first, rows, beside):
        blocks = differences(
            kind, potentials, beside, spots(turn, first, rows), last_strip, rows
        )
        return [blocks[0]] + [
            lax.ppermute(
                blocks[k], "cores", [(i, towards(i, k)) for i in range(groups_of)]
            )
            for k in range(1, groups_of)
        ]

    beside = lax.ppermute(
        first_columns(potentials), "strip", [(i, i - 1) for i in range(1, strips)]
    )
    own_labels = []
    for turn in range(turns):
        half = lax.dynamic_slice_in_dim(labels, halves[turn] * width, width, 1)
        own_labels.append(lax.ppermute(half, ("cores", "strip"), moves(turn, False)))
    groups, linear = prepare(pair_include)
    pieces = []
    for kind, turn, first, rows in chunks:
        parts = exchange(kind, turn, first, rows, beside)
        sums = pairs(
            base, groups, parts, own_labels[turn][first : first + rows], linear
        )
        pieces.append(lax.ppermute(sums, ("cores", "strip"), moves(turn, True)))
    return finish(chunks, halves, pieces, conduct_across, conduct_down)


def solution(mesh):
    return jax.shard_map(
        local,
        mesh=mesh,
        in_specs=(
            P("cores", None, "strip"),
            P(),
            P("strip", "cores"),
            P("strip", "cores"),
            P("strip", "cores"),
        ),
        out_specs=(P("strip", "cores"), P("strip", "cores")),
        check_vma=False,
    )
```

time: 343 us -> 102 us (0.30)
  other arithmetic: 125 us -> 0.15 us
  local copies, waits for them, and re-layouts: 130 us -> 12.5 us
  waiting for transfers between devices: 54.5 us -> 18.2 us
  Pallas kernels: 0 us -> 34.1 us
  starting transfers between devices: 28 us -> 35.3 us
    reduce_sum x16 -> x0, other arithmetic: 103 us -> none  [the longest x8 101 us: accumulate(): jnp.sum(factor * jnp.abs(own_down[:, None, :] - flat_down[None, :, :].ast...]
    all_to_all x4 -> x0, waiting for transfers between devices: 54.5 us -> none  [the longest x1 29.5 us: local(): lax.all_to_all(sideways, 'strip', split_axis=1, concat_axis=2, tiled=True)]
    all_to_all x6 -> x0, local copies, waits for them, and re-layouts: 46 us -> none  [the longest x1 12.9 us: local(): lax.all_to_all(sideways, 'strip', split_axis=1, concat_axis=2, tiled=True)]
    unnamed x20 -> x24, local copies, waits for them, and re-layouts: 49.6 us -> 10.2 us
    pallas_call x0 -> x11, Pallas kernels: none -> 34.1 us  [the longest x4 24.9 us: pairs(): pl.pallas_call(functools.partial(pairs_kernel, scale=2.0 / (fields * (fie...]
    ppermute x1 -> x19, starting transfers between devices: 1.29 us -> 35.3 us  [the longest x4 14.9 us: local(): pieces.append(lax.ppermute(sums, ('cores', 'strip'), moves(turn, True)))]
    all_to_all x4 -> x0, starting transfers between devices: 26.7 us -> none  [the longest x1 11.8 us: local(): lax.all_to_all(sideways, 'strip', split_axis=1, concat_axis=2, tiled=True)]
    while x32 -> x0, local copies, waits for them, and re-layouts: 20.5 us -> none
  transfers between devices with their start and end apart: 5 -> 19, of which waited for: 3 -> 7; matrix products, arithmetic and copies ran while one was open for 26% -> 2% of each run, Pallas kernels for 0% -> 32%
where the time goes in v1:
time: 102 us; the launch traced here: 101 us
  starting transfers between devices  35.3 us (35%)
  Pallas kernels  34.1 us (33%)
  waiting for transfers between devices  18.2 us (18%)
  local copies, waits for them, and re-layouts  12.5 us (12%)
    pallas_call x4, Pallas kernels, pairs(): pl.pallas_call(functools.partial(pairs_kernel, scale=2.0 / (fields * (fie...  24.9 us
    ppermute x4, starting transfers between devices, local(): pieces.append(lax.ppermute(sums, ('cores', 'strip'), moves(turn, True)))  14.9 us
    ppermute x12, starting transfers between devices, exchange(): lax.ppermute(blocks[k], 'cores', [(i, towards(i, k)) for i in range(group...  10.7 us
    unnamed x24, local copies, waits for them, and re-layouts  10.2 us
    ppermute x12, waiting for transfers between devices, exchange(): lax.ppermute(blocks[k], 'cores', [(i, towards(i, k)) for i in range(group...  10.1 us
    ppermute x2, starting transfers between devices, local(): lax.ppermute(half, ('cores', 'strip'), moves(turn, False))  8.31 us
    ppermute x4, waiting for transfers between devices, local(): pieces.append(lax.ppermute(sums, ('cores', 'strip'), moves(turn, True)))  7.06 us
    pallas_call x4, Pallas kernels, differences(): pl.pallas_call(body, grid_spec=pltpu.PrefetchScalarGridSpec(num_scalar_pr...  6.39 us
  transfers between devices with their start and end apart: 19, of which 7 were waited for; matrix products, arithmetic and copies ran while one was open for 2% of the time, Pallas kernels for 32%

profile of v1, /device:TPU:6, one launch (start us, length us, event | category | flops | bytes accessed | tf_op | source)
XLA Modules:
  0.0 101.0 jit_solution(17141768795452086229)
XLA Ops:
  0.7 2.2 %copy-done = f32[16,256,256]{2,1,0:T(8,128)S(1)} copy-done((f32[16,256,256]{2,1,0:T(8,128)S(1)}, f32[16,256,256]{2,1,0:T(8,128)}, u32[]{:S(2)}) %copy-start) | copy-done | bytes 4194328
  2.9 0.8 down.2
  5.1 1.0 edge.1
  6.1 1.3 %collective-permute-start.10 = (f32[256,128]{1,0:T(8,128)S(1)}, f32[256,128]{1,0:T(8,128)S(1)}, u32[]{:S(2)}, u32[]{:S(2)}) collective-permute-start(f32[256,128]{1,0:T(8,128)S(1)} %edge.1), channel_id=1, source_target_pairs={{1,0},{2,1},{3,2},{4,3},{5,4},{6,5},{7,6},{9,8},{10,9},{11,10},{12... | collective-permute-start | bytes 393224 | tf_op jit(solution)/shard_map/ppermute | solution.py:302
  7.5 6.1 %collective-permute-start.8 = (s32[32,256]{1,0:T(8,128)S(1)}, s32[32,256]{1,0:T(8,128)S(1)}, u32[]{:S(2)}, u32[]{:S(2)}) collective-permute-start(s32[32,256]{1,0:T(8,128)S(1)} %get-tuple-element.38), channel_id=1, source_target_pairs={{1,0},{0,1},{9,2},{8,3},{17,4},{16,5},{25,6},{24,7},{3,8},{2,9},{1... | collective-permute-start | bytes 98312 | tf_op jit(solution)/shard_map/ppermute | solution.py:308
  13.5 2.2 %collective-permute-start.3 = (s32[32,256]{1,0:T(8,128)S(1)}, s32[32,256]{1,0:T(8,128)S(1)}, u32[]{:S(2)}, u32[]{:S(2)}) collective-permute-start(s32[32,256]{1,0:T(8,128)S(1)} %get-tuple-element.39), channel_id=1, source_target_pairs={{0,0},{1,1},{8,2},{9,3},{16,4},{17,5},{24,6},{25,7},{2,8},{3,9},{1... | collective-permute-start | bytes 98312 | tf_op jit(solution)/shard_map/ppermute | solution.py:308
  15.9 2.2 %copy-done.2 = f32[16,256,256]{2,1,0:T(8,128)S(1)} copy-done((f32[16,256,256]{2,1,0:T(8,128)S(1)}, f32[16,256,256]{2,1,0:T(8,128)}, u32[]{:S(2)}) %copy-start.2) | copy-done | bytes 4194328
  19.6 2.3 %side.3 = (bf16[16,32,256]{2,1,0:T(8,128)(2,1)S(1)}, bf16[16,32,256]{2,1,0:T(8,128)(2,1)S(1)}, bf16[16,32,256]{2,1,0:T(8,128)(2,1)}, bf16[16,32,256]{2,1,0:T(8,128)(2,1)}) custom-call(s32[5]{0:T(128)S(1)} %concatenate.9.spots_ref, f32[16,256,256]{2,1,0:T(8,128)S(1)} %copy-done.2, f32[16,256,256]{2,1,0:T(8,128)S(1)} %copy-done.2, ...), custom_call_target="tpu_custom_call" | custom-call | flops 2097152 | bytes 3145728 | tf_op jit(solution)/shard_map/side/pallas_call | solution.py:193
  22.0 1.0 collective-permute-done.3.refs_4_
  23.6 2.4 %collective-permute-start.6 = (bf16[16,32,256]{2,1,0:T(8,128)(2,1)S(1)}, bf16[16,32,256]{2,1,0:T(8,128)(2,1)S(1)}, u32[]{:S(2)}, u32[]{:S(2)}) collective-permute-start(bf16[16,32,256]{2,1,0:T(8,128)(2,1)S(1)} %get-tuple-element.28), channel_id=1, source_target_pairs={{0,16},{8,24},{16,0},{24,8},{1,17},{9,25},{17,1},{25,9},{2,18},{10... | collective-permute-start | bytes 786440 | tf_op jit(solution)/shard_map/ppermute | solution.py:296
  26.0 1.4 %collective-permute-start.15 = (bf16[16,32,256]{2,1,0:T(8,128)(2,1)S(1)}, bf16[16,32,256]{2,1,0:T(8,128)(2,1)S(1)}, u32[]{:S(2)}, u32[]{:S(2)}) collective-permute-start(bf16[16,32,256]{2,1,0:T(8,128)(2,1)S(1)} %get-tuple-element.35), channel_id=1, source_target_pairs={{0,8},{8,0},{16,24},{24,16},{1,9},{9,1},{17,25},{25,17},{2,10},{10... | collective-permute-start | bytes 786440 | tf_op jit(solution)/shard_map/ppermute | solution.py:296
  27.4 2.2 %collective-permute-done.2.refs_3_ = bf16[16,32,256]{2,1,0:T(8,128)(2,1)S(1)} collective-permute-done((bf16[16,32,256]{2,1,0:T(8,128)(2,1)S(1)}, bf16[16,32,256]{2,1,0:T(8,128)(2,1)S(1)}, u32[]{:S(2)}, u32[]{:S(2)}) %collective-permute-start.2) | collective-permute-done | bytes 262176 | tf_op jit(solution)/shard_map/ppermute | solution.py:296
  29.6 2.8 %collective-permute-done.5.refs_1_ = bf16[16,32,256]{2,1,0:T(8,128)(2,1)S(1)} collective-permute-done((bf16[16,32,256]{2,1,0:T(8,128)(2,1)S(1)}, bf16[16,32,256]{2,1,0:T(8,128)(2,1)S(1)}, u32[]{:S(2)}, u32[]{:S(2)}) %collective-permute-start.5) | collective-permute-done | bytes 262176 | tf_op jit(solution)/shard_map/ppermute | solution.py:296
  32.4 2.4 %collective-permute-start.17 = (bf16[16,32,256]{2,1,0:T(8,128)(2,1)}, bf16[16,32,256]{2,1,0:T(8,128)(2,1)}, u32[]{:S(2)}, u32[]{:S(2)}) collective-permute-start(bf16[16,32,256]{2,1,0:T(8,128)(2,1)} %get-tuple-element.37), channel_id=1, source_target_pairs={{0,24},{8,16},{16,8},{24,0},{1,25},{9,17},{17,9},{25,1},{2,26},{10... | collective-permute-start | bytes 786440 | tf_op jit(solution)/shard_map/ppermute | solution.py:296
  34.8 2.4 %side.2 = (bf16[16,32,256]{2,1,0:T(8,128)(2,1)S(1)}, bf16[16,32,256]{2,1,0:T(8,128)(2,1)}, bf16[16,32,256]{2,1,0:T(8,128)(2,1)}, bf16[16,32,256]{2,1,0:T(8,128)(2,1)}) custom-call(s32[5]{0:T(128)S(1)} %concatenate.8.spots_ref, f32[16,256,256]{2,1,0:T(8,128)S(1)} %copy-done.3, f32[16,256,256]{2,1,0:T(8,128)S(1)} %copy-done.3, f32[16,256,256]{2,1,0:T(8,128)S(1)} %copy-done.3, ...), custom_call_target="tpu_custom_call" | custom-call | flops 2097152 | bytes 3145728 | tf_op jit(solution)/shard_map/side/pallas_call | solution.py:193
  37.2 1.1 %collective-permute-done.6.refs_2_ = bf16[16,32,256]{2,1,0:T(8,128)(2,1)S(1)} collective-permute-done((bf16[16,32,256]{2,1,0:T(8,128)(2,1)S(1)}, bf16[16,32,256]{2,1,0:T(8,128)(2,1)S(1)}, u32[]{:S(2)}, u32[]{:S(2)}) %collective-permute-start.6) | collective-permute-done | bytes 262176 | tf_op jit(solution)/shard_map/ppermute | solution.py:296
  38.4 1.3 %collective-permute-start.11 = (bf16[16,32,256]{2,1,0:T(8,128)(2,1)}, bf16[16,32,256]{2,1,0:T(8,128)(2,1)S(1)}, u32[]{:S(2)}, u32[]{:S(2)}) collective-permute-start(bf16[16,32,256]{2,1,0:T(8,128)(2,1)} %get-tuple-element.31), channel_id=1, source_target_pairs={{0,8},{8,0},{16,24},{24,16},{1,9},{9,1},{17,25},{25,17},{2,10},{10... | collective-permute-start | bytes 786440 | tf_op jit(solution)/shard_map/ppermute | solution.py:296
  39.7 1.2 %collective-permute-done.7.refs_3_ = bf16[16,32,256]{2,1,0:T(8,128)(2,1)S(1)} collective-permute-done((bf16[16,32,256]{2,1,0:T(8,128)(2,1)S(1)}, bf16[16,32,256]{2,1,0:T(8,128)(2,1)S(1)}, u32[]{:S(2)}, u32[]{:S(2)}) %collective-permute-start.7) | collective-permute-done | bytes 262176 | tf_op jit(solution)/shard_map/ppermute | solution.py:296
  40.9 2.8 %collective-permute-done.15.refs_1_ = bf16[16,32,256]{2,1,0:T(8,128)(2,1)S(1)} collective-permute-done((bf16[16,32,256]{2,1,0:T(8,128)(2,1)S(1)}, bf16[16,32,256]{2,1,0:T(8,128)(2,1)S(1)}, u32[]{:S(2)}, u32[]{:S(2)}) %collective-permute-start.15) | collective-permute-done | bytes 262176 | tf_op jit(solution)/shard_map/ppermute | solution.py:296
  43.7 2.4 %collective-permute-start.13 = (bf16[16,32,256]{2,1,0:T(8,128)(2,1)}, bf16[16,32,256]{2,1,0:T(8,128)(2,1)}, u32[]{:S(2)}, u32[]{:S(2)}) collective-permute-start(bf16[16,32,256]{2,1,0:T(8,128)(2,1)} %get-tuple-element.33), channel_id=1, source_target_pairs={{0,24},{8,16},{16,8},{24,0},{1,25},{9,17},{17,9},{25,1},{2,26},{10... | collective-permute-start | bytes 786440 | tf_op jit(solution)/shard_map/ppermute | solution.py:296
  47.5 0.9 copy.7
  48.4 1.1 %reshape.7.groups_ref = s32[5120]{0:T(1024)S(1)} reshape(s32[640,8]{1,0:T(8,128)} %copy.7) | data formatting | bytes 40960 | tf_op jit(solution)/shard_map/reshape | solution.py:85
  50.3 6.2 %pairs.4 = f32[32,256]{1,0:T(8,128)S(1)} custom-call(s32[4]{0:T(128)S(1)} %pad_add_fusion.1.base_ref, s32[5120]{0:T(1024)S(1)} %reshape.7.groups_ref, bf16[16,32,256]{2,1,0:T(8,128)(2,1)S(1)} %get-tuple-element.21.refs_0_, bf16[16,32,256]{2,1,0:T(8,128)(2,1)S(1)} %collective-permute-done.refs_1_, bf16[16,32,256]{2,1,0:T(8,128)(2,1)S(1)} %collective-permute-done.1.refs_2_, ...), custom_call_target="tpu_custom_call" | custom-call | flops 33554432 | bytes 2097152 | tf_op jit(solution)/shard_map/pairs/pallas_call | solution.py:128
  57.3 6.2 %pairs.5 = f32[32,256]{1,0:T(8,128)S(1)} custom-call(s32[4]{0:T(128)S(1)} %pad_add_fusion.1.base_ref, s32[5120]{0:T(1024)S(1)} %reshape.7.groups_ref, bf16[16,32,256]{2,1,0:T(8,128)(2,1)S(1)} %get-tuple-element.26.refs_0_, bf16[16,32,256]{2,1,0:T(8,128)(2,1)S(1)} %collective-permute-done.5.refs_1_, bf16[16,32,256]{2,1,0:T(8,128)(2,1)S(1)} %collective-permute-done.6.refs_2_, ...), custom_call_target="tpu_custom_call" | custom-call | flops 33554432 | bytes 2097152 | tf_op jit(solution)/shard_map/pairs/pallas_call | solution.py:128
  63.4 7.2 %collective-permute-start.4 = (f32[32,256]{1,0:T(8,128)S(1)}, f32[32,256]{1,0:T(8,128)S(1)}, u32[]{:S(2)}, u32[]{:S(2)}) collective-permute-start(f32[32,256]{1,0:T(8,128)S(1)} %pairs.4), channel_id=1, source_target_pairs={{0,0},{1,1},{2,8},{3,9},{4,16},{5,17},{6,24},{7,25},{8,2},{9,3},{1... | collective-permute-start | bytes 98312 | tf_op jit(solution)/shard_map/ppermute | solution.py:316
  70.7 6.2 %pairs.7 = f32[32,256]{1,0:T(8,128)S(1)} custom-call(s32[4]{0:T(128)S(1)} %pad_add_fusion.1.base_ref, s32[5120]{0:T(1024)S(1)} %reshape.7.groups_ref, bf16[16,32,256]{2,1,0:T(8,128)(2,1)S(1)} %get-tuple-element.34.refs_0_, bf16[16,32,256]{2,1,0:T(8,128)(2,1)S(1)} %collective-permute-done.15.refs_1_, ...), custom_call_target="tpu_custom_call" | custom-call | flops 33554432 | bytes 2097152 | tf_op jit(solution)/shard_map/pairs/pallas_call | solution.py:128
  77.0 5.4 %collective-permute-start.18 = (f32[32,256]{1,0:T(8,128)S(1)}, f32[32,256]{1,0:T(8,128)S(1)}, u32[]{:S(2)}, u32[]{:S(2)}) collective-permute-start(f32[32,256]{1,0:T(8,128)S(1)} %pairs.7), channel_id=1, source_target_pairs={{0,1},{1,0},{2,9},{3,8},{4,17},{5,16},{6,25},{7,24},{8,3},{9,2},{1... | collective-permute-start | bytes 98312 | tf_op jit(solution)/shard_map/ppermute | solution.py:316
  82.4 6.3 %pairs.6 = f32[32,256]{1,0:T(8,128)S(1)} custom-call(s32[4]{0:T(128)S(1)} %pad_add_fusion.1.base_ref, s32[5120]{0:T(1024)S(1)} %reshape.7.groups_ref, bf16[16,32,256]{2,1,0:T(8,128)(2,1)S(1)} %get-tuple-element.30.refs_0_, bf16[16,32,256]{2,1,0:T(8,128)(2,1)S(1)} %collective-permute-done.11.refs_1_, bf16[16,32,256]{2,1,0:T(8,128)(2,1)} %collective-permute-done.12.refs_2_, ...), custom_call_target="tpu_custom_call" | custom-call | flops 33554432 | bytes 2097152 | tf_op jit(solution)/shard_map/pairs/pallas_call | solution.py:128
  88.7 2.3 %collective-permute-start.14 = (f32[32,256]{1,0:T(8,128)S(1)}, f32[32,256]{1,0:T(8,128)S(1)}, u32[]{:S(2)}, u32[]{:S(2)}) collective-permute-start(f32[32,256]{1,0:T(8,128)S(1)} %pairs.6), channel_id=1, source_target_pairs={{0,0},{1,1},{2,8},{3,9},{4,16},{5,17},{6,24},{7,25},{8,2},{9,3},{1... | collective-permute-start | bytes 98312 | tf_op jit(solution)/shard_map/ppermute | solution.py:316
  91.1 7.0 %collective-permute-done.14.refs_2_ = f32[32,256]{1,0:T(8,128)S(1)} collective-permute-done((f32[32,256]{1,0:T(8,128)S(1)}, f32[32,256]{1,0:T(8,128)S(1)}, u32[]{:S(2)}, u32[]{:S(2)}) %collective-permute-start.14) | collective-permute-done | bytes 32800 | tf_op jit(solution)/shard_map/ppermute | solution.py:316
  98.1 0.8 copy-done.8
  99.8 1.2 %finish.1 = (f32[32,512]{1,0:T(8,128)}, f32[32,512]{1,0:T(8,128)}) custom-call(s32[2]{0:T(128)S(1)} %pad_add_fusion.halves_ref, f32[32,256]{1,0:T(8,128)S(1)} %collective-permute-done.4.refs_0_, f32[32,256]{1,0:T(8,128)S(1)} %collective-permute-done.9.refs_1_, f32[32,256]{1,0:T(8,128)S(1)} %collective-permute-done.14.refs_2_, ...), custom_call_target="tpu_custom_call" | custom-call | tf_op jit(solution)/shard_map/finish/pallas_call | solution.py:245
  (48 shorter events, 7.7 us)
Async XLA Ops:
  0.7 2.2 %copy-start = (f32[16,256,256]{2,1,0:T(8,128)S(1)}, f32[16,256,256]{2,1,0:T(8,128)}, u32[]{:S(2)}) copy-start(f32[16,256,256]{2,1,0:T(8,128)} %refs_3_.7) | copy-start | bytes 12582916
  2.9 2.2 %copy-start.1 = (f32[16,256,256]{2,1,0:T(8,128)S(1)}, f32[16,256,256]{2,1,0:T(8,128)}, u32[]{:S(2)}) copy-start(f32[16,256,256]{2,1,0:T(8,128)} %refs_3_.7) | copy-start | bytes 12582916
  3.8 3.7 %copy-start.11 = (s32[32,512]{1,0:T(8,128)S(1)}, s32[32,512]{1,0:T(8,128)}, u32[]{:S(2)}) copy-start(s32[32,512]{1,0:T(8,128)} %param.7) | copy-start | bytes 196612
  3.8 22.2 %collective-permute-start = (bf16[16,32,256]{2,1,0:T(8,128)(2,1)S(1)}, bf16[16,32,256]{2,1,0:T(8,128)(2,1)S(1)}, u32[]{:S(2)}, u32[]{:S(2)}) collective-permute-start(bf16[16,32,256]{2,1,0:T(8,128)(2,1)S(1)} %get-tuple-element.22), channel_id=1, source_target_pairs={{0,8},{8,0},{16,24},{24,16},{1,9},{9,1},{17,25},{25,17},{2,10},{10... | collective-permute-start | bytes 786440 | tf_op jit(solution)/shard_map/ppermute | solution.py:296
  4.4 21.7 %collective-permute-start.1 = (bf16[16,32,256]{2,1,0:T(8,128)(2,1)S(1)}, bf16[16,32,256]{2,1,0:T(8,128)(2,1)S(1)}, u32[]{:S(2)}, u32[]{:S(2)}) collective-permute-start(bf16[16,32,256]{2,1,0:T(8,128)(2,1)S(1)} %get-tuple-element.23), channel_id=1, source_target_pairs={{0,16},{8,24},{16,0},{24,8},{1,17},{9,25},{17,1},{25,9},{2,18},{10... | collective-permute-start | bytes 786440 | tf_op jit(solution)/shard_map/ppermute | solution.py:296
  6.1 13.4 %collective-permute-start.10 = (f32[256,128]{1,0:T(8,128)S(1)}, f32[256,128]{1,0:T(8,128)S(1)}, u32[]{:S(2)}, u32[]{:S(2)}) collective-permute-start(f32[256,128]{1,0:T(8,128)S(1)} %edge.1), channel_id=1, source_target_pairs={{1,0},{2,1},{3,2},{4,3},{5,4},{6,5},{7,6},{9,8},{10,9},{11,10},{12... | collective-permute-start | bytes 393224 | tf_op jit(solution)/shard_map/ppermute | solution.py:302
  7.5 11.4 %collective-permute-start.8 = (s32[32,256]{1,0:T(8,128)S(1)}, s32[32,256]{1,0:T(8,128)S(1)}, u32[]{:S(2)}, u32[]{:S(2)}) collective-permute-start(s32[32,256]{1,0:T(8,128)S(1)} %get-tuple-element.38), channel_id=1, source_target_pairs={{1,0},{0,1},{9,2},{8,3},{17,4},{16,5},{25,6},{24,7},{3,8},{2,9},{1... | collective-permute-start | bytes 98312 | tf_op jit(solution)/shard_map/ppermute | solution.py:308
  13.5 9.4 %collective-permute-start.3 = (s32[32,256]{1,0:T(8,128)S(1)}, s32[32,256]{1,0:T(8,128)S(1)}, u32[]{:S(2)}, u32[]{:S(2)}) collective-permute-start(s32[32,256]{1,0:T(8,128)S(1)} %get-tuple-element.39), channel_id=1, source_target_pairs={{0,0},{1,1},{8,2},{9,3},{16,4},{17,5},{24,6},{25,7},{2,8},{3,9},{1... | collective-permute-start | bytes 98312 | tf_op jit(solution)/shard_map/ppermute | solution.py:308
  15.9 2.2 %copy-start.2 = (f32[16,256,256]{2,1,0:T(8,128)S(1)}, f32[16,256,256]{2,1,0:T(8,128)}, u32[]{:S(2)}) copy-start(f32[16,256,256]{2,1,0:T(8,128)} %refs_3_.7) | copy-start | bytes 12582916
  18.9 0.6 copy-start.6
  19.5 10.1 %collective-permute-start.2 = (bf16[16,32,256]{2,1,0:T(8,128)(2,1)S(1)}, bf16[16,32,256]{2,1,0:T(8,128)(2,1)S(1)}, u32[]{:S(2)}, u32[]{:S(2)}) collective-permute-start(bf16[16,32,256]{2,1,0:T(8,128)(2,1)S(1)} %get-tuple-element.24), channel_id=1, source_target_pairs={{0,24},{8,16},{16,8},{24,0},{1,25},{9,17},{17,9},{25,1},{2,26},{10... | collective-permute-start | bytes 786440 | tf_op jit(solution)/shard_map/ppermute | solution.py:296
  19.6 15.3 %copy-start.3 = (f32[16,256,256]{2,1,0:T(8,128)S(1)}, f32[16,256,256]{2,1,0:T(8,128)}, u32[]{:S(2)}) copy-start(f32[16,256,256]{2,1,0:T(8,128)} %refs_3_.7) | copy-start | bytes 12582916
  19.6 12.9 %collective-permute-start.5 = (bf16[16,32,256]{2,1,0:T(8,128)(2,1)S(1)}, bf16[16,32,256]{2,1,0:T(8,128)(2,1)S(1)}, u32[]{:S(2)}, u32[]{:S(2)}) collective-permute-start(bf16[16,32,256]{2,1,0:T(8,128)(2,1)S(1)} %get-tuple-element.27), channel_id=1, source_target_pairs={{0,8},{8,0},{16,24},{24,16},{1,9},{9,1},{17,25},{25,17},{2,10},{10... | collective-permute-start | bytes 786440 | tf_op jit(solution)/shard_map/ppermute | solution.py:296
  22.9 0.6 copy-start.4
  23.6 14.8 %collective-permute-start.6 = (bf16[16,32,256]{2,1,0:T(8,128)(2,1)S(1)}, bf16[16,32,256]{2,1,0:T(8,128)(2,1)S(1)}, u32[]{:S(2)}, u32[]{:S(2)}) collective-permute-start(bf16[16,32,256]{2,1,0:T(8,128)(2,1)S(1)} %get-tuple-element.28), channel_id=1, source_target_pairs={{0,16},{8,24},{16,0},{24,8},{1,17},{9,25},{17,1},{25,9},{2,18},{10... | collective-permute-start | bytes 786440 | tf_op jit(solution)/shard_map/ppermute | solution.py:296
  26.0 15.0 %collective-permute-start.7 = (bf16[16,32,256]{2,1,0:T(8,128)(2,1)S(1)}, bf16[16,32,256]{2,1,0:T(8,128)(2,1)S(1)}, u32[]{:S(2)}, u32[]{:S(2)}) collective-permute-start(bf16[16,32,256]{2,1,0:T(8,128)(2,1)S(1)} %get-tuple-element.29), channel_id=1, source_target_pairs={{0,24},{8,16},{16,8},{24,0},{1,25},{9,17},{17,9},{25,1},{2,26},{10... | collective-permute-start | bytes 786440 | tf_op jit(solution)/shard_map/ppermute | solution.py:296
  26.0 17.7 %collective-permute-start.15 = (bf16[16,32,256]{2,1,0:T(8,128)(2,1)S(1)}, bf16[16,32,256]{2,1,0:T(8,128)(2,1)S(1)}, u32[]{:S(2)}, u32[]{:S(2)}) collective-permute-start(bf16[16,32,256]{2,1,0:T(8,128)(2,1)S(1)} %get-tuple-element.35), channel_id=1, source_target_pairs={{0,8},{8,0},{16,24},{24,16},{1,9},{9,1},{17,25},{25,17},{2,10},{10... | collective-permute-start | bytes 786440 | tf_op jit(solution)/shard_map/ppermute | solution.py:296
  29.6 33.8 %collective-permute-start.16 = (bf16[16,32,256]{2,1,0:T(8,128)(2,1)}, bf16[16,32,256]{2,1,0:T(8,128)(2,1)S(1)}, u32[]{:S(2)}, u32[]{:S(2)}) collective-permute-start(bf16[16,32,256]{2,1,0:T(8,128)(2,1)} %get-tuple-element.36), channel_id=1, source_target_pairs={{0,16},{8,24},{16,0},{24,8},{1,17},{9,25},{17,1},{25,9},{2,18},{10... | collective-permute-start | bytes 786440 | tf_op jit(solution)/shard_map/ppermute | solution.py:296
  32.4 38.2 %collective-permute-start.17 = (bf16[16,32,256]{2,1,0:T(8,128)(2,1)}, bf16[16,32,256]{2,1,0:T(8,128)(2,1)}, u32[]{:S(2)}, u32[]{:S(2)}) collective-permute-start(bf16[16,32,256]{2,1,0:T(8,128)(2,1)} %get-tuple-element.37), channel_id=1, source_target_pairs={{0,24},{8,16},{16,8},{24,0},{1,25},{9,17},{17,9},{25,1},{2,26},{10... | collective-permute-start | bytes 786440 | tf_op jit(solution)/shard_map/ppermute | solution.py:296
  38.4 38.6 %collective-permute-start.11 = (bf16[16,32,256]{2,1,0:T(8,128)(2,1)}, bf16[16,32,256]{2,1,0:T(8,128)(2,1)S(1)}, u32[]{:S(2)}, u32[]{:S(2)}) collective-permute-start(bf16[16,32,256]{2,1,0:T(8,128)(2,1)} %get-tuple-element.31), channel_id=1, source_target_pairs={{0,8},{8,0},{16,24},{24,16},{1,9},{9,1},{17,25},{25,17},{2,10},{10... | collective-permute-start | bytes 786440 | tf_op jit(solution)/shard_map/ppermute | solution.py:296
  40.9 41.5 %collective-permute-start.12 = (bf16[16,32,256]{2,1,0:T(8,128)(2,1)}, bf16[16,32,256]{2,1,0:T(8,128)(2,1)}, u32[]{:S(2)}, u32[]{:S(2)}) collective-permute-start(bf16[16,32,256]{2,1,0:T(8,128)(2,1)} %get-tuple-element.32), channel_id=1, source_target_pairs={{0,16},{8,24},{16,0},{24,8},{1,17},{9,25},{17,1},{25,9},{2,18},{10... | collective-permute-start | bytes 786440 | tf_op jit(solution)/shard_map/ppermute | solution.py:296
  43.7 38.7 %collective-permute-start.13 = (bf16[16,32,256]{2,1,0:T(8,128)(2,1)}, bf16[16,32,256]{2,1,0:T(8,128)(2,1)}, u32[]{:S(2)}, u32[]{:S(2)}) collective-permute-start(bf16[16,32,256]{2,1,0:T(8,128)(2,1)} %get-tuple-element.33), channel_id=1, source_target_pairs={{0,24},{8,16},{16,8},{24,0},{1,25},{9,17},{17,9},{25,1},{2,26},{10... | collective-permute-start | bytes 786440 | tf_op jit(solution)/shard_map/ppermute | solution.py:296
  46.1 0.8 copy-start.10
  49.6 0.8 copy-start.5
  56.5 0.8 copy-start.7
  63.4 27.6 %collective-permute-start.4 = (f32[32,256]{1,0:T(8,128)S(1)}, f32[32,256]{1,0:T(8,128)S(1)}, u32[]{:S(2)}, u32[]{:S(2)}) collective-permute-start(f32[32,256]{1,0:T(8,128)S(1)} %pairs.4), channel_id=1, source_target_pairs={{0,0},{1,1},{2,8},{3,9},{4,16},{5,17},{6,24},{7,25},{8,2},{9,3},{1... | collective-permute-start | bytes 98312 | tf_op jit(solution)/shard_map/ppermute | solution.py:316
  70.7 20.4 %collective-permute-start.9 = (f32[32,256]{1,0:T(8,128)S(1)}, f32[32,256]{1,0:T(8,128)S(1)}, u32[]{:S(2)}, u32[]{:S(2)}) collective-permute-start(f32[32,256]{1,0:T(8,128)S(1)} %pairs.5), channel_id=1, source_target_pairs={{0,1},{1,0},{2,9},{3,8},{4,17},{5,16},{6,25},{7,24},{8,3},{9,2},{1... | collective-permute-start | bytes 98312 | tf_op jit(solution)/shard_map/ppermute | solution.py:316
  77.0 14.1 %collective-permute-start.18 = (f32[32,256]{1,0:T(8,128)S(1)}, f32[32,256]{1,0:T(8,128)S(1)}, u32[]{:S(2)}, u32[]{:S(2)}) collective-permute-start(f32[32,256]{1,0:T(8,128)S(1)} %pairs.7), channel_id=1, source_target_pairs={{0,1},{1,0},{2,9},{3,8},{4,17},{5,16},{6,25},{7,24},{8,3},{9,2},{1... | collective-permute-start | bytes 98312 | tf_op jit(solution)/shard_map/ppermute | solution.py:316
  88.7 9.4 %collective-permute-start.14 = (f32[32,256]{1,0:T(8,128)S(1)}, f32[32,256]{1,0:T(8,128)S(1)}, u32[]{:S(2)}, u32[]{:S(2)}) collective-permute-start(f32[32,256]{1,0:T(8,128)S(1)} %pairs.6), channel_id=1, source_target_pairs={{0,0},{1,1},{2,8},{3,9},{4,16},{5,17},{6,24},{7,25},{8,2},{9,3},{1... | collective-permute-start | bytes 98312 | tf_op jit(solution)/shard_map/ppermute | solution.py:316
  98.1 0.8 copy-start.8
  99.0 0.8 copy-start.9

commit v2 on v1

v2 whole, which is shorter than its diff:
```python
import functools

import jax
import jax.numpy as jnp
from jax import lax
from jax.experimental import pallas as pl
from jax.experimental.pallas import tpu as pltpu
from jax.sharding import PartitionSpec as P

PARTNERS = 4
LOW = -64.0
LANES = 128
VMEM = pl.BlockSpec(memory_space=pltpu.VMEM)
SMEM = pl.BlockSpec(memory_space=pltpu.SMEM)
HBM = pl.BlockSpec(memory_space=pltpu.HBM)
LOADS = 4
LIMIT = pltpu.CompilerParams(vmem_limit_bytes=16 * 2**20)
ALL = pltpu.CompilerParams(vmem_limit_bytes=60 * 2**20)


def prepare_kernel(include_ref, groups_ref, linear_ref):
    fields = include_ref.shape[0]
    slots = groups_ref.shape[1]
    f32 = jnp.float32

    def dot(a, b, over):
        return lax.dot_general(
            a.astype(jnp.bfloat16),
            b.astype(jnp.bfloat16),
            ((over[:1], over[1:]), ((), ())),
            preferred_element_type=f32,
        )

    row = lax.broadcasted_iota(jnp.int32, (fields, fields), 0)
    column = lax.broadcasted_iota(jnp.int32, (fields, fields), 1)
    upper = jnp.where(column > row, 1.0, 0.0)
    lower = jnp.where(column < row, 1.0, 0.0)
    eye = jnp.where(column == row, 1.0, 0.0)
    included = jnp.where(column > row, include_ref[...], 0).astype(f32)
    place = dot(included, upper, (1, 0))
    both = included + dot(included, eye, (0, 0))
    count = jnp.sum(included, axis=1, keepdims=True)
    degree = jnp.sum(both, axis=1, keepdims=True)
    groups = jnp.floor((count + (PARTNERS - 1)) * (1.0 / PARTNERS))
    start = dot(lower, jnp.broadcast_to(groups, (fields, LANES)), (1, 0))[:, :1]
    total = jnp.sum(groups, axis=0, keepdims=True)
    slot = lax.broadcasted_iota(jnp.int32, (fields, slots), 1).astype(f32)
    ids = lax.broadcasted_iota(jnp.int32, (fields, slots), 0).astype(f32)
    inside = jnp.where((slot >= start) & (slot < start + groups), 1.0, 0.0)
    used = jnp.sum(inside, axis=0, keepdims=True)
    own = jnp.sum(inside * ids, axis=0, keepdims=True)
    first = jnp.sum(inside * (slot - start) * PARTNERS, axis=0, keepdims=True)
    places = dot(jnp.where(included > 0, place, -8.0), inside, (0, 0))
    places = jnp.where(used > 0, places, -8.0)
    groups_ref[...] = jnp.zeros(groups_ref.shape, jnp.int32)
    for u in range(PARTNERS):
        hit = jnp.where(places == first + u, 1.0, 0.0)
        found = jnp.sum(hit, axis=0, keepdims=True)
        partner = jnp.sum(hit * ids, axis=0, keepdims=True)
        absent = jnp.where(used > 0, float(fields), float(fields + 1))
        groups_ref[u : u + 1, :] = jnp.where(found > 0, partner, absent).astype(jnp.int32)
    owner = jnp.where(used > 0, own, float(fields + 1))
    groups_ref[PARTNERS : PARTNERS + 1, :] = owner.astype(jnp.int32)
    groups_ref[PARTNERS + 1 : PARTNERS + 2, :] = jnp.broadcast_to(total, (1, slots)).astype(
        jnp.int32
    )
    lanes = linear_ref.shape[1]
    padding = 2.0 * (groups * PARTNERS - count)
    wide = jnp.concatenate([both, jnp.zeros((fields, lanes - fields), f32)], axis=1)
    row = lax.broadcasted_iota(jnp.int32, (fields, lanes), 0)
    column = lax.broadcasted_iota(jnp.int32, (fields, lanes), 1)
    linear_ref[...] = jnp.where(row == column, 0.0, degree + wide) + padding


def prepare(pair_include):
    fields = pair_include.shape[0]
    most = sum(pl.cdiv(fields - 1 - a, PARTNERS) for a in range(fields))
    slots = pl.cdiv(most + 8, LANES) * LANES
    groups, linear = pl.pallas_call(
        prepare_kernel,
        out_shape=(
            jax.ShapeDtypeStruct((8, slots), jnp.int32),
            jax.ShapeDtypeStruct((fields, LANES), jnp.float32),
        ),
        compiler_params=LIMIT,
        name="prepare",
    )(pair_include)
    return groups.T.reshape(-1), linear


def factors_kernel(labels_ref, linear_ref, out_ref):
    turns, fields, band, width = out_ref.shape

    def one(field, carry):
        table = jnp.broadcast_to(linear_ref[pl.ds(field, 1), :], (band, LANES))
        for t in range(turns):
            mine = labels_ref[t * band : (t + 1) * band, :]
            factor = jnp.concatenate(
                [
                    jnp.take_along_axis(table, mine[:, at : at + LANES], axis=1)
                    for at in range(0, width, LANES)
                ],
                axis=1,
            )
            out_ref[t, field] = factor.astype(jnp.bfloat16)
        return carry

    lax.fori_loop(0, fields, one, 0, unroll=4)


def pairs_kernel(base_ref, groups_ref, *refs, scale, unroll, at_turn, label_turn):
    *parts, labels_ref, factors_ref, out_ref, held = refs
    fields = factors_ref.shape[1]
    _, each, rows, width = parts[0].shape
    held[fields] = jnp.full((rows, width), LOW, jnp.float32)
    held[fields + 1] = jnp.zeros((rows, width), jnp.float32)
    labels = labels_ref[...]
    linear = jnp.zeros((rows, width), jnp.float32)
    for k, part in enumerate(parts):
        for i in range(each):
            field = base_ref[k] + i
            values = jnp.where(labels == field, LOW, part[at_turn, i].astype(jnp.float32))
            held[field] = values
            linear = linear + factors_ref[label_turn, field].astype(jnp.float32) * values

    def step(number, total):
        for v in range(unroll):
            at = (number * unroll + v) * 8
            own = held[groups_ref[at + PARTNERS]]
            for u in range(PARTNERS):
                total = total + jnp.maximum(own, held[groups_ref[at + u]])
        return total

    steps = (groups_ref[PARTNERS + 1] + (unroll - 1)) // unroll
    total = lax.fori_loop(0, steps, step, jnp.zeros((rows, width), jnp.float32))
    out_ref[...] = (2.0 * total - linear) * scale


def pairs(base, groups, parts, labels, factors, at_turn, label_turn):
    fields = factors.shape[1]
    work = fields * fields * labels.size
    return pl.pallas_call(
        functools.partial(
            pairs_kernel,
            scale=2.0 / (fields * (fields - 1)),
            unroll=8,
            at_turn=at_turn,
            label_turn=label_turn,
        ),
        in_specs=[SMEM, SMEM] + [VMEM] * (len(parts) + 2),
        out_specs=VMEM,
        out_shape=jax.ShapeDtypeStruct(labels.shape, jnp.float32),
        scratch_shapes=[pltpu.VMEM((fields + 2, *labels.shape), jnp.float32)],
        compiler_params=LIMIT,
        cost_estimate=pl.CostEstimate(flops=work, bytes_accessed=work // 16, transcendentals=0),
        name="pairs",
    )(base, groups, *parts, labels, factors)


def load_fields(potentials_ref, held, sems):
    each = held.shape[0]
    step = max(each // LOADS, 1)
    copies = []
    for number, at in enumerate(range(0, each, step)):
        span = pl.ds(at, step)
        copies.append(
            pltpu.make_async_copy(potentials_ref.at[span], held.at[span], sems.at[number])
        )
        copies[-1].start()
    for number, copy in enumerate(copies):
        copy.wait()
        yield from range(number * step, (number + 1) * step)


def down_kernel(first_ref, potentials_ref, *refs):
    *outs, edge_ref, held, sems = refs
    _, height, width = held.shape
    turns, _, rows, _ = outs[0].shape
    row = lax.broadcasted_iota(jnp.int32, (rows, width), 0)
    lane = lax.broadcasted_iota(jnp.int32, (height, LANES), 1)
    for i in load_fields(potentials_ref, held, sems):
        for k, out in enumerate(outs):
            for t in range(turns):
                first = pl.multiple_of(first_ref[k * turns + t] * rows, rows)
                following = pl.multiple_of(jnp.minimum(first + rows, height - 8), 8)
                at_end = first + rows == height
                here = held[i, pl.ds(first, rows), :]
                below = held[i, pl.ds(following, 8), :]
                below = jnp.concatenate([here[1:], below[:1]], axis=0)
                change = jnp.where((row == rows - 1) & at_end, 0.0, below - here)
                out[t, i] = change.astype(jnp.bfloat16)
        edge_ref[...] = jnp.where(lane == i, held[i, :, 0:1], edge_ref[...] if i else 0.0)


def side_kernel(first_ref, potentials_ref, beside_ref, *outs, turns):
    _, each, rows, width = outs[0].shape
    parts = len(outs) // turns
    lane = lax.broadcasted_iota(jnp.int32, (rows, width), 1)
    at_end = first_ref[len(outs)] == 1
    for k in range(parts):
        for t in range(turns):
            first = pl.multiple_of(first_ref[k * turns + t] * rows, rows)
            for i in range(each):
                here = potentials_ref[i, pl.ds(first, rows), :]
                right = pltpu.roll(here, width - 1, 1)
                beside = beside_ref[pl.ds(first, rows), i : i + 1]
                right = jnp.where(lane == width - 1, beside, right)
                change = jnp.where((lane == width - 1) & at_end, 0.0, right - here)
                outs[t * parts + k][0, i] = change.astype(jnp.bfloat16)


def on_tile(body, name, out_shape, scalars, *arrays, fields=None):
    work = sum(a.size for a in arrays)
    specs = [VMEM] * len(arrays)
    scratch = []
    if fields is not None:
        arrays, specs = (fields, *arrays), [HBM, *specs]
        scratch = [pltpu.VMEM(fields.shape, fields.dtype), pltpu.SemaphoreType.DMA((LOADS,))]
        work = 2 * fields.size
    return pl.pallas_call(
        body,
        in_specs=[SMEM] * len(scalars) + specs,
        out_specs=jax.tree.map(lambda _: VMEM, out_shape),
        out_shape=out_shape,
        scratch_shapes=scratch,
        compiler_params=LIMIT if fields is None else ALL,
        cost_estimate=pl.CostEstimate(
            flops=4 * work, bytes_accessed=6 * work, transcendentals=0
        ),
        name=name,
    )(*scalars, *arrays)


def finish_kernel(halves_ref, *refs, chunks, width):
    *pieces, across, down, out_across, out_down = refs
    for (turn, contents), piece in zip(chunks, pieces):
        lanes = pl.ds(pl.multiple_of(halves_ref[turn] * width, width), width)
        at = 0
        for kind, first, rows in contents:
            conduct, out = (down, out_down) if kind == "down" else (across, out_across)
            out[first : first + rows, lanes] = (
                conduct[first : first + rows, lanes] * piece[at : at + rows]
            )
            at += rows


def finish(chunks, halves, pieces, conduct_across, conduct_down):
    shape = jax.ShapeDtypeStruct(conduct_across.shape, jnp.float32)
    return pl.pallas_call(
        functools.partial(finish_kernel, chunks=chunks, width=pieces[0].shape[1]),
        in_specs=[SMEM] + [VMEM] * (len(pieces) + 2),
        out_specs=[VMEM, VMEM],
        out_shape=[shape, shape],
        compiler_params=LIMIT,
        name="finish",
    )(halves, *pieces, conduct_across, conduct_down)


def after(value, *others):
    return lax.optimization_barrier((value, *others))[0]


def towards(index, step, size):
    return index ^ step if size & (size - 1) == 0 else (index + step) % size


def source(index, step, size):
    return index ^ step if size & (size - 1) == 0 else (index + size - step) % size


def local(potentials, pair_include, labels, conduct_across, conduct_down):
    parts, strips = lax.axis_size("cores"), lax.axis_size("strip")
    core, strip = lax.axis_index("cores"), lax.axis_index("strip")
    each, height, width = potentials.shape
    rows = labels.shape[0]
    turns = strips // parts

    flat = [(c, s // turns, s % turns) for c in range(parts) for s in range(strips)]

    def number(c, group, j):
        return c * strips + group * turns + j

    def move(array, to):
        moves = [(number(*at), number(*to(*at))) for at in flat]
        return lax.ppermute(array, ("cores", "strip"), moves)

    def send_home(array, turn):
        return move(array, lambda c, g, j: (g, c, towards(j, turn, turns)))

    def exchange(block, k):
        moves = [(i, towards(i, k, parts)) for i in range(parts)]
        return lax.ppermute(block, "cores", moves)

    inside = strip % turns
    ts = jnp.arange(turns, dtype=jnp.int32)
    ks = jnp.arange(parts, dtype=jnp.int32)
    base = source(core, ks, parts) * each
    first = towards(core, ks, parts)[:, None] * turns + towards(inside, ts, turns)[None]
    last = (strip == strips - 1).astype(jnp.int32)
    first = jnp.concatenate([first.reshape(-1), last[None]])
    halves = source(inside, ts, turns)

    block = jax.ShapeDtypeStruct((turns, each, rows, width), jnp.bfloat16)
    column = jax.ShapeDtypeStruct((height, LANES), jnp.float32)
    *down, edge = on_tile(
        down_kernel, "down", [block] * parts + [column], [first], fields=potentials
    )
    far = list(range(parts - 1, 0, -1))
    down = [down[0], *[exchange(down[k], k) for k in far][::-1]]
    beside = lax.ppermute(edge, "strip", [(i, i - 1) for i in range(1, strips)])
    labels = move(after(labels, edge), lambda c, g, j: (g, c, j))
    groups, linear = prepare(after(pair_include, edge))

    own_labels = []
    for t in range(turns):
        to = towards(inside, t, turns)
        part = lax.dynamic_slice_in_dim(labels, to * width, width, 1)
        back = (turns - t) % turns if turns & (turns - 1) else t
        own_labels.append((back, move(part, lambda c, g, j: (c, g, towards(j, t, turns))) if t else part))
    own_labels = [part for _, part in sorted(own_labels, key=lambda pair: pair[0])]

    block = jax.ShapeDtypeStruct((1, each, rows, width), jnp.bfloat16)
    side = on_tile(
        functools.partial(side_kernel, turns=turns),
        "side",
        [block] * (parts * turns),
        [after(first, *own_labels, groups)],
        potentials,
        beside,
    )
    factors = on_tile(
        factors_kernel,
        "factors",
        jax.ShapeDtypeStruct((turns, parts * each, rows, width), jnp.bfloat16),
        [],
        jnp.concatenate(own_labels, axis=0),
        after(linear, *side),
    )
    blocks = [side[t * parts : (t + 1) * parts] for t in range(turns)]
    down[0] = after(down[0], *down[1:])
    down_sums = [pairs(base, groups, down, own_labels[t], factors, t, t) for t in range(turns)]
    arrived = []
    for t in range(turns):
        got = [blocks[t][0]]
        for k in far:
            if t == 0:
                waits = [factors] if k == 1 else []
            else:
                waits = [down_sums[min(t, turns - 1) if k == 1 else t - 1]]
            got.insert(1, exchange(after(blocks[t][k], *waits), k))
        arrived.append(got)
    side_sums, pieces = [], []
    for t in range(turns):
        got = arrived[t]
        got[0] = after(got[0], (side_sums or down_sums)[-1])
        side_sums.append(pairs(base, groups, got, own_labels[t], factors, 0, t))
        joined = jnp.concatenate([down_sums[t], side_sums[t]], axis=0)
        pieces.append(send_home(joined, t))
    contents = tuple((t, (("down", 0, rows), ("side", 0, rows))) for t in range(turns))
    return finish(contents, halves, pieces, conduct_across, conduct_down)


def solution(mesh):
    return jax.shard_map(
        local,
        mesh=mesh,
        in_specs=(
            P("cores", None, "strip"),
            P(),
            P("strip", "cores"),
            P("strip", "cores"),
            P("strip", "cores"),
        ),
        out_specs=(P("strip", "cores"), P("strip", "cores")),
        check_vma=False,
    )
```

time: 102 us -> 77.9 us (0.76)
  local copies, waits for them, and re-layouts: 12.5 us -> 2.65 us
  starting transfers between devices: 35.3 us -> 26.3 us
  waiting for transfers between devices: 18.2 us -> 12.9 us
    ppermute x19 -> x14, starting transfers between devices: 35.3 us -> 26.3 us  [the longest x9 15 us: exchange(): return lax.ppermute(block, 'cores', moves)]
    unnamed x24 -> x14, local copies, waits for them, and re-layouts: 10.2 us -> 2.22 us
    ppermute x19 -> x14, waiting for transfers between devices: 18.2 us -> 12.9 us  [the longest x4 10.8 us: move(): return lax.ppermute(array, ('cores', 'strip'), moves)]
    pallas_call x5 -> x3, Pallas kernels: 7.37 us -> 11 us  [on_tile(): pl.pallas_call(body, in_specs=[SMEM] * len(scalars) + specs, out_specs=ja...]
    pallas_call x4, Pallas kernels: 24.9 us -> 21.4 us  [pairs(): pl.pallas_call(functools.partial(pairs_kernel, scale=2.0 / (fields * (fie...]
  transfers between devices with their start and end apart: 19 -> 14, of which waited for: 7 -> 4; matrix products, arithmetic and copies ran while one was open for 2% -> 0% of each run, Pallas kernels for 32% -> 37%
where the time goes in v2:
time: 77.9 us; the launch traced here: 77.8 us
  Pallas kernels  34.2 us (44%)
  starting transfers between devices  26.3 us (34%)
  waiting for transfers between devices  12.9 us (17%)
  local copies, waits for them, and re-layouts  2.65 us (3%)
  between operations  0.92 us (1%)
    pallas_call x4, Pallas kernels, pairs(): pl.pallas_call(functools.partial(pairs_kernel, scale=2.0 / (fields * (fie...  21.4 us
    ppermute x9, starting transfers between devices, exchange(): return lax.ppermute(block, 'cores', moves)  15 us
    pallas_call x3, Pallas kernels, on_tile(): pl.pallas_call(body, in_specs=[SMEM] * len(scalars) + specs, out_specs=ja...  11 us
    ppermute x4, waiting for transfers between devices, move(): return lax.ppermute(array, ('cores', 'strip'), moves)  10.8 us
    ppermute x4, starting transfers between devices, move(): return lax.ppermute(array, ('cores', 'strip'), moves)  10.1 us
    unnamed x14, local copies, waits for them, and re-layouts  2.22 us
    ppermute x9, waiting for transfers between devices, exchange(): return lax.ppermute(block, 'cores', moves)  2.14 us
  transfers between devices with their start and end apart: 14, of which 4 were waited for; matrix products, arithmetic and copies ran while one was open for 0% of the time, Pallas kernels for 37%

profile of v2, /device:TPU:6, one launch (start us, length us, event | category | flops | bytes accessed | tf_op | source)
XLA Modules:
  0.0 77.8 jit_solution(9081497435211424036)
XLA Ops:
  0.7 0.1 broadcast_add_fusion
  0.8 0.1 add.31
  0.8 0.6 pad_add_fusion.1.first_ref
  1.4 4.5 %down.1 = (bf16[2,16,32,256]{3,2,1,0:T(8,128)(2,1)}, bf16[2,16,32,256]{3,2,1,0:T(8,128)(2,1)}, bf16[2,16,32,256]{3,2,1,0:T(8,128)(2,1)}, bf16[2,16,32,256]{3,2,1,0:T(8,128)(2,1)}, f32[256,128]{1,0:T(8,128)}) custom-call(s32[9]{0:T(128)} %pad_add_fusion.1.first_ref, f32[16,256,256]{2,1,0:T(8,128)} %potentials_ref.3), custom_call_target="tpu_custom_call" | custom-call | flops 8388608 | bytes 12582912 | tf_op jit(solution)/shard_map/down/pallas_call | solution.py:220
  6.0 0.6 collective-permute-start
  6.6 0.0 collective-permute-start.1
  6.6 2.9 %collective-permute-start.2 = (bf16[2,16,32,256]{3,2,1,0:T(8,128)(2,1)}, bf16[2,16,32,256]{3,2,1,0:T(8,128)(2,1)S(1)}, u32[]{:S(2)}, u32[]{:S(2)}) collective-permute-start(bf16[2,16,32,256]{3,2,1,0:T(8,128)(2,1)} %get-tuple-element.34), channel_id=1, source_target_pairs={{0,24},{8,16},{16,8},{24,0},{1,25},{9,17},{17,9},{25,1},{2,26},{10... | collective-permute-start | bytes 1572872 | tf_op jit(solution)/shard_map/ppermute | solution.py:292
  9.5 5.4 %collective-permute-start.3 = (s32[32,512]{1,0:T(8,128)S(1)}, s32[32,512]{1,0:T(8,128)S(1)}, u32[]{:S(2)}, u32[]{:S(2)}) collective-permute-start(s32[32,512]{1,0:T(8,128)S(1)} %copy-done.6), channel_id=1, source_target_pairs={{0,0},{1,1},{2,8},{3,9},{4,16},{5,17},{6,24},{7,25},{8,2},{9,3},{1... | collective-permute-start | bytes 196616 | tf_op jit(solution)/shard_map/ppermute | solution.py:285
  15.0 1.3 %collective-permute-start.5 = (f32[256,128]{1,0:T(8,128)}, f32[256,128]{1,0:T(8,128)S(1)}, u32[]{:S(2)}, u32[]{:S(2)}) collective-permute-start(f32[256,128]{1,0:T(8,128)} %get-tuple-element.28), channel_id=1, source_target_pairs={{1,0},{2,1},{3,2},{4,3},{5,4},{6,5},{7,6},{9,8},{10,9},{11,10},{12... | collective-permute-start | bytes 393224 | tf_op jit(solution)/shard_map/ppermute | solution.py:310
  16.3 3.2 %collective-permute-done.3 = s32[32,512]{1,0:T(8,128)S(1)} collective-permute-done((s32[32,512]{1,0:T(8,128)S(1)}, s32[32,512]{1,0:T(8,128)S(1)}, u32[]{:S(2)}, u32[]{:S(2)}) %collective-permute-start.3) | collective-permute-done | bytes 65568 | tf_op jit(solution)/shard_map/ppermute | solution.py:285
  19.5 0.6 prepare.1
  20.1 0.2 copy.7
  20.3 0.2 reshape.21.groups_ref
  20.5 0.2 collective-permute-done.4.refs_4_
  20.7 2.2 %copy-done = f32[16,256,256]{2,1,0:T(8,128)S(1)} copy-done((f32[16,256,256]{2,1,0:T(8,128)S(1)}, f32[16,256,256]{2,1,0:T(8,128)}, u32[]{:S(2)}) %copy-start) | copy-done | bytes 4194328
  22.9 2.6 %side.1 = (bf16[1,16,32,256]{3,2,1,0:T(8,128)(2,1)S(1)}, bf16[1,16,32,256]{3,2,1,0:T(8,128)(2,1)S(1)}, bf16[1,16,32,256]{3,2,1,0:T(8,128)(2,1)S(1)}, bf16[1,16,3...) custom-call(s32[9]{0:T(128)S(1)} %copy-done.5, ...), custom_call_target="tpu_custom_call" | custom-call | flops 4325376 | bytes 6488064 | tf_op jit(solution)/shard_map/side/pallas_call | solution.py:220
  25.5 0.1 collective-permute-start.8
  25.6 0.7 collective-permute-start.7
  26.2 3.9 %factors.1.refs_5_ = bf16[2,64,32,256]{3,2,1,0:T(8,128)(2,1)S(1)} custom-call(s32[64,256]{1,0:T(8,128)S(1)} %pad_add_fusion.labels_ref, f32[64,128]{1,0:T(8,128)S(1)} %get-tuple-element.47.linear_ref), custom_call_target="tpu_custom_call" | custom-call | flops 98304 | bytes 147456 | tf_op jit(solution)/shard_map/factors/pallas_call | solution.py:220
  30.2 2.9 %collective-permute-start.6 = (bf16[1,16,32,256]{3,2,1,0:T(8,128)(2,1)S(1)}, bf16[1,16,32,256]{3,2,1,0:T(8,128)(2,1)S(1)}, u32[]{:S(2)}, u32[]{:S(2)}) collective-permute-start(bf16[1,16,32,256]{3,2,1,0:T(8,128)(2,1)S(1)} %get-tuple-element.49), channel_id=1, source_target_pairs={{0,8},{8,0},{16,24},{24,16},{1,9},{9,1},{17,25},{25,17},{2,10},{10... | collective-permute-start | bytes 786440 | tf_op jit(solution)/shard_map/ppermute | solution.py:292
  33.0 2.1 %collective-permute-done.2.refs_3_ = bf16[2,16,32,256]{3,2,1,0:T(8,128)(2,1)S(1)} collective-permute-done((bf16[2,16,32,256]{3,2,1,0:T(8,128)(2,1)}, bf16[2,16,32,256]{3,2,1,0:T(8,128)(2,1)S(1)}, u32[]{:S(2)}, u32[]{:S(2)}) %collective-permute-start.2) | collective-permute-done | bytes 524320 | tf_op jit(solution)/shard_map/ppermute | solution.py:292
  35.2 5.3 %pairs.4 = f32[32,256]{1,0:T(8,128)S(1)} custom-call(s32[4]{0:T(128)S(1)} %fusion.1.base_ref, s32[5120]{0:T(1024)S(1)} %reshape.21.groups_ref, bf16[2,16,32,256]{3,2,1,0:T(8,128)(2,1)S(1)} %copy-done.1, bf16[2,16,32,256]{3,2,1,0:T(8,128)(2,1)S(1)} %collective-permute-done.refs_1_, bf16[2,16,32,256]{3,2,1,0:T(8,128)(2,1)S(1)} %collective-permute-done.1.refs_2_, ...), custom_call_target="tpu_custom_call" | custom-call | flops 33554432 | bytes 2097152 | tf_op jit(solution)/shard_map/pairs/pallas_call | solution.py:142
  40.5 5.3 %pairs.5 = f32[32,256]{1,0:T(8,128)S(1)} custom-call(s32[4]{0:T(128)S(1)} %fusion.1.base_ref, s32[5120]{0:T(1024)S(1)} %reshape.21.groups_ref, bf16[2,16,32,256]{3,2,1,0:T(8,128)(2,1)S(1)} %copy-done.1, bf16[2,16,32,256]{3,2,1,0:T(8,128)(2,1)S(1)} %collective-permute-done.refs_1_, bf16[2,16,32,256]{3,2,1,0:T(8,128)(2,1)S(1)} %collective-permute-done.1.refs_2_, ...), custom_call_target="tpu_custom_call" | custom-call | flops 33554432 | bytes 2097152 | tf_op jit(solution)/shard_map/pairs/pallas_call | solution.py:142
  45.8 0.0 copy-start.2
  45.9 6.3 %collective-permute-start.10 = (bf16[1,16,32,256]{3,2,1,0:T(8,128)(2,1)S(1)}, bf16[1,16,32,256]{3,2,1,0:T(8,128)(2,1)S(1)}, u32[]{:S(2)}, u32[]{:S(2)}) collective-permute-start(bf16[1,16,32,256]{3,2,1,0:T(8,128)(2,1)S(1)} %get-tuple-element.51), channel_id=1, source_target_pairs={{0,8},{8,0},{16,24},{24,16},{1,9},{9,1},{17,25},{25,17},{2,10},{10... | collective-permute-start | bytes 786440 | tf_op jit(solution)/shard_map/ppermute | solution.py:292
  52.2 1.5 %collective-permute-start.12 = (bf16[1,16,32,256]{3,2,1,0:T(8,128)(2,1)S(1)}, bf16[1,16,32,256]{3,2,1,0:T(8,128)(2,1)S(1)}, u32[]{:S(2)}, u32[]{:S(2)}) collective-permute-start(bf16[1,16,32,256]{3,2,1,0:T(8,128)(2,1)S(1)} %get-tuple-element.53), channel_id=1, source_target_pairs={{0,24},{8,16},{16,8},{24,0},{1,25},{9,17},{17,9},{25,1},{2,26},{10... | collective-permute-start | bytes 786440 | tf_op jit(solution)/shard_map/ppermute | solution.py:292
  53.7 5.4 %pairs.6 = f32[32,256]{1,0:T(8,128)S(1)} custom-call(s32[4]{0:T(128)S(1)} %fusion.1.base_ref, s32[5120]{0:T(1024)S(1)} %reshape.21.groups_ref, bf16[1,16,32,256]{3,2,1,0:T(8,128)(2,1)S(1)} %get-tuple-element.48.refs_0_, bf16[1,16,32,256]{3,2,1,0:T(8,128)(2,1)S(1)} %collective-permute-done.6.refs_1_, ...), custom_call_target="tpu_custom_call" | custom-call | flops 33554432 | bytes 2097152 | tf_op jit(solution)/shard_map/pairs/pallas_call | solution.py:142
  59.1 4.6 %collective-permute-start.9 = (f32[64,256]{1,0:T(8,128)S(1)}, f32[64,256]{1,0:T(8,128)S(1)}, u32[]{:S(2)}, u32[]{:S(2)}) collective-permute-start(f32[64,256]{1,0:T(8,128)S(1)} %pad_maximum_fusion), channel_id=1, source_target_pairs={{0,0},{1,1},{2,8},{3,9},{4,16},{5,17},{6,24},{7,25},{8,2},{9,3},{1... | collective-permute-start | bytes 196616 | tf_op jit(solution)/shard_map/ppermute | solution.py:285
  63.7 5.4 %pairs.7 = f32[32,256]{1,0:T(8,128)S(1)} custom-call(s32[4]{0:T(128)S(1)} %fusion.1.base_ref, s32[5120]{0:T(1024)S(1)} %reshape.21.groups_ref, bf16[1,16,32,256]{3,2,1,0:T(8,128)(2,1)S(1)} %get-tuple-element.50.refs_0_, bf16[1,16,32,256]{3,2,1,0:T(8,128)(2,1)S(1)} %collective-permute-done.10.refs_1_, ...), custom_call_target="tpu_custom_call" | custom-call | flops 33554432 | bytes 2097152 | tf_op jit(solution)/shard_map/pairs/pallas_call | solution.py:142
  69.1 0.1 collective-permute-start.13
  69.2 7.4 %collective-permute-done.13.refs_1_ = f32[64,256]{1,0:T(8,128)S(1)} collective-permute-done((f32[64,256]{1,0:T(8,128)S(1)}, f32[64,256]{1,0:T(8,128)S(1)}, u32[]{:S(2)}, u32[]{:S(2)}) %collective-permute-start.13) | collective-permute-done | bytes 65568 | tf_op jit(solution)/shard_map/ppermute | solution.py:285
  76.6 1.2 %finish.1 = (f32[32,512]{1,0:T(8,128)}, f32[32,512]{1,0:T(8,128)}) custom-call(s32[2]{0:T(128)S(1)} %iota_xor_fusion.1.halves_ref, f32[64,256]{1,0:T(8,128)S(1)} %collective-permute-done.9.refs_0_, f32[64,256]{1,0:T(8,128)S(1)} %collective-permute-done.13.refs_1_, f32[32,512]{1,0:T(8,128)S(1)} %copy-done.2, f32[32,512]{1,0:T(8,128)S(1)} %copy-done.3), custom_call_target="tpu_custom_call" | custom-call | tf_op jit(solution)/shard_map/finish/pallas_call | solution.py:249
  (31 shorter events, 0.1 us)
Async XLA Ops:
  0.6 8.9 %copy-start.6 = (s32[32,512]{1,0:T(8,128)S(1)}, s32[32,512]{1,0:T(8,128)}, u32[]{:S(2)}) copy-start(s32[32,512]{1,0:T(8,128)} %param.7) | copy-start | bytes 196612
  0.6 18.8 %copy-start.4 = (s32[64,64]{1,0:T(8,128)S(1)}, s32[64,64]{1,0:T(8,128)}, u32[]{:S(2)}) copy-start(s32[64,64]{1,0:T(8,128)} %include_ref) | copy-start | bytes 49156
  1.4 19.2 %copy-start.5 = (s32[9]{0:T(128)S(1)}, s32[9]{0:T(128)}, u32[]{:S(2)}) copy-start(s32[9]{0:T(128)} %pad_add_fusion.1.first_ref) | copy-start | bytes 112
  6.0 29.2 %copy-start.1 = (bf16[2,16,32,256]{3,2,1,0:T(8,128)(2,1)S(1)}, bf16[2,16,32,256]{3,2,1,0:T(8,128)(2,1)}, u32[]{:S(2)}) copy-start(bf16[2,16,32,256]{3,2,1,0:T(8,128)(2,1)} %get-tuple-element.35.refs_0_) | copy-start | bytes 1572868
  6.0 24.2 %collective-permute-start = (bf16[2,16,32,256]{3,2,1,0:T(8,128)(2,1)}, bf16[2,16,32,256]{3,2,1,0:T(8,128)(2,1)S(1)}, u32[]{:S(2)}, u32[]{:S(2)}) collective-permute-start(bf16[2,16,32,256]{3,2,1,0:T(8,128)(2,1)} %get-tuple-element.32), channel_id=1, source_target_pairs={{0,8},{8,0},{16,24},{24,16},{1,9},{9,1},{17,25},{25,17},{2,10},{10... | collective-permute-start | bytes 1572872 | tf_op jit(solution)/shard_map/ppermute | solution.py:292
  6.6 26.5 %collective-permute-start.1 = (bf16[2,16,32,256]{3,2,1,0:T(8,128)(2,1)}, bf16[2,16,32,256]{3,2,1,0:T(8,128)(2,1)S(1)}, u32[]{:S(2)}, u32[]{:S(2)}) collective-permute-start(bf16[2,16,32,256]{3,2,1,0:T(8,128)(2,1)} %get-tuple-element.33), channel_id=1, source_target_pairs={{0,16},{8,24},{16,0},{24,8},{1,17},{9,25},{17,1},{25,9},{2,18},{10... | collective-permute-start | bytes 1572872 | tf_op jit(solution)/shard_map/ppermute | solution.py:292
  6.6 28.5 %collective-permute-start.2 = (bf16[2,16,32,256]{3,2,1,0:T(8,128)(2,1)}, bf16[2,16,32,256]{3,2,1,0:T(8,128)(2,1)S(1)}, u32[]{:S(2)}, u32[]{:S(2)}) collective-permute-start(bf16[2,16,32,256]{3,2,1,0:T(8,128)(2,1)} %get-tuple-element.34), channel_id=1, source_target_pairs={{0,24},{8,16},{16,8},{24,0},{1,25},{9,17},{17,9},{25,1},{2,26},{10... | collective-permute-start | bytes 1572872 | tf_op jit(solution)/shard_map/ppermute | solution.py:292
  9.5 9.9 %collective-permute-start.3 = (s32[32,512]{1,0:T(8,128)S(1)}, s32[32,512]{1,0:T(8,128)S(1)}, u32[]{:S(2)}, u32[]{:S(2)}) collective-permute-start(s32[32,512]{1,0:T(8,128)S(1)} %copy-done.6), channel_id=1, source_target_pairs={{0,0},{1,1},{2,8},{3,9},{4,16},{5,17},{6,24},{7,25},{8,2},{9,3},{1... | collective-permute-start | bytes 196616 | tf_op jit(solution)/shard_map/ppermute | solution.py:285
  15.0 5.7 %collective-permute-start.5 = (f32[256,128]{1,0:T(8,128)}, f32[256,128]{1,0:T(8,128)S(1)}, u32[]{:S(2)}, u32[]{:S(2)}) collective-permute-start(f32[256,128]{1,0:T(8,128)} %get-tuple-element.28), channel_id=1, source_target_pairs={{1,0},{2,1},{3,2},{4,3},{5,4},{6,5},{7,6},{9,8},{10,9},{11,10},{12... | collective-permute-start | bytes 393224 | tf_op jit(solution)/shard_map/ppermute | solution.py:310
  19.5 1.2 %collective-permute-start.4 = (s32[32,256]{1,0:T(8,128)S(1)}, s32[32,256]{1,0:T(8,128)S(1)}, u32[]{:S(2)}, u32[]{:S(2)}) collective-permute-start(s32[32,256]{1,0:T(8,128)S(1)} %get-tuple-element.54), channel_id=1, source_target_pairs={{0,1},{1,0},{2,3},{3,2},{4,5},{5,4},{6,7},{7,6},{8,9},{9,8},{10,11... | collective-permute-start | bytes 98312 | tf_op jit(solution)/shard_map/ppermute | solution.py:285
  20.7 2.2 %copy-start = (f32[16,256,256]{2,1,0:T(8,128)S(1)}, f32[16,256,256]{2,1,0:T(8,128)}, u32[]{:S(2)}) copy-start(f32[16,256,256]{2,1,0:T(8,128)} %potentials_ref.3) | copy-start | bytes 12582916
  25.5 26.7 %collective-permute-start.8 = (bf16[1,16,32,256]{3,2,1,0:T(8,128)(2,1)S(1)}, bf16[1,16,32,256]{3,2,1,0:T(8,128)(2,1)S(1)}, u32[]{:S(2)}, u32[]{:S(2)}) collective-permute-start(bf16[1,16,32,256]{3,2,1,0:T(8,128)(2,1)S(1)} %get-tuple-element.42), channel_id=1, source_target_pairs={{0,24},{8,16},{16,8},{24,0},{1,25},{9,17},{17,9},{25,1},{2,26},{10... | collective-permute-start | bytes 786440 | tf_op jit(solution)/shard_map/ppermute | solution.py:292
  25.6 28.1 %collective-permute-start.7 = (bf16[1,16,32,256]{3,2,1,0:T(8,128)(2,1)S(1)}, bf16[1,16,32,256]{3,2,1,0:T(8,128)(2,1)S(1)}, u32[]{:S(2)}, u32[]{:S(2)}) collective-permute-start(bf16[1,16,32,256]{3,2,1,0:T(8,128)(2,1)S(1)} %get-tuple-element.41), channel_id=1, source_target_pairs={{0,16},{8,24},{16,0},{24,8},{1,17},{9,25},{17,1},{25,9},{2,18},{10... | collective-permute-start | bytes 786440 | tf_op jit(solution)/shard_map/ppermute | solution.py:292
  30.2 23.6 %collective-permute-start.6 = (bf16[1,16,32,256]{3,2,1,0:T(8,128)(2,1)S(1)}, bf16[1,16,32,256]{3,2,1,0:T(8,128)(2,1)S(1)}, u32[]{:S(2)}, u32[]{:S(2)}) collective-permute-start(bf16[1,16,32,256]{3,2,1,0:T(8,128)(2,1)S(1)} %get-tuple-element.49), channel_id=1, source_target_pairs={{0,8},{8,0},{16,24},{24,16},{1,9},{9,1},{17,25},{25,17},{2,10},{10... | collective-permute-start | bytes 786440 | tf_op jit(solution)/shard_map/ppermute | solution.py:292
  45.8 30.7 %copy-start.2 = (f32[32,512]{1,0:T(8,128)S(1)}, f32[32,512]{1,0:T(8,128)}, u32[]{:S(2)}) copy-start(f32[32,512]{1,0:T(8,128)} %refs_2_.1) | copy-start | bytes 196612
  45.8 30.7 %copy-start.3 = (f32[32,512]{1,0:T(8,128)S(1)}, f32[32,512]{1,0:T(8,128)}, u32[]{:S(2)}) copy-start(f32[32,512]{1,0:T(8,128)} %refs_3_.1) | copy-start | bytes 196612
  45.9 17.8 %collective-permute-start.10 = (bf16[1,16,32,256]{3,2,1,0:T(8,128)(2,1)S(1)}, bf16[1,16,32,256]{3,2,1,0:T(8,128)(2,1)S(1)}, u32[]{:S(2)}, u32[]{:S(2)}) collective-permute-start(bf16[1,16,32,256]{3,2,1,0:T(8,128)(2,1)S(1)} %get-tuple-element.51), channel_id=1, source_target_pairs={{0,8},{8,0},{16,24},{24,16},{1,9},{9,1},{17,25},{25,17},{2,10},{10... | collective-permute-start | bytes 786440 | tf_op jit(solution)/shard_map/ppermute | solution.py:292
  52.2 11.5 %collective-permute-start.11 = (bf16[1,16,32,256]{3,2,1,0:T(8,128)(2,1)S(1)}, bf16[1,16,32,256]{3,2,1,0:T(8,128)(2,1)S(1)}, u32[]{:S(2)}, u32[]{:S(2)}) collective-permute-start(bf16[1,16,32,256]{3,2,1,0:T(8,128)(2,1)S(1)} %get-tuple-element.52), channel_id=1, source_target_pairs={{0,16},{8,24},{16,0},{24,8},{1,17},{9,25},{17,1},{25,9},{2,18},{10... | collective-permute-start | bytes 786440 | tf_op jit(solution)/shard_map/ppermute | solution.py:292
  52.2 11.5 %collective-permute-start.12 = (bf16[1,16,32,256]{3,2,1,0:T(8,128)(2,1)S(1)}, bf16[1,16,32,256]{3,2,1,0:T(8,128)(2,1)S(1)}, u32[]{:S(2)}, u32[]{:S(2)}) collective-permute-start(bf16[1,16,32,256]{3,2,1,0:T(8,128)(2,1)S(1)} %get-tuple-element.53), channel_id=1, source_target_pairs={{0,24},{8,16},{16,8},{24,0},{1,25},{9,17},{17,9},{25,1},{2,26},{10... | collective-permute-start | bytes 786440 | tf_op jit(solution)/shard_map/ppermute | solution.py:292
  59.1 10.1 %collective-permute-start.9 = (f32[64,256]{1,0:T(8,128)S(1)}, f32[64,256]{1,0:T(8,128)S(1)}, u32[]{:S(2)}, u32[]{:S(2)}) collective-permute-start(f32[64,256]{1,0:T(8,128)S(1)} %pad_maximum_fusion), channel_id=1, source_target_pairs={{0,0},{1,1},{2,8},{3,9},{4,16},{5,17},{6,24},{7,25},{8,2},{9,3},{1... | collective-permute-start | bytes 196616 | tf_op jit(solution)/shard_map/ppermute | solution.py:285
  69.1 7.5 %collective-permute-start.13 = (f32[64,256]{1,0:T(8,128)S(1)}, f32[64,256]{1,0:T(8,128)S(1)}, u32[]{:S(2)}, u32[]{:S(2)}) collective-permute-start(f32[64,256]{1,0:T(8,128)S(1)} %pad_maximum_fusion.1), channel_id=1, source_target_pairs={{0,1},{1,0},{2,9},{3,8},{4,17},{5,16},{6,25},{7,24},{8,3},{9,2},{1... | collective-permute-start | bytes 196616 | tf_op jit(solution)/shard_map/ppermute | solution.py:285

commit v3 on v2

--- a/solution.py
+++ b/solution.py
@@ -337,18 +337,20 @@
         after(linear, *side),
     )
     blocks = [side[t * parts : (t + 1) * parts] for t in range(turns)]
+    def band_sums(t, got):
+        return pairs(base, groups, got, own_labels[t], factors, t, t)
+
     down[0] = after(down[0], *down[1:])
-    down_sums = [pairs(base, groups, down, own_labels[t], factors, t, t) for t in range(turns)]
+    down_sums = [band_sums(0, down)]
     arrived = []
     for t in range(turns):
         got = [blocks[t][0]]
         for k in far:
-            if t == 0:
-                waits = [factors] if k == 1 else []
-            else:
-                waits = [down_sums[min(t, turns - 1) if k == 1 else t - 1]]
+            waits = [] if t == 0 else down_sums[-1:]
             got.insert(1, exchange(after(blocks[t][k], *waits), k))
         arrived.append(got)
+    down[0] = after(down[0], arrived[0][1])
+    down_sums += [band_sums(t, down) for t in range(1, turns)]
     side_sums, pieces = [], []
     for t in range(turns):
         got = arrived[t]

time: 77.9 us -> 75.4 us (0.968)
  starting transfers between devices: 26.3 us -> 23.8 us
    ppermute x9, starting transfers between devices: 15 us -> 10.6 us  [exchange(): return lax.ppermute(block, 'cores', moves)]
    ppermute x4, starting transfers between devices: 10.1 us -> 11.9 us  [move(): return lax.ppermute(array, ('cores', 'strip'), moves)]
  transfers between devices with their start and end apart: 14 -> 14, of which waited for: 4 -> 4; matrix products, arithmetic and copies ran while one was open for 0% -> 0% of each run, Pallas kernels for 37% -> 38%
where the time goes in v3:
time: 75.4 us; the launch traced here: 75.2 us
  Pallas kernels  34.2 us (45%)
  starting transfers between devices  23.8 us (32%)
  waiting for transfers between devices  12.8 us (17%)
  local copies, waits for them, and re-layouts  2.65 us (4%)
  between operations  0.94 us (1%)
    pallas_call x4, Pallas kernels, pairs(): pl.pallas_call(functools.partial(pairs_kernel, scale=2.0 / (fields * (fie...  21.4 us
    ppermute x4, starting transfers between devices, move(): return lax.ppermute(array, ('cores', 'strip'), moves)  11.9 us
    pallas_call x3, Pallas kernels, on_tile(): pl.pallas_call(body, in_specs=[SMEM] * len(scalars) + specs, out_specs=ja...  11 us
    ppermute x4, waiting for transfers between devices, move(): return lax.ppermute(array, ('cores', 'strip'), moves)  10.7 us
    ppermute x9, starting transfers between devices, exchange(): return lax.ppermute(block, 'cores', moves)  10.6 us
    unnamed x14, local copies, waits for them, and re-layouts  2.22 us
    ppermute x9, waiting for transfers between devices, exchange(): return lax.ppermute(block, 'cores', moves)  2.14 us
  transfers between devices with their start and end apart: 14, of which 4 were waited for; matrix products, arithmetic and copies ran while one was open for 0% of the time, Pallas kernels for 38%

profile of v3, /device:TPU:6, one launch (start us, length us, event | category | flops | bytes accessed | tf_op | source)
XLA Modules:
  0.0 75.2 jit_solution(14867179080225864406)
XLA Ops:
  0.7 0.1 broadcast_add_fusion
  0.8 0.1 add.31
  0.8 0.6 pad_add_fusion.1.first_ref
  1.4 4.5 %down.1 = (bf16[2,16,32,256]{3,2,1,0:T(8,128)(2,1)}, bf16[2,16,32,256]{3,2,1,0:T(8,128)(2,1)}, bf16[2,16,32,256]{3,2,1,0:T(8,128)(2,1)}, bf16[2,16,32,256]{3,2,1,0:T(8,128)(2,1)}, f32[256,128]{1,0:T(8,128)}) custom-call(s32[9]{0:T(128)} %pad_add_fusion.1.first_ref, f32[16,256,256]{2,1,0:T(8,128)} %potentials_ref.3), custom_call_target="tpu_custom_call" | custom-call | flops 8388608 | bytes 12582912 | tf_op jit(solution)/shard_map/down/pallas_call | solution.py:220
  6.0 0.6 collective-permute-start
  6.6 0.0 collective-permute-start.1
  6.6 2.9 %collective-permute-start.2 = (bf16[2,16,32,256]{3,2,1,0:T(8,128)(2,1)}, bf16[2,16,32,256]{3,2,1,0:T(8,128)(2,1)S(1)}, u32[]{:S(2)}, u32[]{:S(2)}) collective-permute-start(bf16[2,16,32,256]{3,2,1,0:T(8,128)(2,1)} %get-tuple-element.34), channel_id=1, source_target_pairs={{0,24},{8,16},{16,8},{24,0},{1,25},{9,17},{17,9},{25,1},{2,26},{10... | collective-permute-start | bytes 1572872 | tf_op jit(solution)/shard_map/ppermute | solution.py:292
  9.5 5.4 %collective-permute-start.3 = (s32[32,512]{1,0:T(8,128)S(1)}, s32[32,512]{1,0:T(8,128)S(1)}, u32[]{:S(2)}, u32[]{:S(2)}) collective-permute-start(s32[32,512]{1,0:T(8,128)S(1)} %copy-done.6), channel_id=1, source_target_pairs={{0,0},{1,1},{2,8},{3,9},{4,16},{5,17},{6,24},{7,25},{8,2},{9,3},{1... | collective-permute-start | bytes 196616 | tf_op jit(solution)/shard_map/ppermute | solution.py:285
  15.0 1.3 %collective-permute-start.5 = (f32[256,128]{1,0:T(8,128)}, f32[256,128]{1,0:T(8,128)S(1)}, u32[]{:S(2)}, u32[]{:S(2)}) collective-permute-start(f32[256,128]{1,0:T(8,128)} %get-tuple-element.28), channel_id=1, source_target_pairs={{1,0},{2,1},{3,2},{4,3},{5,4},{6,5},{7,6},{9,8},{10,9},{11,10},{12... | collective-permute-start | bytes 393224 | tf_op jit(solution)/shard_map/ppermute | solution.py:310
  16.3 3.2 %collective-permute-done.3 = s32[32,512]{1,0:T(8,128)S(1)} collective-permute-done((s32[32,512]{1,0:T(8,128)S(1)}, s32[32,512]{1,0:T(8,128)S(1)}, u32[]{:S(2)}, u32[]{:S(2)}) %collective-permute-start.3) | collective-permute-done | bytes 65568 | tf_op jit(solution)/shard_map/ppermute | solution.py:285
  19.5 0.6 prepare.1
  20.1 0.2 copy.7
  20.3 0.2 reshape.21.groups_ref
  20.5 0.2 collective-permute-done.4.refs_4_
  20.7 2.2 %copy-done = f32[16,256,256]{2,1,0:T(8,128)S(1)} copy-done((f32[16,256,256]{2,1,0:T(8,128)S(1)}, f32[16,256,256]{2,1,0:T(8,128)}, u32[]{:S(2)}) %copy-start) | copy-done | bytes 4194328
  22.9 2.6 %side.1 = (bf16[1,16,32,256]{3,2,1,0:T(8,128)(2,1)S(1)}, bf16[1,16,32,256]{3,2,1,0:T(8,128)(2,1)S(1)}, bf16[1,16,32,256]{3,2,1,0:T(8,128)(2,1)S(1)}, bf16[1,16,3...) custom-call(s32[9]{0:T(128)S(1)} %copy-done.5, ...), custom_call_target="tpu_custom_call" | custom-call | flops 4325376 | bytes 6488064 | tf_op jit(solution)/shard_map/side/pallas_call | solution.py:220
  25.5 0.1 collective-permute-start.6
  25.6 0.1 collective-permute-start.8
  25.7 3.4 %collective-permute-start.7 = (bf16[1,16,32,256]{3,2,1,0:T(8,128)(2,1)S(1)}, bf16[1,16,32,256]{3,2,1,0:T(8,128)(2,1)S(1)}, u32[]{:S(2)}, u32[]{:S(2)}) collective-permute-start(bf16[1,16,32,256]{3,2,1,0:T(8,128)(2,1)S(1)} %get-tuple-element.41), channel_id=1, source_target_pairs={{0,16},{8,24},{16,0},{24,8},{1,17},{9,25},{17,1},{25,9},{2,18},{10... | collective-permute-start | bytes 786440 | tf_op jit(solution)/shard_map/ppermute | solution.py:292
  29.0 3.9 %factors.1.refs_5_ = bf16[2,64,32,256]{3,2,1,0:T(8,128)(2,1)S(1)} custom-call(s32[64,256]{1,0:T(8,128)S(1)} %pad_add_fusion.labels_ref, f32[64,128]{1,0:T(8,128)S(1)} %get-tuple-element.47.linear_ref), custom_call_target="tpu_custom_call" | custom-call | flops 98304 | bytes 147456 | tf_op jit(solution)/shard_map/factors/pallas_call | solution.py:220
  33.0 2.1 %collective-permute-done.2.refs_3_ = bf16[2,16,32,256]{3,2,1,0:T(8,128)(2,1)S(1)} collective-permute-done((bf16[2,16,32,256]{3,2,1,0:T(8,128)(2,1)}, bf16[2,16,32,256]{3,2,1,0:T(8,128)(2,1)S(1)}, u32[]{:S(2)}, u32[]{:S(2)}) %collective-permute-start.2) | collective-permute-done | bytes 524320 | tf_op jit(solution)/shard_map/ppermute | solution.py:292
  35.1 5.3 %pairs.4 = f32[32,256]{1,0:T(8,128)S(1)} custom-call(s32[4]{0:T(128)S(1)} %fusion.1.base_ref, s32[5120]{0:T(1024)S(1)} %reshape.21.groups_ref, bf16[2,16,32,256]{3,2,1,0:T(8,128)(2,1)S(1)} %copy-done.1, bf16[2,16,32,256]{3,2,1,0:T(8,128)(2,1)S(1)} %collective-permute-done.refs_1_, bf16[2,16,32,256]{3,2,1,0:T(8,128)(2,1)S(1)} %collective-permute-done.1.refs_2_, ...), custom_call_target="tpu_custom_call" | custom-call | flops 33554432 | bytes 2097152 | tf_op jit(solution)/shard_map/pairs/pallas_call | solution.py:142
  40.4 0.7 collective-permute-start.10
  41.2 2.8 %collective-permute-start.12 = (bf16[1,16,32,256]{3,2,1,0:T(8,128)(2,1)S(1)}, bf16[1,16,32,256]{3,2,1,0:T(8,128)(2,1)S(1)}, u32[]{:S(2)}, u32[]{:S(2)}) collective-permute-start(bf16[1,16,32,256]{3,2,1,0:T(8,128)(2,1)S(1)} %get-tuple-element.53), channel_id=1, source_target_pairs={{0,24},{8,16},{16,8},{24,0},{1,25},{9,17},{17,9},{25,1},{2,26},{10... | collective-permute-start | bytes 786440 | tf_op jit(solution)/shard_map/ppermute | solution.py:292
  44.0 5.3 %pairs.5 = f32[32,256]{1,0:T(8,128)S(1)} custom-call(s32[4]{0:T(128)S(1)} %fusion.1.base_ref, s32[5120]{0:T(1024)S(1)} %reshape.21.groups_ref, bf16[2,16,32,256]{3,2,1,0:T(8,128)(2,1)S(1)} %copy-done.1, bf16[2,16,32,256]{3,2,1,0:T(8,128)(2,1)S(1)} %collective-permute-done.refs_1_, bf16[2,16,32,256]{3,2,1,0:T(8,128)(2,1)S(1)} %collective-permute-done.1.refs_2_, ...), custom_call_target="tpu_custom_call" | custom-call | flops 33554432 | bytes 2097152 | tf_op jit(solution)/shard_map/pairs/pallas_call | solution.py:142
  49.3 0.0 copy-start.2
  49.4 5.4 %pairs.6 = f32[32,256]{1,0:T(8,128)S(1)} custom-call(s32[4]{0:T(128)S(1)} %fusion.1.base_ref, s32[5120]{0:T(1024)S(1)} %reshape.21.groups_ref, bf16[1,16,32,256]{3,2,1,0:T(8,128)(2,1)S(1)} %get-tuple-element.49.refs_0_, bf16[1,16,32,256]{3,2,1,0:T(8,128)(2,1)S(1)} %collective-permute-done.6.refs_1_, ...), custom_call_target="tpu_custom_call" | custom-call | flops 33554432 | bytes 2097152 | tf_op jit(solution)/shard_map/pairs/pallas_call | solution.py:142
  54.8 6.4 %collective-permute-start.9 = (f32[64,256]{1,0:T(8,128)S(1)}, f32[64,256]{1,0:T(8,128)S(1)}, u32[]{:S(2)}, u32[]{:S(2)}) collective-permute-start(f32[64,256]{1,0:T(8,128)S(1)} %pad_maximum_fusion), channel_id=1, source_target_pairs={{0,0},{1,1},{2,8},{3,9},{4,16},{5,17},{6,24},{7,25},{8,2},{9,3},{1... | collective-permute-start | bytes 196616 | tf_op jit(solution)/shard_map/ppermute | solution.py:285
  61.2 5.3 %pairs.7 = f32[32,256]{1,0:T(8,128)S(1)} custom-call(s32[4]{0:T(128)S(1)} %fusion.1.base_ref, s32[5120]{0:T(1024)S(1)} %reshape.21.groups_ref, bf16[1,16,32,256]{3,2,1,0:T(8,128)(2,1)S(1)} %get-tuple-element.50.refs_0_, bf16[1,16,32,256]{3,2,1,0:T(8,128)(2,1)S(1)} %collective-permute-done.10.refs_1_, ...), custom_call_target="tpu_custom_call" | custom-call | flops 33554432 | bytes 2097152 | tf_op jit(solution)/shard_map/pairs/pallas_call | solution.py:142
  66.6 0.1 collective-permute-start.13
  66.7 7.3 %collective-permute-done.13.refs_1_ = f32[64,256]{1,0:T(8,128)S(1)} collective-permute-done((f32[64,256]{1,0:T(8,128)S(1)}, f32[64,256]{1,0:T(8,128)S(1)}, u32[]{:S(2)}, u32[]{:S(2)}) %collective-permute-start.13) | collective-permute-done | bytes 65568 | tf_op jit(solution)/shard_map/ppermute | solution.py:285
  74.0 1.2 %finish.1 = (f32[32,512]{1,0:T(8,128)}, f32[32,512]{1,0:T(8,128)}) custom-call(s32[2]{0:T(128)S(1)} %iota_xor_fusion.1.halves_ref, f32[64,256]{1,0:T(8,128)S(1)} %collective-permute-done.9.refs_0_, f32[64,256]{1,0:T(8,128)S(1)} %collective-permute-done.13.refs_1_, f32[32,512]{1,0:T(8,128)S(1)} %copy-done.2, f32[32,512]{1,0:T(8,128)S(1)} %copy-done.3), custom_call_target="tpu_custom_call" | custom-call | tf_op jit(solution)/shard_map/finish/pallas_call | solution.py:249
  (31 shorter events, 0.1 us)
Async XLA Ops:
  0.6 8.9 %copy-start.6 = (s32[32,512]{1,0:T(8,128)S(1)}, s32[32,512]{1,0:T(8,128)}, u32[]{:S(2)}) copy-start(s32[32,512]{1,0:T(8,128)} %param.7) | copy-start | bytes 196612
  0.6 18.8 %copy-start.4 = (s32[64,64]{1,0:T(8,128)S(1)}, s32[64,64]{1,0:T(8,128)}, u32[]{:S(2)}) copy-start(s32[64,64]{1,0:T(8,128)} %include_ref) | copy-start | bytes 49156
  1.4 19.2 %copy-start.5 = (s32[9]{0:T(128)S(1)}, s32[9]{0:T(128)}, u32[]{:S(2)}) copy-start(s32[9]{0:T(128)} %pad_add_fusion.1.first_ref) | copy-start | bytes 112
  6.0 29.1 %copy-start.1 = (bf16[2,16,32,256]{3,2,1,0:T(8,128)(2,1)S(1)}, bf16[2,16,32,256]{3,2,1,0:T(8,128)(2,1)}, u32[]{:S(2)}) copy-start(bf16[2,16,32,256]{3,2,1,0:T(8,128)(2,1)} %get-tuple-element.48.refs_0_) | copy-start | bytes 1572868
  6.0 19.7 %collective-permute-start = (bf16[2,16,32,256]{3,2,1,0:T(8,128)(2,1)}, bf16[2,16,32,256]{3,2,1,0:T(8,128)(2,1)S(1)}, u32[]{:S(2)}, u32[]{:S(2)}) collective-permute-start(bf16[2,16,32,256]{3,2,1,0:T(8,128)(2,1)} %get-tuple-element.32), channel_id=1, source_target_pairs={{0,8},{8,0},{16,24},{24,16},{1,9},{9,1},{17,25},{25,17},{2,10},{10... | collective-permute-start | bytes 1572872 | tf_op jit(solution)/shard_map/ppermute | solution.py:292
  6.6 26.4 %collective-permute-start.1 = (bf16[2,16,32,256]{3,2,1,0:T(8,128)(2,1)}, bf16[2,16,32,256]{3,2,1,0:T(8,128)(2,1)S(1)}, u32[]{:S(2)}, u32[]{:S(2)}) collective-permute-start(bf16[2,16,32,256]{3,2,1,0:T(8,128)(2,1)} %get-tuple-element.33), channel_id=1, source_target_pairs={{0,16},{8,24},{16,0},{24,8},{1,17},{9,25},{17,1},{25,9},{2,18},{10... | collective-permute-start | bytes 1572872 | tf_op jit(solution)/shard_map/ppermute | solution.py:292
  6.6 28.5 %collective-permute-start.2 = (bf16[2,16,32,256]{3,2,1,0:T(8,128)(2,1)}, bf16[2,16,32,256]{3,2,1,0:T(8,128)(2,1)S(1)}, u32[]{:S(2)}, u32[]{:S(2)}) collective-permute-start(bf16[2,16,32,256]{3,2,1,0:T(8,128)(2,1)} %get-tuple-element.34), channel_id=1, source_target_pairs={{0,24},{8,16},{16,8},{24,0},{1,25},{9,17},{17,9},{25,1},{2,26},{10... | collective-permute-start | bytes 1572872 | tf_op jit(solution)/shard_map/ppermute | solution.py:292
  9.5 9.9 %collective-permute-start.3 = (s32[32,512]{1,0:T(8,128)S(1)}, s32[32,512]{1,0:T(8,128)S(1)}, u32[]{:S(2)}, u32[]{:S(2)}) collective-permute-start(s32[32,512]{1,0:T(8,128)S(1)} %copy-done.6), channel_id=1, source_target_pairs={{0,0},{1,1},{2,8},{3,9},{4,16},{5,17},{6,24},{7,25},{8,2},{9,3},{1... | collective-permute-start | bytes 196616 | tf_op jit(solution)/shard_map/ppermute | solution.py:285
  15.0 5.7 %collective-permute-start.5 = (f32[256,128]{1,0:T(8,128)}, f32[256,128]{1,0:T(8,128)S(1)}, u32[]{:S(2)}, u32[]{:S(2)}) collective-permute-start(f32[256,128]{1,0:T(8,128)} %get-tuple-element.28), channel_id=1, source_target_pairs={{1,0},{2,1},{3,2},{4,3},{5,4},{6,5},{7,6},{9,8},{10,9},{11,10},{12... | collective-permute-start | bytes 393224 | tf_op jit(solution)/shard_map/ppermute | solution.py:310
  19.5 1.2 %collective-permute-start.4 = (s32[32,256]{1,0:T(8,128)S(1)}, s32[32,256]{1,0:T(8,128)S(1)}, u32[]{:S(2)}, u32[]{:S(2)}) collective-permute-start(s32[32,256]{1,0:T(8,128)S(1)} %get-tuple-element.54), channel_id=1, source_target_pairs={{0,1},{1,0},{2,3},{3,2},{4,5},{5,4},{6,7},{7,6},{8,9},{9,8},{10,11... | collective-permute-start | bytes 98312 | tf_op jit(solution)/shard_map/ppermute | solution.py:285
  20.7 2.2 %copy-start = (f32[16,256,256]{2,1,0:T(8,128)S(1)}, f32[16,256,256]{2,1,0:T(8,128)}, u32[]{:S(2)}) copy-start(f32[16,256,256]{2,1,0:T(8,128)} %potentials_ref.3) | copy-start | bytes 12582916
  25.5 15.7 %collective-permute-start.6 = (bf16[1,16,32,256]{3,2,1,0:T(8,128)(2,1)S(1)}, bf16[1,16,32,256]{3,2,1,0:T(8,128)(2,1)S(1)}, u32[]{:S(2)}, u32[]{:S(2)}) collective-permute-start(bf16[1,16,32,256]{3,2,1,0:T(8,128)(2,1)S(1)} %get-tuple-element.40), channel_id=1, source_target_pairs={{0,8},{8,0},{16,24},{24,16},{1,9},{9,1},{17,25},{25,17},{2,10},{10... | collective-permute-start | bytes 786440 | tf_op jit(solution)/shard_map/ppermute | solution.py:292
  25.6 23.8 %collective-permute-start.8 = (bf16[1,16,32,256]{3,2,1,0:T(8,128)(2,1)S(1)}, bf16[1,16,32,256]{3,2,1,0:T(8,128)(2,1)S(1)}, u32[]{:S(2)}, u32[]{:S(2)}) collective-permute-start(bf16[1,16,32,256]{3,2,1,0:T(8,128)(2,1)S(1)} %get-tuple-element.42), channel_id=1, source_target_pairs={{0,24},{8,16},{16,8},{24,0},{1,25},{9,17},{17,9},{25,1},{2,26},{10... | collective-permute-start | bytes 786440 | tf_op jit(solution)/shard_map/ppermute | solution.py:292
  25.7 23.7 %collective-permute-start.7 = (bf16[1,16,32,256]{3,2,1,0:T(8,128)(2,1)S(1)}, bf16[1,16,32,256]{3,2,1,0:T(8,128)(2,1)S(1)}, u32[]{:S(2)}, u32[]{:S(2)}) collective-permute-start(bf16[1,16,32,256]{3,2,1,0:T(8,128)(2,1)S(1)} %get-tuple-element.41), channel_id=1, source_target_pairs={{0,16},{8,24},{16,0},{24,8},{1,17},{9,25},{17,1},{25,9},{2,18},{10... | collective-permute-start | bytes 786440 | tf_op jit(solution)/shard_map/ppermute | solution.py:292
  40.4 20.8 %collective-permute-start.10 = (bf16[1,16,32,256]{3,2,1,0:T(8,128)(2,1)S(1)}, bf16[1,16,32,256]{3,2,1,0:T(8,128)(2,1)S(1)}, u32[]{:S(2)}, u32[]{:S(2)}) collective-permute-start(bf16[1,16,32,256]{3,2,1,0:T(8,128)(2,1)S(1)} %get-tuple-element.51), channel_id=1, source_target_pairs={{0,8},{8,0},{16,24},{24,16},{1,9},{9,1},{17,25},{25,17},{2,10},{10... | collective-permute-start | bytes 786440 | tf_op jit(solution)/shard_map/ppermute | solution.py:292
  41.2 20.0 %collective-permute-start.11 = (bf16[1,16,32,256]{3,2,1,0:T(8,128)(2,1)S(1)}, bf16[1,16,32,256]{3,2,1,0:T(8,128)(2,1)S(1)}, u32[]{:S(2)}, u32[]{:S(2)}) collective-permute-start(bf16[1,16,32,256]{3,2,1,0:T(8,128)(2,1)S(1)} %get-tuple-element.52), channel_id=1, source_target_pairs={{0,16},{8,24},{16,0},{24,8},{1,17},{9,25},{17,1},{25,9},{2,18},{10... | collective-permute-start | bytes 786440 | tf_op jit(solution)/shard_map/ppermute | solution.py:292
  41.2 20.0 %collective-permute-start.12 = (bf16[1,16,32,256]{3,2,1,0:T(8,128)(2,1)S(1)}, bf16[1,16,32,256]{3,2,1,0:T(8,128)(2,1)S(1)}, u32[]{:S(2)}, u32[]{:S(2)}) collective-permute-start(bf16[1,16,32,256]{3,2,1,0:T(8,128)(2,1)S(1)} %get-tuple-element.53), channel_id=1, source_target_pairs={{0,24},{8,16},{16,8},{24,0},{1,25},{9,17},{17,9},{25,1},{2,26},{10... | collective-permute-start | bytes 786440 | tf_op jit(solution)/shard_map/ppermute | solution.py:292
  49.3 24.6 %copy-start.2 = (f32[32,512]{1,0:T(8,128)S(1)}, f32[32,512]{1,0:T(8,128)}, u32[]{:S(2)}) copy-start(f32[32,512]{1,0:T(8,128)} %refs_2_.1) | copy-start | bytes 196612
  49.3 24.6 %copy-start.3 = (f32[32,512]{1,0:T(8,128)S(1)}, f32[32,512]{1,0:T(8,128)}, u32[]{:S(2)}) copy-start(f32[32,512]{1,0:T(8,128)} %refs_3_.1) | copy-start | bytes 196612
  54.8 11.9 %collective-permute-start.9 = (f32[64,256]{1,0:T(8,128)S(1)}, f32[64,256]{1,0:T(8,128)S(1)}, u32[]{:S(2)}, u32[]{:S(2)}) collective-permute-start(f32[64,256]{1,0:T(8,128)S(1)} %pad_maximum_fusion), channel_id=1, source_target_pairs={{0,0},{1,1},{2,8},{3,9},{4,16},{5,17},{6,24},{7,25},{8,2},{9,3},{1... | collective-permute-start | bytes 196616 | tf_op jit(solution)/shard_map/ppermute | solution.py:285
  66.6 7.4 %collective-permute-start.13 = (f32[64,256]{1,0:T(8,128)S(1)}, f32[64,256]{1,0:T(8,128)S(1)}, u32[]{:S(2)}, u32[]{:S(2)}) collective-permute-start(f32[64,256]{1,0:T(8,128)S(1)} %pad_maximum_fusion.1), channel_id=1, source_target_pairs={{0,1},{1,0},{2,9},{3,8},{4,17},{5,16},{6,25},{7,24},{8,3},{9,2},{1... | collective-permute-start | bytes 196616 | tf_op jit(solution)/shard_map/ppermute | solution.py:285

commit v4 on v3

--- a/solution.py
+++ b/solution.py
@@ -37,9 +37,12 @@
     lower = jnp.where(column < row, 1.0, 0.0)
     eye = jnp.where(column == row, 1.0, 0.0)
     included = jnp.where(column > row, include_ref[...], 0).astype(f32)
-    place = dot(included, upper, (1, 0))
     both = included + dot(included, eye, (0, 0))
-    count = jnp.sum(included, axis=1, keepdims=True)
+    many = jnp.sum(jnp.sum(included, axis=1, keepdims=True), axis=0, keepdims=True)
+    rest = jnp.where(many > fields * (fields - 1) / 4, 1.0, 0.0)
+    listed = jnp.where(rest > 0, upper - included, included)
+    place = dot(listed, upper, (1, 0))
+    count = jnp.sum(listed, axis=1, keepdims=True)
     degree = jnp.sum(both, axis=1, keepdims=True)
     groups = jnp.floor((count + (PARTNERS - 1)) * (1.0 / PARTNERS))
     start = dot(lower, jnp.broadcast_to(groups, (fields, LANES)), (1, 0))[:, :1]
@@ -50,7 +53,7 @@
     used = jnp.sum(inside, axis=0, keepdims=True)
     own = jnp.sum(inside * ids, axis=0, keepdims=True)
     first = jnp.sum(inside * (slot - start) * PARTNERS, axis=0, keepdims=True)
-    places = dot(jnp.where(included > 0, place, -8.0), inside, (0, 0))
+    places = dot(jnp.where(listed > 0, place, -8.0), inside, (0, 0))
     places = jnp.where(used > 0, places, -8.0)
     groups_ref[...] = jnp.zeros(groups_ref.shape, jnp.int32)
     for u in range(PARTNERS):
@@ -64,8 +67,11 @@
     groups_ref[PARTNERS + 1 : PARTNERS + 2, :] = jnp.broadcast_to(total, (1, slots)).astype(
         jnp.int32
     )
+    groups_ref[PARTNERS + 2 : PARTNERS + 3, :] = jnp.broadcast_to(rest, (1, slots)).astype(
+        jnp.int32
+    )
     lanes = linear_ref.shape[1]
-    padding = 2.0 * (groups * PARTNERS - count)
+    padding = (2.0 - 4.0 * rest) * (groups * PARTNERS - count)
     wide = jnp.concatenate([both, jnp.zeros((fields, lanes - fields), f32)], axis=1)
     row = lax.broadcasted_iota(jnp.int32, (fields, lanes), 0)
     column = lax.broadcasted_iota(jnp.int32, (fields, lanes), 1)
@@ -108,8 +114,66 @@
     lax.fori_loop(0, fields, one, 0, unroll=4)
 
 
+def sort_steps(size):
+    p = 1
+    while p < size:
+        k = p
+        while k >= 1:
+            for j in range(k % p, size - k, 2 * k):
+                for i in range(min(k, size - j - k)):
+                    if (i + j) // (2 * p) == (i + j + k) // (2 * p):
+                        yield i + j, i + j + k
+            k //= 2
+        p *= 2
+
+
+def compare(values, steps):
+    for i, j in steps:
+        low = jnp.minimum(values[i], values[j])
+        values[j] = jnp.maximum(values[i], values[j])
+        values[i] = low
+    return values
+
+
+def merge_steps(size):
+    k = size // 2
+    while k >= 1:
+        for i in range(size):
+            if not i & k:
+                yield i, i + k
+        k //= 2
+
+
+def rank_sums(ranked, out_ref):
+    fields, rows, width = ranked.shape
+    half = fields // 2
+    columns = width // LANES
+
+    def block(number, carry):
+        place = (
+            pl.ds(pl.multiple_of(number // columns * 16, 16), 16),
+            pl.ds(pl.multiple_of(number % columns * LANES, LANES), LANES),
+        )
+        for start in (0, half):
+            values = [ranked[(start + i, *place)] for i in range(half)]
+            for i, value in enumerate(compare(values, sort_steps(half))):
+                ranked[(start + i, *place)] = value
+        total = jnp.zeros((16, LANES), jnp.float32)
+        for start, pick in ((0, jnp.minimum), (half, jnp.maximum)):
+            values = [
+                pick(ranked[(i, *place)], ranked[(fields - 1 - i, *place)]) for i in range(half)
+            ]
+            for i, value in enumerate(compare(values, merge_steps(half))):
+                if start + i:
+                    total = total + value.astype(jnp.float32) * float(start + i)
+        out_ref[place] = total
+        return carry
+
+    lax.fori_loop(0, rows // 16 * columns, block, 0)
+
+
 def pairs_kernel(base_ref, groups_ref, *refs, scale, unroll, at_turn, label_turn):
-    *parts, labels_ref, factors_ref, out_ref, held = refs
+    *parts, labels_ref, factors_ref, out_ref, held, ranked = refs
     fields = factors_ref.shape[1]
     _, each, rows, width = parts[0].shape
     held[fields] = jnp.full((rows, width), LOW, jnp.float32)
@@ -121,7 +185,14 @@
             field = base_ref[k] + i
             values = jnp.where(labels == field, LOW, part[at_turn, i].astype(jnp.float32))
             held[field] = values
+            ranked[k * each + i] = values.astype(jnp.bfloat16)
             linear = linear + factors_ref[label_turn, field].astype(jnp.float32) * values
+
+    out_ref[...] = jnp.zeros((rows, width), jnp.float32)
+
+    @pl.when(groups_ref[PARTNERS + 2] == 1)
+    def _():
+        rank_sums(ranked, out_ref)
 
     def step(number, total):
         for v in range(unroll):
@@ -133,7 +204,8 @@
 
     steps = (groups_ref[PARTNERS + 1] + (unroll - 1)) // unroll
     total = lax.fori_loop(0, steps, step, jnp.zeros((rows, width), jnp.float32))
-    out_ref[...] = (2.0 * total - linear) * scale
+    sign = 1.0 - 2.0 * groups_ref[PARTNERS + 2].astype(jnp.float32)
+    out_ref[...] = (2.0 * (out_ref[...] + sign * total) - linear) * scale
 
 
 def pairs(base, groups, parts, labels, factors, at_turn, label_turn):
@@ -150,7 +222,10 @@
         in_specs=[SMEM, SMEM] + [VMEM] * (len(parts) + 2),
         out_specs=VMEM,
         out_shape=jax.ShapeDtypeStruct(labels.shape, jnp.float32),
-        scratch_shapes=[pltpu.VMEM((fields + 2, *labels.shape), jnp.float32)],
+        scratch_shapes=[
+            pltpu.VMEM((fields + 2, *labels.shape), jnp.float32),
+            pltpu.VMEM((fields, *labels.shape), jnp.bfloat16),
+        ],
         compiler_params=LIMIT,
         cost_estimate=pl.CostEstimate(flops=work, bytes_accessed=work // 16, transcendentals=0),
         name="pairs",
@@ -285,7 +360,9 @@
         return lax.ppermute(array, ("cores", "strip"), moves)
 
     def send_home(array, turn):
-        return move(array, lambda c, g, j: (g, c, towards(j, turn, turns)))
+        return move(
+            array, lambda c, g, j: (g, towards(c, g, parts), towards(j, turn, turns))
+        )
 
     def exchange(block, k):
         moves = [(i, towards(i, k, parts)) for i in range(parts)]
@@ -295,7 +372,8 @@
     ts = jnp.arange(turns, dtype=jnp.int32)
     ks = jnp.arange(parts, dtype=jnp.int32)
     base = source(core, ks, parts) * each
-    first = towards(core, ks, parts)[:, None] * turns + towards(inside, ts, turns)[None]
+    region = towards(towards(core, ks, parts), strip // turns, parts)
+    first = region[:, None] * turns + towards(inside, ts, turns)[None]
     last = (strip == strips - 1).astype(jnp.int32)
     first = jnp.concatenate([first.reshape(-1), last[None]])
     halves = source(inside, ts, turns)
@@ -306,9 +384,10 @@
         down_kernel, "down", [block] * parts + [column], [first], fields=potentials
     )
     far = list(range(parts - 1, 0, -1))
+    beside = lax.ppermute(edge, "strip", [(i, i - 1) for i in range(1, strips)])
+    labels = move(labels, lambda c, g, j: (source(g, c, parts), c, j))
+    down = after(tuple(down), labels)
     down = [down[0], *[exchange(down[k], k) for k in far][::-1]]
-    beside = lax.ppermute(edge, "strip", [(i, i - 1) for i in range(1, strips)])
-    labels = move(after(labels, edge), lambda c, g, j: (g, c, j))
     groups, linear = prepare(after(pair_include, edge))
 
     own_labels = []
@@ -346,7 +425,7 @@
     for t in range(turns):
         got = [blocks[t][0]]
         for k in far:
-            waits = [] if t == 0 else down_sums[-1:]
+            waits = [factors] if t == 0 else down_sums[-1:]
             got.insert(1, exchange(after(blocks[t][k], *waits), k))
         arrived.append(got)
     down[0] = after(down[0], arrived[0][1])

time: 75.4 us -> 73.2 us (0.971)
  Pallas kernels: 34.2 us -> 32 us
  starting transfers between devices: 23.8 us -> 22.3 us
  waiting for transfers between devices: 12.8 us -> 13.7 us
    ppermute x4, waiting for transfers between devices: 10.7 us -> 5.47 us  [move(): return lax.ppermute(array, ('cores', 'strip'), moves)]
    ppermute x9, waiting for transfers between devices: 2.14 us -> 7.16 us  [exchange(): return lax.ppermute(block, 'cores', moves)]
    pallas_call x4, Pallas kernels: 21.4 us -> 19 us  [pairs(): pl.pallas_call(functools.partial(pairs_kernel, scale=2.0 / (fields * (fie...]
    ppermute x4, starting transfers between devices: 11.9 us -> 9.93 us  [move(): return lax.ppermute(array, ('cores', 'strip'), moves)]
    ppermute x1, waiting for transfers between devices: 0.01 us -> 1.03 us  [local(): beside = lax.ppermute(edge, 'strip', [(i, i - 1) for i in range(1, strips)])]
    unnamed x14 -> x12, local copies, waits for them, and re-layouts: 2.22 us -> 2.21 us
  transfers between devices with their start and end apart: 14 -> 14, of which waited for: 4 -> 3; matrix products, arithmetic and copies ran while one was open for 0% -> 2% of each run, Pallas kernels for 38% -> 43%
where the time goes in v4:
time: 73.2 us; the launch traced here: 72.2 us
  Pallas kernels  32 us (44%)
  starting transfers between devices  22.3 us (30%)
  waiting for transfers between devices  13.7 us (19%)
  local copies, waits for them, and re-layouts  2.64 us (4%)
  between operations  0.93 us (1%)
    pallas_call x4, Pallas kernels, pairs(): pl.pallas_call(functools.partial(pairs_kernel, scale=2.0 / (fields * (fie...  19 us
    ppermute x9, starting transfers between devices, exchange(): return lax.ppermute(block, 'cores', moves)  11.1 us
    pallas_call x3, Pallas kernels, on_tile(): pl.pallas_call(body, in_specs=[SMEM] * len(scalars) + specs, out_specs=ja...  11 us
    ppermute x4, starting transfers between devices, move(): return lax.ppermute(array, ('cores', 'strip'), moves)  9.93 us
    ppermute x9, waiting for transfers between devices, exchange(): return lax.ppermute(block, 'cores', moves)  7.16 us
    ppermute x4, waiting for transfers between devices, move(): return lax.ppermute(array, ('cores', 'strip'), moves)  5.47 us
    unnamed x12, local copies, waits for them, and re-layouts  2.21 us
  transfers between devices with their start and end apart: 14, of which 3 were waited for; matrix products, arithmetic and copies ran while one was open for 2% of the time, Pallas kernels for 43%

profile of v4, /device:TPU:6, one launch (start us, length us, event | category | flops | bytes accessed | tf_op | source)
XLA Modules:
  0.0 72.2 jit_solution(11455283770251834765)
XLA Ops:
  0.6 5.5 %collective-permute-start = (s32[32,512]{1,0:T(8,128)}, s32[32,512]{1,0:T(8,128)S(1)}, u32[]{:S(2)}, u32[]{:S(2)}) collective-permute-start(s32[32,512]{1,0:T(8,128)} %param.7), channel_id=1, source_target_pairs={{0,0},{1,1},{2,8},{3,9},{4,16},{5,17},{6,24},{7,25},{8,10},{9,11},... | collective-permute-start | bytes 196616 | tf_op jit(solution)/shard_map/ppermute | solution.py:360
  6.2 0.1 broadcast_add_fusion
  6.3 0.1 add.32
  6.4 0.6 pad_add_fusion.1.first_ref
  7.0 4.5 %down.1 = (bf16[2,16,32,256]{3,2,1,0:T(8,128)(2,1)}, bf16[2,16,32,256]{3,2,1,0:T(8,128)(2,1)}, bf16[2,16,32,256]{3,2,1,0:T(8,128)(2,1)}, bf16[2,16,32,256]{3,2,1,0:T(8,128)(2,1)}, f32[256,128]{1,0:T(8,128)}) custom-call(s32[9]{0:T(128)} %pad_add_fusion.1.first_ref, f32[16,256,256]{2,1,0:T(8,128)} %potentials_ref.3), custom_call_target="tpu_custom_call" | custom-call | flops 8388608 | bytes 12582912 | tf_op jit(solution)/shard_map/down/pallas_call | solution.py:295
  11.5 0.1 collective-permute-start.1
  11.6 0.1 collective-permute-start.2
  11.7 3.4 %collective-permute-start.3 = (bf16[2,16,32,256]{3,2,1,0:T(8,128)(2,1)}, bf16[2,16,32,256]{3,2,1,0:T(8,128)(2,1)S(1)}, u32[]{:S(2)}, u32[]{:S(2)}) collective-permute-start(bf16[2,16,32,256]{3,2,1,0:T(8,128)(2,1)} %get-tuple-element.44), channel_id=1, source_target_pairs={{0,24},{8,16},{16,8},{24,0},{1,25},{9,17},{17,9},{25,1},{2,26},{10... | collective-permute-start | bytes 1572872 | tf_op jit(solution)/shard_map/ppermute | solution.py:369
  15.1 1.3 %collective-permute-start.5 = (f32[256,128]{1,0:T(8,128)}, f32[256,128]{1,0:T(8,128)S(1)}, u32[]{:S(2)}, u32[]{:S(2)}) collective-permute-start(f32[256,128]{1,0:T(8,128)} %get-tuple-element.34), channel_id=1, source_target_pairs={{1,0},{2,1},{3,2},{4,3},{5,4},{6,5},{7,6},{9,8},{10,9},{11,10},{12... | collective-permute-start | bytes 393224 | tf_op jit(solution)/shard_map/ppermute | solution.py:387
  16.4 0.7 %prepare.1 = (s32[8,640]{1,0:T(8,128)S(1)}, f32[64,128]{1,0:T(8,128)S(1)}) custom-call(s32[64,64]{1,0:T(8,128)S(1)} %copy-done.4), custom_call_target="tpu_custom_call" | custom-call | tf_op jit(solution)/shard_map/prepare/pallas_call | solution.py:85
  17.1 0.2 copy.7
  17.3 0.2 reshape.22.groups_ref
  17.5 1.0 %collective-permute-done.5.beside_ref = f32[256,128]{1,0:T(8,128)S(1)} collective-permute-done((f32[256,128]{1,0:T(8,128)}, f32[256,128]{1,0:T(8,128)S(1)}, u32[]{:S(2)}, u32[]{:S(2)}) %collective-permute-start.5) | collective-permute-done | bytes 131104 | tf_op jit(solution)/shard_map/ppermute | solution.py:387
  18.5 2.2 %copy-done = f32[16,256,256]{2,1,0:T(8,128)S(1)} copy-done((f32[16,256,256]{2,1,0:T(8,128)S(1)}, f32[16,256,256]{2,1,0:T(8,128)}, u32[]{:S(2)}) %copy-start) | copy-done | bytes 4194328
  20.7 2.6 %side.1 = (bf16[1,16,32,256]{3,2,1,0:T(8,128)(2,1)S(1)}, bf16[1,16,32,256]{3,2,1,0:T(8,128)(2,1)S(1)}, bf16[1,16,32,256]{3,2,1,0:T(8,128)(2,1)S(1)}, bf16[1,16,3...) custom-call(s32[9]{0:T(128)S(1)} %copy-done.5, ...), custom_call_target="tpu_custom_call" | custom-call | flops 4325376 | bytes 6488064 | tf_op jit(solution)/shard_map/side/pallas_call | solution.py:295
  23.3 3.9 %factors.1.refs_5_ = bf16[2,64,32,256]{3,2,1,0:T(8,128)(2,1)S(1)} custom-call(s32[64,256]{1,0:T(8,128)S(1)} %pad_add_fusion.labels_ref, f32[64,128]{1,0:T(8,128)S(1)} %get-tuple-element.56.linear_ref), custom_call_target="tpu_custom_call" | custom-call | flops 98304 | bytes 147456 | tf_op jit(solution)/shard_map/factors/pallas_call | solution.py:295
  27.2 0.1 collective-permute-start.6
  27.4 0.6 collective-permute-start.7
  27.9 2.8 %collective-permute-start.8 = (bf16[1,16,32,256]{3,2,1,0:T(8,128)(2,1)S(1)}, bf16[1,16,32,256]{3,2,1,0:T(8,128)(2,1)S(1)}, u32[]{:S(2)}, u32[]{:S(2)}) collective-permute-start(bf16[1,16,32,256]{3,2,1,0:T(8,128)(2,1)S(1)} %get-tuple-element.61), channel_id=1, source_target_pairs={{0,24},{8,16},{16,8},{24,0},{1,25},{9,17},{17,9},{25,1},{2,26},{10... | collective-permute-start | bytes 786440 | tf_op jit(solution)/shard_map/ppermute | solution.py:369
  30.8 7.1 %collective-permute-done.2.refs_2_ = bf16[2,16,32,256]{3,2,1,0:T(8,128)(2,1)S(1)} collective-permute-done((bf16[2,16,32,256]{3,2,1,0:T(8,128)(2,1)}, bf16[2,16,32,256]{3,2,1,0:T(8,128)(2,1)S(1)}, u32[]{:S(2)}, u32[]{:S(2)}) %collective-permute-start.2) | collective-permute-done | bytes 524320 | tf_op jit(solution)/shard_map/ppermute | solution.py:369
  37.9 4.7 %pairs.4 = f32[32,256]{1,0:T(8,128)S(1)} custom-call(s32[4]{0:T(128)S(1)} %fusion.base_ref, s32[5120]{0:T(1024)S(1)} %reshape.22.groups_ref, bf16[2,16,32,256]{3,2,1,0:T(8,128)(2,1)S(1)} %copy-done.1, bf16[2,16,32,256]{3,2,1,0:T(8,128)(2,1)S(1)} %collective-permute-done.1.refs_1_, bf16[2,16,32,256]{3,2,1,0:T(8,128)(2,1)S(1)} %collective-permute-done.2.refs_2_, ...), custom_call_target="tpu_custom_call" | custom-call | flops 33554432 | bytes 2097152 | tf_op jit(solution)/shard_map/pairs/pallas_call | solution.py:214
  42.7 2.5 %collective-permute-start.10 = (bf16[1,16,32,256]{3,2,1,0:T(8,128)(2,1)S(1)}, bf16[1,16,32,256]{3,2,1,0:T(8,128)(2,1)S(1)}, u32[]{:S(2)}, u32[]{:S(2)}) collective-permute-start(bf16[1,16,32,256]{3,2,1,0:T(8,128)(2,1)S(1)} %get-tuple-element.63), channel_id=1, source_target_pairs={{0,8},{8,0},{16,24},{24,16},{1,9},{9,1},{17,25},{25,17},{2,10},{10... | collective-permute-start | bytes 786440 | tf_op jit(solution)/shard_map/ppermute | solution.py:369
  45.2 1.5 %collective-permute-start.12 = (bf16[1,16,32,256]{3,2,1,0:T(8,128)(2,1)S(1)}, bf16[1,16,32,256]{3,2,1,0:T(8,128)(2,1)S(1)}, u32[]{:S(2)}, u32[]{:S(2)}) collective-permute-start(bf16[1,16,32,256]{3,2,1,0:T(8,128)(2,1)S(1)} %get-tuple-element.65), channel_id=1, source_target_pairs={{0,24},{8,16},{16,8},{24,0},{1,25},{9,17},{17,9},{25,1},{2,26},{10... | collective-permute-start | bytes 786440 | tf_op jit(solution)/shard_map/ppermute | solution.py:369
  46.7 4.7 %pairs.5 = f32[32,256]{1,0:T(8,128)S(1)} custom-call(s32[4]{0:T(128)S(1)} %fusion.base_ref, s32[5120]{0:T(1024)S(1)} %reshape.22.groups_ref, bf16[2,16,32,256]{3,2,1,0:T(8,128)(2,1)S(1)} %copy-done.1, bf16[2,16,32,256]{3,2,1,0:T(8,128)(2,1)S(1)} %collective-permute-done.1.refs_1_, bf16[2,16,32,256]{3,2,1,0:T(8,128)(2,1)S(1)} %collective-permute-done.2.refs_2_, ...), custom_call_target="tpu_custom_call" | custom-call | flops 33554432 | bytes 2097152 | tf_op jit(solution)/shard_map/pairs/pallas_call | solution.py:214
  51.5 0.0 copy-start.2
  51.5 0.0 copy-start.3
  51.5 4.8 %pairs.6 = f32[32,256]{1,0:T(8,128)S(1)} custom-call(s32[4]{0:T(128)S(1)} %fusion.base_ref, s32[5120]{0:T(1024)S(1)} %reshape.22.groups_ref, bf16[1,16,32,256]{3,2,1,0:T(8,128)(2,1)S(1)} %get-tuple-element.59.refs_0_, bf16[1,16,32,256]{3,2,1,0:T(8,128)(2,1)S(1)} %collective-permute-done.6.refs_1_, ...), custom_call_target="tpu_custom_call" | custom-call | flops 33554432 | bytes 2097152 | tf_op jit(solution)/shard_map/pairs/pallas_call | solution.py:214
  56.3 4.4 %collective-permute-start.9 = (f32[64,256]{1,0:T(8,128)S(1)}, f32[64,256]{1,0:T(8,128)S(1)}, u32[]{:S(2)}, u32[]{:S(2)}) collective-permute-start(f32[64,256]{1,0:T(8,128)S(1)} %pad_maximum_fusion), channel_id=1, source_target_pairs={{0,0},{1,1},{2,10},{3,11},{4,20},{5,21},{6,30},{7,31},{8,2},{9,3},... | collective-permute-start | bytes 196616 | tf_op jit(solution)/shard_map/ppermute | solution.py:360
  60.7 4.8 %pairs.7 = f32[32,256]{1,0:T(8,128)S(1)} custom-call(s32[4]{0:T(128)S(1)} %fusion.base_ref, s32[5120]{0:T(1024)S(1)} %reshape.22.groups_ref, bf16[1,16,32,256]{3,2,1,0:T(8,128)(2,1)S(1)} %get-tuple-element.62.refs_0_, bf16[1,16,32,256]{3,2,1,0:T(8,128)(2,1)S(1)} %collective-permute-done.10.refs_1_, ...), custom_call_target="tpu_custom_call" | custom-call | flops 33554432 | bytes 2097152 | tf_op jit(solution)/shard_map/pairs/pallas_call | solution.py:214
  65.5 0.1 collective-permute-start.13
  65.6 5.5 %collective-permute-done.13.refs_1_ = f32[64,256]{1,0:T(8,128)S(1)} collective-permute-done((f32[64,256]{1,0:T(8,128)S(1)}, f32[64,256]{1,0:T(8,128)S(1)}, u32[]{:S(2)}, u32[]{:S(2)}) %collective-permute-start.13) | collective-permute-done | bytes 65568 | tf_op jit(solution)/shard_map/ppermute | solution.py:360
  71.0 1.2 %finish.1 = (f32[32,512]{1,0:T(8,128)}, f32[32,512]{1,0:T(8,128)}) custom-call(s32[2]{0:T(128)S(1)} %iota_xor_fusion.1.halves_ref, f32[64,256]{1,0:T(8,128)S(1)} %collective-permute-done.9.refs_0_, f32[64,256]{1,0:T(8,128)S(1)} %collective-permute-done.13.refs_1_, f32[32,512]{1,0:T(8,128)S(1)} %copy-done.2, f32[32,512]{1,0:T(8,128)S(1)} %copy-done.3), custom_call_target="tpu_custom_call" | custom-call | tf_op jit(solution)/shard_map/finish/pallas_call | solution.py:324
  (29 shorter events, 0.1 us)
Async XLA Ops:
  0.6 15.7 %copy-start.4 = (s32[64,64]{1,0:T(8,128)S(1)}, s32[64,64]{1,0:T(8,128)}, u32[]{:S(2)}) copy-start(s32[64,64]{1,0:T(8,128)} %include_ref) | copy-start | bytes 49156
  0.6 10.9 %collective-permute-start = (s32[32,512]{1,0:T(8,128)}, s32[32,512]{1,0:T(8,128)S(1)}, u32[]{:S(2)}, u32[]{:S(2)}) collective-permute-start(s32[32,512]{1,0:T(8,128)} %param.7), channel_id=1, source_target_pairs={{0,0},{1,1},{2,8},{3,9},{4,16},{5,17},{6,24},{7,25},{8,10},{9,11},... | collective-permute-start | bytes 196616 | tf_op jit(solution)/shard_map/ppermute | solution.py:360
  7.0 11.6 %copy-start.5 = (s32[9]{0:T(128)S(1)}, s32[9]{0:T(128)}, u32[]{:S(2)}) copy-start(s32[9]{0:T(128)} %pad_add_fusion.1.first_ref) | copy-start | bytes 112
  11.5 26.5 %copy-start.1 = (bf16[2,16,32,256]{3,2,1,0:T(8,128)(2,1)S(1)}, bf16[2,16,32,256]{3,2,1,0:T(8,128)(2,1)}, u32[]{:S(2)}) copy-start(bf16[2,16,32,256]{3,2,1,0:T(8,128)(2,1)} %get-tuple-element.58.refs_0_) | copy-start | bytes 1572868
  11.5 16.4 %collective-permute-start.1 = (bf16[2,16,32,256]{3,2,1,0:T(8,128)(2,1)}, bf16[2,16,32,256]{3,2,1,0:T(8,128)(2,1)S(1)}, u32[]{:S(2)}, u32[]{:S(2)}) collective-permute-start(bf16[2,16,32,256]{3,2,1,0:T(8,128)(2,1)} %get-tuple-element.42), channel_id=1, source_target_pairs={{0,8},{8,0},{16,24},{24,16},{1,9},{9,1},{17,25},{25,17},{2,10},{10... | collective-permute-start | bytes 1572872 | tf_op jit(solution)/shard_map/ppermute | solution.py:369
  11.6 26.4 %collective-permute-start.2 = (bf16[2,16,32,256]{3,2,1,0:T(8,128)(2,1)}, bf16[2,16,32,256]{3,2,1,0:T(8,128)(2,1)S(1)}, u32[]{:S(2)}, u32[]{:S(2)}) collective-permute-start(bf16[2,16,32,256]{3,2,1,0:T(8,128)(2,1)} %get-tuple-element.43), channel_id=1, source_target_pairs={{0,16},{8,24},{16,0},{24,8},{1,17},{9,25},{17,1},{25,9},{2,18},{10... | collective-permute-start | bytes 1572872 | tf_op jit(solution)/shard_map/ppermute | solution.py:369
  11.7 26.3 %collective-permute-start.3 = (bf16[2,16,32,256]{3,2,1,0:T(8,128)(2,1)}, bf16[2,16,32,256]{3,2,1,0:T(8,128)(2,1)S(1)}, u32[]{:S(2)}, u32[]{:S(2)}) collective-permute-start(bf16[2,16,32,256]{3,2,1,0:T(8,128)(2,1)} %get-tuple-element.44), channel_id=1, source_target_pairs={{0,24},{8,16},{16,8},{24,0},{1,25},{9,17},{17,9},{25,1},{2,26},{10... | collective-permute-start | bytes 1572872 | tf_op jit(solution)/shard_map/ppermute | solution.py:369
  15.1 2.4 %collective-permute-start.4 = (s32[32,256]{1,0:T(8,128)S(1)}, s32[32,256]{1,0:T(8,128)S(1)}, u32[]{:S(2)}, u32[]{:S(2)}) collective-permute-start(s32[32,256]{1,0:T(8,128)S(1)} %get-tuple-element.66), channel_id=1, source_target_pairs={{0,1},{1,0},{2,3},{3,2},{4,5},{5,4},{6,7},{7,6},{8,9},{9,8},{10,11... | collective-permute-start | bytes 98312 | tf_op jit(solution)/shard_map/ppermute | solution.py:360
  15.1 3.5 %collective-permute-start.5 = (f32[256,128]{1,0:T(8,128)}, f32[256,128]{1,0:T(8,128)S(1)}, u32[]{:S(2)}, u32[]{:S(2)}) collective-permute-start(f32[256,128]{1,0:T(8,128)} %get-tuple-element.34), channel_id=1, source_target_pairs={{1,0},{2,1},{3,2},{4,3},{5,4},{6,5},{7,6},{9,8},{10,9},{11,10},{12... | collective-permute-start | bytes 393224 | tf_op jit(solution)/shard_map/ppermute | solution.py:387
  18.5 2.2 %copy-start = (f32[16,256,256]{2,1,0:T(8,128)S(1)}, f32[16,256,256]{2,1,0:T(8,128)}, u32[]{:S(2)}) copy-start(f32[16,256,256]{2,1,0:T(8,128)} %potentials_ref.3) | copy-start | bytes 12582916
  27.2 17.9 %collective-permute-start.6 = (bf16[1,16,32,256]{3,2,1,0:T(8,128)(2,1)S(1)}, bf16[1,16,32,256]{3,2,1,0:T(8,128)(2,1)S(1)}, u32[]{:S(2)}, u32[]{:S(2)}) collective-permute-start(bf16[1,16,32,256]{3,2,1,0:T(8,128)(2,1)S(1)} %get-tuple-element.57), channel_id=1, source_target_pairs={{0,8},{8,0},{16,24},{24,16},{1,9},{9,1},{17,25},{25,17},{2,10},{10... | collective-permute-start | bytes 786440 | tf_op jit(solution)/shard_map/ppermute | solution.py:369
  27.4 24.1 %collective-permute-start.7 = (bf16[1,16,32,256]{3,2,1,0:T(8,128)(2,1)S(1)}, bf16[1,16,32,256]{3,2,1,0:T(8,128)(2,1)S(1)}, u32[]{:S(2)}, u32[]{:S(2)}) collective-permute-start(bf16[1,16,32,256]{3,2,1,0:T(8,128)(2,1)S(1)} %get-tuple-element.60), channel_id=1, source_target_pairs={{0,16},{8,24},{16,0},{24,8},{1,17},{9,25},{17,1},{25,9},{2,18},{10... | collective-permute-start | bytes 786440 | tf_op jit(solution)/shard_map/ppermute | solution.py:369
  27.9 23.5 %collective-permute-start.8 = (bf16[1,16,32,256]{3,2,1,0:T(8,128)(2,1)S(1)}, bf16[1,16,32,256]{3,2,1,0:T(8,128)(2,1)S(1)}, u32[]{:S(2)}, u32[]{:S(2)}) collective-permute-start(bf16[1,16,32,256]{3,2,1,0:T(8,128)(2,1)S(1)} %get-tuple-element.61), channel_id=1, source_target_pairs={{0,24},{8,16},{16,8},{24,0},{1,25},{9,17},{17,9},{25,1},{2,26},{10... | collective-permute-start | bytes 786440 | tf_op jit(solution)/shard_map/ppermute | solution.py:369
  42.7 17.9 %collective-permute-start.10 = (bf16[1,16,32,256]{3,2,1,0:T(8,128)(2,1)S(1)}, bf16[1,16,32,256]{3,2,1,0:T(8,128)(2,1)S(1)}, u32[]{:S(2)}, u32[]{:S(2)}) collective-permute-start(bf16[1,16,32,256]{3,2,1,0:T(8,128)(2,1)S(1)} %get-tuple-element.63), channel_id=1, source_target_pairs={{0,8},{8,0},{16,24},{24,16},{1,9},{9,1},{17,25},{25,17},{2,10},{10... | collective-permute-start | bytes 786440 | tf_op jit(solution)/shard_map/ppermute | solution.py:369
  45.2 15.5 %collective-permute-start.11 = (bf16[1,16,32,256]{3,2,1,0:T(8,128)(2,1)S(1)}, bf16[1,16,32,256]{3,2,1,0:T(8,128)(2,1)S(1)}, u32[]{:S(2)}, u32[]{:S(2)}) collective-permute-start(bf16[1,16,32,256]{3,2,1,0:T(8,128)(2,1)S(1)} %get-tuple-element.64), channel_id=1, source_target_pairs={{0,16},{8,24},{16,0},{24,8},{1,17},{9,25},{17,1},{25,9},{2,18},{10... | collective-permute-start | bytes 786440 | tf_op jit(solution)/shard_map/ppermute | solution.py:369
  45.2 15.5 %collective-permute-start.12 = (bf16[1,16,32,256]{3,2,1,0:T(8,128)(2,1)S(1)}, bf16[1,16,32,256]{3,2,1,0:T(8,128)(2,1)S(1)}, u32[]{:S(2)}, u32[]{:S(2)}) collective-permute-start(bf16[1,16,32,256]{3,2,1,0:T(8,128)(2,1)S(1)} %get-tuple-element.65), channel_id=1, source_target_pairs={{0,24},{8,16},{16,8},{24,0},{1,25},{9,17},{17,9},{25,1},{2,26},{10... | collective-permute-start | bytes 786440 | tf_op jit(solution)/shard_map/ppermute | solution.py:369
  51.5 19.6 %copy-start.2 = (f32[32,512]{1,0:T(8,128)S(1)}, f32[32,512]{1,0:T(8,128)}, u32[]{:S(2)}) copy-start(f32[32,512]{1,0:T(8,128)} %refs_2_.1) | copy-start | bytes 196612
  51.5 19.6 %copy-start.3 = (f32[32,512]{1,0:T(8,128)S(1)}, f32[32,512]{1,0:T(8,128)}, u32[]{:S(2)}) copy-start(f32[32,512]{1,0:T(8,128)} %refs_3_.1) | copy-start | bytes 196612
  56.3 9.3 %collective-permute-start.9 = (f32[64,256]{1,0:T(8,128)S(1)}, f32[64,256]{1,0:T(8,128)S(1)}, u32[]{:S(2)}, u32[]{:S(2)}) collective-permute-start(f32[64,256]{1,0:T(8,128)S(1)} %pad_maximum_fusion), channel_id=1, source_target_pairs={{0,0},{1,1},{2,10},{3,11},{4,20},{5,21},{6,30},{7,31},{8,2},{9,3},... | collective-permute-start | bytes 196616 | tf_op jit(solution)/shard_map/ppermute | solution.py:360
  65.5 5.5 %collective-permute-start.13 = (f32[64,256]{1,0:T(8,128)S(1)}, f32[64,256]{1,0:T(8,128)S(1)}, u32[]{:S(2)}, u32[]{:S(2)}) collective-permute-start(f32[64,256]{1,0:T(8,128)S(1)} %pad_maximum_fusion.1), channel_id=1, source_target_pairs={{0,1},{1,0},{2,11},{3,10},{4,21},{5,20},{6,31},{7,30},{8,3},{9,2},... | collective-permute-start | bytes 196616 | tf_op jit(solution)/shard_map/ppermute | solution.py:360

commit v5 on v4

--- a/solution.py
+++ b/solution.py
@@ -144,32 +144,33 @@
         k //= 2
 
 
-def rank_sums(ranked, out_ref):
-    fields, rows, width = ranked.shape
+def rank_sums(held, ranked, out_ref):
+    fields = ranked.shape[0]
+    rows, width = out_ref.shape
     half = fields // 2
     columns = width // LANES
 
     def block(number, carry):
         place = (
-            pl.ds(pl.multiple_of(number // columns * 16, 16), 16),
+            pl.ds(pl.multiple_of(number // columns * 8, 8), 8),
             pl.ds(pl.multiple_of(number % columns * LANES, LANES), LANES),
         )
         for start in (0, half):
-            values = [ranked[(start + i, *place)] for i in range(half)]
+            values = [held[(start + i, *place)] for i in range(half)]
             for i, value in enumerate(compare(values, sort_steps(half))):
-                ranked[(start + i, *place)] = value
-        total = jnp.zeros((16, LANES), jnp.float32)
+                ranked[start + i] = value
+        total = jnp.zeros((8, LANES), jnp.float32)
         for start, pick in ((0, jnp.minimum), (half, jnp.maximum)):
             values = [
-                pick(ranked[(i, *place)], ranked[(fields - 1 - i, *place)]) for i in range(half)
+                pick(ranked[i], ranked[fields - 1 - i]) for i in range(half)
             ]
             for i, value in enumerate(compare(values, merge_steps(half))):
                 if start + i:
-                    total = total + value.astype(jnp.float32) * float(start + i)
+                    total = total + value * float(start + i)
         out_ref[place] = total
         return carry
 
-    lax.fori_loop(0, rows // 16 * columns, block, 0)
+    lax.fori_loop(0, rows // 8 * columns, block, 0)
 
 
 def pairs_kernel(base_ref, groups_ref, *refs, scale, unroll, at_turn, label_turn):
@@ -185,14 +186,13 @@
             field = base_ref[k] + i
             values = jnp.where(labels == field, LOW, part[at_turn, i].astype(jnp.float32))
             held[field] = values
-            ranked[k * each + i] = values.astype(jnp.bfloat16)
             linear = linear + factors_ref[label_turn, field].astype(jnp.float32) * values
 
     out_ref[...] = jnp.zeros((rows, width), jnp.float32)
 
     @pl.when(groups_ref[PARTNERS + 2] == 1)
     def _():
-        rank_sums(ranked, out_ref)
+        rank_sums(held, ranked, out_ref)
 
     def step(number, total):
         for v in range(unroll):
@@ -224,7 +224,7 @@
         out_shape=jax.ShapeDtypeStruct(labels.shape, jnp.float32),
         scratch_shapes=[
             pltpu.VMEM((fields + 2, *labels.shape), jnp.float32),
-            pltpu.VMEM((fields, *labels.shape), jnp.bfloat16),
+            pltpu.VMEM((fields, 8, LANES), jnp.float32),
         ],
         compiler_params=LIMIT,
         cost_estimate=pl.CostEstimate(flops=work, bytes_accessed=work // 16, transcendentals=0),

time: 73.2 us -> 72.5 us (level)
  Pallas kernels: 32 us -> 31.1 us
    pallas_call x4, Pallas kernels: 19 us -> 18.1 us  [pairs(): pl.pallas_call(functools.partial(pairs_kernel, scale=2.0 / (fields * (fie...]
  transfers between devices with their start and end apart: 14 -> 14, of which waited for: 3 -> 3; matrix products, arithmetic and copies ran while one was open for 2% -> 2% of each run, Pallas kernels for 43% -> 42%
where the time goes in v5:
time: 72.5 us; the launch traced here: 71.3 us
  Pallas kernels  31.1 us (43%)
  starting transfers between devices  22.3 us (31%)
  waiting for transfers between devices  13.7 us (19%)
  local copies, waits for them, and re-layouts  2.64 us (4%)
  between operations  0.93 us (1%)
    pallas_call x4, Pallas kernels, pairs(): pl.pallas_call(functools.partial(pairs_kernel, scale=2.0 / (fields * (fie...  18.1 us
    ppermute x9, starting transfers between devices, exchange(): return lax.ppermute(block, 'cores', moves)  11.1 us
    pallas_call x3, Pallas kernels, on_tile(): pl.pallas_call(body, in_specs=[SMEM] * len(scalars) + specs, out_specs=ja...  11 us
    ppermute x4, starting transfers between devices, move(): return lax.ppermute(array, ('cores', 'strip'), moves)  9.93 us
    ppermute x9, waiting for transfers between devices, exchange(): return lax.ppermute(block, 'cores', moves)  7.16 us
    ppermute x4, waiting for transfers between devices, move(): return lax.ppermute(array, ('cores', 'strip'), moves)  5.47 us
    unnamed x12, local copies, waits for them, and re-layouts  2.21 us
  transfers between devices with their start and end apart: 14, of which 3 were waited for; matrix products, arithmetic and copies ran while one was open for 2% of the time, Pallas kernels for 42%

profile of v5, /device:TPU:6, one launch (start us, length us, event | category | flops | bytes accessed | tf_op | source)
XLA Modules:
  0.0 71.3 jit_solution(11819118724710807939)
XLA Ops:
  0.6 5.5 %collective-permute-start = (s32[32,512]{1,0:T(8,128)}, s32[32,512]{1,0:T(8,128)S(1)}, u32[]{:S(2)}, u32[]{:S(2)}) collective-permute-start(s32[32,512]{1,0:T(8,128)} %param.7), channel_id=1, source_target_pairs={{0,0},{1,1},{2,8},{3,9},{4,16},{5,17},{6,24},{7,25},{8,10},{9,11},... | collective-permute-start | bytes 196616 | tf_op jit(solution)/shard_map/ppermute | solution.py:360
  6.2 0.1 broadcast_add_fusion
  6.3 0.1 add.32
  6.4 0.6 pad_add_fusion.1.first_ref
  7.0 4.5 %down.1 = (bf16[2,16,32,256]{3,2,1,0:T(8,128)(2,1)}, bf16[2,16,32,256]{3,2,1,0:T(8,128)(2,1)}, bf16[2,16,32,256]{3,2,1,0:T(8,128)(2,1)}, bf16[2,16,32,256]{3,2,1,0:T(8,128)(2,1)}, f32[256,128]{1,0:T(8,128)}) custom-call(s32[9]{0:T(128)} %pad_add_fusion.1.first_ref, f32[16,256,256]{2,1,0:T(8,128)} %potentials_ref.3), custom_call_target="tpu_custom_call" | custom-call | flops 8388608 | bytes 12582912 | tf_op jit(solution)/shard_map/down/pallas_call | solution.py:295
  11.5 0.1 collective-permute-start.1
  11.6 0.1 collective-permute-start.2
  11.7 3.4 %collective-permute-start.3 = (bf16[2,16,32,256]{3,2,1,0:T(8,128)(2,1)}, bf16[2,16,32,256]{3,2,1,0:T(8,128)(2,1)S(1)}, u32[]{:S(2)}, u32[]{:S(2)}) collective-permute-start(bf16[2,16,32,256]{3,2,1,0:T(8,128)(2,1)} %get-tuple-element.44), channel_id=1, source_target_pairs={{0,24},{8,16},{16,8},{24,0},{1,25},{9,17},{17,9},{25,1},{2,26},{10... | collective-permute-start | bytes 1572872 | tf_op jit(solution)/shard_map/ppermute | solution.py:369
  15.1 1.3 %collective-permute-start.5 = (f32[256,128]{1,0:T(8,128)}, f32[256,128]{1,0:T(8,128)S(1)}, u32[]{:S(2)}, u32[]{:S(2)}) collective-permute-start(f32[256,128]{1,0:T(8,128)} %get-tuple-element.34), channel_id=1, source_target_pairs={{1,0},{2,1},{3,2},{4,3},{5,4},{6,5},{7,6},{9,8},{10,9},{11,10},{12... | collective-permute-start | bytes 393224 | tf_op jit(solution)/shard_map/ppermute | solution.py:387
  16.4 0.7 %prepare.1 = (s32[8,640]{1,0:T(8,128)S(1)}, f32[64,128]{1,0:T(8,128)S(1)}) custom-call(s32[64,64]{1,0:T(8,128)S(1)} %copy-done.4), custom_call_target="tpu_custom_call" | custom-call | tf_op jit(solution)/shard_map/prepare/pallas_call | solution.py:85
  17.1 0.2 copy.7
  17.3 0.2 reshape.22.groups_ref
  17.5 1.0 %collective-permute-done.5.beside_ref = f32[256,128]{1,0:T(8,128)S(1)} collective-permute-done((f32[256,128]{1,0:T(8,128)}, f32[256,128]{1,0:T(8,128)S(1)}, u32[]{:S(2)}, u32[]{:S(2)}) %collective-permute-start.5) | collective-permute-done | bytes 131104 | tf_op jit(solution)/shard_map/ppermute | solution.py:387
  18.5 2.2 %copy-done = f32[16,256,256]{2,1,0:T(8,128)S(1)} copy-done((f32[16,256,256]{2,1,0:T(8,128)S(1)}, f32[16,256,256]{2,1,0:T(8,128)}, u32[]{:S(2)}) %copy-start) | copy-done | bytes 4194328
  20.7 2.6 %side.1 = (bf16[1,16,32,256]{3,2,1,0:T(8,128)(2,1)S(1)}, bf16[1,16,32,256]{3,2,1,0:T(8,128)(2,1)S(1)}, bf16[1,16,32,256]{3,2,1,0:T(8,128)(2,1)S(1)}, bf16[1,16,3...) custom-call(s32[9]{0:T(128)S(1)} %copy-done.5, ...), custom_call_target="tpu_custom_call" | custom-call | flops 4325376 | bytes 6488064 | tf_op jit(solution)/shard_map/side/pallas_call | solution.py:295
  23.3 3.9 %factors.1.refs_5_ = bf16[2,64,32,256]{3,2,1,0:T(8,128)(2,1)S(1)} custom-call(s32[64,256]{1,0:T(8,128)S(1)} %pad_add_fusion.labels_ref, f32[64,128]{1,0:T(8,128)S(1)} %get-tuple-element.56.linear_ref), custom_call_target="tpu_custom_call" | custom-call | flops 98304 | bytes 147456 | tf_op jit(solution)/shard_map/factors/pallas_call | solution.py:295
  27.2 0.1 collective-permute-start.6
  27.4 0.6 collective-permute-start.7
  27.9 2.8 %collective-permute-start.8 = (bf16[1,16,32,256]{3,2,1,0:T(8,128)(2,1)S(1)}, bf16[1,16,32,256]{3,2,1,0:T(8,128)(2,1)S(1)}, u32[]{:S(2)}, u32[]{:S(2)}) collective-permute-start(bf16[1,16,32,256]{3,2,1,0:T(8,128)(2,1)S(1)} %get-tuple-element.61), channel_id=1, source_target_pairs={{0,24},{8,16},{16,8},{24,0},{1,25},{9,17},{17,9},{25,1},{2,26},{10... | collective-permute-start | bytes 786440 | tf_op jit(solution)/shard_map/ppermute | solution.py:369
  30.8 7.1 %collective-permute-done.2.refs_2_ = bf16[2,16,32,256]{3,2,1,0:T(8,128)(2,1)S(1)} collective-permute-done((bf16[2,16,32,256]{3,2,1,0:T(8,128)(2,1)}, bf16[2,16,32,256]{3,2,1,0:T(8,128)(2,1)S(1)}, u32[]{:S(2)}, u32[]{:S(2)}) %collective-permute-start.2) | collective-permute-done | bytes 524320 | tf_op jit(solution)/shard_map/ppermute | solution.py:369
  37.9 4.5 %pairs.4 = f32[32,256]{1,0:T(8,128)S(1)} custom-call(s32[4]{0:T(128)S(1)} %fusion.base_ref, s32[5120]{0:T(1024)S(1)} %reshape.22.groups_ref, bf16[2,16,32,256]{3,2,1,0:T(8,128)(2,1)S(1)} %copy-done.1, bf16[2,16,32,256]{3,2,1,0:T(8,128)(2,1)S(1)} %collective-permute-done.1.refs_1_, bf16[2,16,32,256]{3,2,1,0:T(8,128)(2,1)S(1)} %collective-permute-done.2.refs_2_, ...), custom_call_target="tpu_custom_call" | custom-call | flops 33554432 | bytes 2097152 | tf_op jit(solution)/shard_map/pairs/pallas_call | solution.py:214
  42.5 2.5 %collective-permute-start.10 = (bf16[1,16,32,256]{3,2,1,0:T(8,128)(2,1)S(1)}, bf16[1,16,32,256]{3,2,1,0:T(8,128)(2,1)S(1)}, u32[]{:S(2)}, u32[]{:S(2)}) collective-permute-start(bf16[1,16,32,256]{3,2,1,0:T(8,128)(2,1)S(1)} %get-tuple-element.63), channel_id=1, source_target_pairs={{0,8},{8,0},{16,24},{24,16},{1,9},{9,1},{17,25},{25,17},{2,10},{10... | collective-permute-start | bytes 786440 | tf_op jit(solution)/shard_map/ppermute | solution.py:369
  44.9 1.5 %collective-permute-start.12 = (bf16[1,16,32,256]{3,2,1,0:T(8,128)(2,1)S(1)}, bf16[1,16,32,256]{3,2,1,0:T(8,128)(2,1)S(1)}, u32[]{:S(2)}, u32[]{:S(2)}) collective-permute-start(bf16[1,16,32,256]{3,2,1,0:T(8,128)(2,1)S(1)} %get-tuple-element.65), channel_id=1, source_target_pairs={{0,24},{8,16},{16,8},{24,0},{1,25},{9,17},{17,9},{25,1},{2,26},{10... | collective-permute-start | bytes 786440 | tf_op jit(solution)/shard_map/ppermute | solution.py:369
  46.5 4.5 %pairs.5 = f32[32,256]{1,0:T(8,128)S(1)} custom-call(s32[4]{0:T(128)S(1)} %fusion.base_ref, s32[5120]{0:T(1024)S(1)} %reshape.22.groups_ref, bf16[2,16,32,256]{3,2,1,0:T(8,128)(2,1)S(1)} %copy-done.1, bf16[2,16,32,256]{3,2,1,0:T(8,128)(2,1)S(1)} %collective-permute-done.1.refs_1_, bf16[2,16,32,256]{3,2,1,0:T(8,128)(2,1)S(1)} %collective-permute-done.2.refs_2_, ...), custom_call_target="tpu_custom_call" | custom-call | flops 33554432 | bytes 2097152 | tf_op jit(solution)/shard_map/pairs/pallas_call | solution.py:214
  51.0 0.0 copy-start.2
  51.0 0.0 copy-start.3
  51.0 4.5 %pairs.6 = f32[32,256]{1,0:T(8,128)S(1)} custom-call(s32[4]{0:T(128)S(1)} %fusion.base_ref, s32[5120]{0:T(1024)S(1)} %reshape.22.groups_ref, bf16[1,16,32,256]{3,2,1,0:T(8,128)(2,1)S(1)} %get-tuple-element.59.refs_0_, bf16[1,16,32,256]{3,2,1,0:T(8,128)(2,1)S(1)} %collective-permute-done.6.refs_1_, ...), custom_call_target="tpu_custom_call" | custom-call | flops 33554432 | bytes 2097152 | tf_op jit(solution)/shard_map/pairs/pallas_call | solution.py:214
  55.6 4.4 %collective-permute-start.9 = (f32[64,256]{1,0:T(8,128)S(1)}, f32[64,256]{1,0:T(8,128)S(1)}, u32[]{:S(2)}, u32[]{:S(2)}) collective-permute-start(f32[64,256]{1,0:T(8,128)S(1)} %pad_maximum_fusion), channel_id=1, source_target_pairs={{0,0},{1,1},{2,10},{3,11},{4,20},{5,21},{6,30},{7,31},{8,2},{9,3},... | collective-permute-start | bytes 196616 | tf_op jit(solution)/shard_map/ppermute | solution.py:360
  60.0 4.5 %pairs.7 = f32[32,256]{1,0:T(8,128)S(1)} custom-call(s32[4]{0:T(128)S(1)} %fusion.base_ref, s32[5120]{0:T(1024)S(1)} %reshape.22.groups_ref, bf16[1,16,32,256]{3,2,1,0:T(8,128)(2,1)S(1)} %get-tuple-element.62.refs_0_, bf16[1,16,32,256]{3,2,1,0:T(8,128)(2,1)S(1)} %collective-permute-done.10.refs_1_, ...), custom_call_target="tpu_custom_call" | custom-call | flops 33554432 | bytes 2097152 | tf_op jit(solution)/shard_map/pairs/pallas_call | solution.py:214
  64.6 0.1 collective-permute-start.13
  64.6 5.5 %collective-permute-done.13.refs_1_ = f32[64,256]{1,0:T(8,128)S(1)} collective-permute-done((f32[64,256]{1,0:T(8,128)S(1)}, f32[64,256]{1,0:T(8,128)S(1)}, u32[]{:S(2)}, u32[]{:S(2)}) %collective-permute-start.13) | collective-permute-done | bytes 65568 | tf_op jit(solution)/shard_map/ppermute | solution.py:360
  70.1 1.2 %finish.1 = (f32[32,512]{1,0:T(8,128)}, f32[32,512]{1,0:T(8,128)}) custom-call(s32[2]{0:T(128)S(1)} %iota_xor_fusion.1.halves_ref, f32[64,256]{1,0:T(8,128)S(1)} %collective-permute-done.9.refs_0_, f32[64,256]{1,0:T(8,128)S(1)} %collective-permute-done.13.refs_1_, f32[32,512]{1,0:T(8,128)S(1)} %copy-done.2, f32[32,512]{1,0:T(8,128)S(1)} %copy-done.3), custom_call_target="tpu_custom_call" | custom-call | tf_op jit(solution)/shard_map/finish/pallas_call | solution.py:324
  (29 shorter events, 0.1 us)
Async XLA Ops:
  0.6 15.7 %copy-start.4 = (s32[64,64]{1,0:T(8,128)S(1)}, s32[64,64]{1,0:T(8,128)}, u32[]{:S(2)}) copy-start(s32[64,64]{1,0:T(8,128)} %include_ref) | copy-start | bytes 49156
  0.6 10.9 %collective-permute-start = (s32[32,512]{1,0:T(8,128)}, s32[32,512]{1,0:T(8,128)S(1)}, u32[]{:S(2)}, u32[]{:S(2)}) collective-permute-start(s32[32,512]{1,0:T(8,128)} %param.7), channel_id=1, source_target_pairs={{0,0},{1,1},{2,8},{3,9},{4,16},{5,17},{6,24},{7,25},{8,10},{9,11},... | collective-permute-start | bytes 196616 | tf_op jit(solution)/shard_map/ppermute | solution.py:360
  7.0 11.6 %copy-start.5 = (s32[9]{0:T(128)S(1)}, s32[9]{0:T(128)}, u32[]{:S(2)}) copy-start(s32[9]{0:T(128)} %pad_add_fusion.1.first_ref) | copy-start | bytes 112
  11.5 26.5 %copy-start.1 = (bf16[2,16,32,256]{3,2,1,0:T(8,128)(2,1)S(1)}, bf16[2,16,32,256]{3,2,1,0:T(8,128)(2,1)}, u32[]{:S(2)}) copy-start(bf16[2,16,32,256]{3,2,1,0:T(8,128)(2,1)} %get-tuple-element.58.refs_0_) | copy-start | bytes 1572868
  11.5 16.4 %collective-permute-start.1 = (bf16[2,16,32,256]{3,2,1,0:T(8,128)(2,1)}, bf16[2,16,32,256]{3,2,1,0:T(8,128)(2,1)S(1)}, u32[]{:S(2)}, u32[]{:S(2)}) collective-permute-start(bf16[2,16,32,256]{3,2,1,0:T(8,128)(2,1)} %get-tuple-element.42), channel_id=1, source_target_pairs={{0,8},{8,0},{16,24},{24,16},{1,9},{9,1},{17,25},{25,17},{2,10},{10... | collective-permute-start | bytes 1572872 | tf_op jit(solution)/shard_map/ppermute | solution.py:369
  11.6 26.4 %collective-permute-start.2 = (bf16[2,16,32,256]{3,2,1,0:T(8,128)(2,1)}, bf16[2,16,32,256]{3,2,1,0:T(8,128)(2,1)S(1)}, u32[]{:S(2)}, u32[]{:S(2)}) collective-permute-start(bf16[2,16,32,256]{3,2,1,0:T(8,128)(2,1)} %get-tuple-element.43), channel_id=1, source_target_pairs={{0,16},{8,24},{16,0},{24,8},{1,17},{9,25},{17,1},{25,9},{2,18},{10... | collective-permute-start | bytes 1572872 | tf_op jit(solution)/shard_map/ppermute | solution.py:369
  11.7 26.3 %collective-permute-start.3 = (bf16[2,16,32,256]{3,2,1,0:T(8,128)(2,1)}, bf16[2,16,32,256]{3,2,1,0:T(8,128)(2,1)S(1)}, u32[]{:S(2)}, u32[]{:S(2)}) collective-permute-start(bf16[2,16,32,256]{3,2,1,0:T(8,128)(2,1)} %get-tuple-element.44), channel_id=1, source_target_pairs={{0,24},{8,16},{16,8},{24,0},{1,25},{9,17},{17,9},{25,1},{2,26},{10... | collective-permute-start | bytes 1572872 | tf_op jit(solution)/shard_map/ppermute | solution.py:369
  15.1 2.4 %collective-permute-start.4 = (s32[32,256]{1,0:T(8,128)S(1)}, s32[32,256]{1,0:T(8,128)S(1)}, u32[]{:S(2)}, u32[]{:S(2)}) collective-permute-start(s32[32,256]{1,0:T(8,128)S(1)} %get-tuple-element.66), channel_id=1, source_target_pairs={{0,1},{1,0},{2,3},{3,2},{4,5},{5,4},{6,7},{7,6},{8,9},{9,8},{10,11... | collective-permute-start | bytes 98312 | tf_op jit(solution)/shard_map/ppermute | solution.py:360
  15.1 3.5 %collective-permute-start.5 = (f32[256,128]{1,0:T(8,128)}, f32[256,128]{1,0:T(8,128)S(1)}, u32[]{:S(2)}, u32[]{:S(2)}) collective-permute-start(f32[256,128]{1,0:T(8,128)} %get-tuple-element.34), channel_id=1, source_target_pairs={{1,0},{2,1},{3,2},{4,3},{5,4},{6,5},{7,6},{9,8},{10,9},{11,10},{12... | collective-permute-start | bytes 393224 | tf_op jit(solution)/shard_map/ppermute | solution.py:387
  18.5 2.2 %copy-start = (f32[16,256,256]{2,1,0:T(8,128)S(1)}, f32[16,256,256]{2,1,0:T(8,128)}, u32[]{:S(2)}) copy-start(f32[16,256,256]{2,1,0:T(8,128)} %potentials_ref.3) | copy-start | bytes 12582916
  27.2 17.7 %collective-permute-start.6 = (bf16[1,16,32,256]{3,2,1,0:T(8,128)(2,1)S(1)}, bf16[1,16,32,256]{3,2,1,0:T(8,128)(2,1)S(1)}, u32[]{:S(2)}, u32[]{:S(2)}) collective-permute-start(bf16[1,16,32,256]{3,2,1,0:T(8,128)(2,1)S(1)} %get-tuple-element.57), channel_id=1, source_target_pairs={{0,8},{8,0},{16,24},{24,16},{1,9},{9,1},{17,25},{25,17},{2,10},{10... | collective-permute-start | bytes 786440 | tf_op jit(solution)/shard_map/ppermute | solution.py:369
  27.4 23.6 %collective-permute-start.7 = (bf16[1,16,32,256]{3,2,1,0:T(8,128)(2,1)S(1)}, bf16[1,16,32,256]{3,2,1,0:T(8,128)(2,1)S(1)}, u32[]{:S(2)}, u32[]{:S(2)}) collective-permute-start(bf16[1,16,32,256]{3,2,1,0:T(8,128)(2,1)S(1)} %get-tuple-element.60), channel_id=1, source_target_pairs={{0,16},{8,24},{16,0},{24,8},{1,17},{9,25},{17,1},{25,9},{2,18},{10... | collective-permute-start | bytes 786440 | tf_op jit(solution)/shard_map/ppermute | solution.py:369
  27.9 23.1 %collective-permute-start.8 = (bf16[1,16,32,256]{3,2,1,0:T(8,128)(2,1)S(1)}, bf16[1,16,32,256]{3,2,1,0:T(8,128)(2,1)S(1)}, u32[]{:S(2)}, u32[]{:S(2)}) collective-permute-start(bf16[1,16,32,256]{3,2,1,0:T(8,128)(2,1)S(1)} %get-tuple-element.61), channel_id=1, source_target_pairs={{0,24},{8,16},{16,8},{24,0},{1,25},{9,17},{17,9},{25,1},{2,26},{10... | collective-permute-start | bytes 786440 | tf_op jit(solution)/shard_map/ppermute | solution.py:369
  42.5 17.5 %collective-permute-start.10 = (bf16[1,16,32,256]{3,2,1,0:T(8,128)(2,1)S(1)}, bf16[1,16,32,256]{3,2,1,0:T(8,128)(2,1)S(1)}, u32[]{:S(2)}, u32[]{:S(2)}) collective-permute-start(bf16[1,16,32,256]{3,2,1,0:T(8,128)(2,1)S(1)} %get-tuple-element.63), channel_id=1, source_target_pairs={{0,8},{8,0},{16,24},{24,16},{1,9},{9,1},{17,25},{25,17},{2,10},{10... | collective-permute-start | bytes 786440 | tf_op jit(solution)/shard_map/ppermute | solution.py:369
  44.9 15.1 %collective-permute-start.11 = (bf16[1,16,32,256]{3,2,1,0:T(8,128)(2,1)S(1)}, bf16[1,16,32,256]{3,2,1,0:T(8,128)(2,1)S(1)}, u32[]{:S(2)}, u32[]{:S(2)}) collective-permute-start(bf16[1,16,32,256]{3,2,1,0:T(8,128)(2,1)S(1)} %get-tuple-element.64), channel_id=1, source_target_pairs={{0,16},{8,24},{16,0},{24,8},{1,17},{9,25},{17,1},{25,9},{2,18},{10... | collective-permute-start | bytes 786440 | tf_op jit(solution)/shard_map/ppermute | solution.py:369
  44.9 15.1 %collective-permute-start.12 = (bf16[1,16,32,256]{3,2,1,0:T(8,128)(2,1)S(1)}, bf16[1,16,32,256]{3,2,1,0:T(8,128)(2,1)S(1)}, u32[]{:S(2)}, u32[]{:S(2)}) collective-permute-start(bf16[1,16,32,256]{3,2,1,0:T(8,128)(2,1)S(1)} %get-tuple-element.65), channel_id=1, source_target_pairs={{0,24},{8,16},{16,8},{24,0},{1,25},{9,17},{17,9},{25,1},{2,26},{10... | collective-permute-start | bytes 786440 | tf_op jit(solution)/shard_map/ppermute | solution.py:369
  51.0 19.1 %copy-start.2 = (f32[32,512]{1,0:T(8,128)S(1)}, f32[32,512]{1,0:T(8,128)}, u32[]{:S(2)}) copy-start(f32[32,512]{1,0:T(8,128)} %refs_2_.1) | copy-start | bytes 196612
  51.0 19.1 %copy-start.3 = (f32[32,512]{1,0:T(8,128)S(1)}, f32[32,512]{1,0:T(8,128)}, u32[]{:S(2)}) copy-start(f32[32,512]{1,0:T(8,128)} %refs_3_.1) | copy-start | bytes 196612
  55.6 9.0 %collective-permute-start.9 = (f32[64,256]{1,0:T(8,128)S(1)}, f32[64,256]{1,0:T(8,128)S(1)}, u32[]{:S(2)}, u32[]{:S(2)}) collective-permute-start(f32[64,256]{1,0:T(8,128)S(1)} %pad_maximum_fusion), channel_id=1, source_target_pairs={{0,0},{1,1},{2,10},{3,11},{4,20},{5,21},{6,30},{7,31},{8,2},{9,3},... | collective-permute-start | bytes 196616 | tf_op jit(solution)/shard_map/ppermute | solution.py:360
  64.6 5.5 %collective-permute-start.13 = (f32[64,256]{1,0:T(8,128)S(1)}, f32[64,256]{1,0:T(8,128)S(1)}, u32[]{:S(2)}, u32[]{:S(2)}) collective-permute-start(f32[64,256]{1,0:T(8,128)S(1)} %pad_maximum_fusion.1), channel_id=1, source_target_pairs={{0,1},{1,0},{2,11},{3,10},{4,21},{5,20},{6,31},{7,30},{8,3},{9,2},... | collective-permute-start | bytes 196616 | tf_op jit(solution)/shard_map/ppermute | solution.py:360

commit v6 on v5

--- a/solution.py
+++ b/solution.py
@@ -247,8 +247,10 @@
         yield from range(number * step, (number + 1) * step)
 
 
-def down_kernel(first_ref, potentials_ref, *refs):
+def down_kernel(potentials_ref, *refs):
     *outs, edge_ref, held, sems = refs
+    parts = len(outs)
+    core, strip = lax.axis_index("cores"), lax.axis_index("strip")
     _, height, width = held.shape
     turns, _, rows, _ = outs[0].shape
     row = lax.broadcasted_iota(jnp.int32, (rows, width), 0)
@@ -256,7 +258,9 @@
     for i in load_fields(potentials_ref, held, sems):
         for k, out in enumerate(outs):
             for t in range(turns):
-                first = pl.multiple_of(first_ref[k * turns + t] * rows, rows)
+                region = towards(towards(core, k, parts), lax.div(strip, turns), parts)
+                band = region * turns + towards(lax.rem(strip, turns), t, turns)
+                first = pl.multiple_of(band * rows, rows)
                 following = pl.multiple_of(jnp.minimum(first + rows, height - 8), 8)
                 at_end = first + rows == height
                 here = held[i, pl.ds(first, rows), :]
@@ -381,11 +385,12 @@
     block = jax.ShapeDtypeStruct((turns, each, rows, width), jnp.bfloat16)
     column = jax.ShapeDtypeStruct((height, LANES), jnp.float32)
     *down, edge = on_tile(
-        down_kernel, "down", [block] * parts + [column], [first], fields=potentials
+        down_kernel, "down", [block] * parts + [column], [], fields=potentials
     )
     far = list(range(parts - 1, 0, -1))
+    labels = move(labels, lambda c, g, j: (source(g, c, parts), c, j))
+    edge = after(edge, labels)
     beside = lax.ppermute(edge, "strip", [(i, i - 1) for i in range(1, strips)])
-    labels = move(labels, lambda c, g, j: (source(g, c, parts), c, j))
     down = after(tuple(down), labels)
     down = [down[0], *[exchange(down[k], k) for k in far][::-1]]
     groups, linear = prepare(after(pair_include, edge))

time: 72.5 us -> 72.1 us (level); the launches traced: 71.3 us -> 71.7 us
  starting transfers between devices: 22.3 us -> 23.6 us
    ppermute x4, starting transfers between devices: 9.93 us -> 11.5 us  [move(): return lax.ppermute(array, ('cores', 'strip'), moves)]
    pallas_call x3, Pallas kernels: 11 us -> 10.2 us  [on_tile(): pl.pallas_call(body, in_specs=[SMEM] * len(scalars) + specs, out_specs=ja...]
    unnamed x12 -> x10, local copies, waits for them, and re-layouts: 2.21 us -> 2.21 us
  transfers between devices with their start and end apart: 14 -> 14, of which waited for: 3 -> 4; matrix products, arithmetic and copies ran while one was open for 2% -> 1% of each run, Pallas kernels for 42% -> 41%
where the time goes in v6:
time: 72.1 us; the launch traced here: 71.7 us
  Pallas kernels  30.6 us (42%)
  starting transfers between devices  23.6 us (33%)
  waiting for transfers between devices  13.7 us (19%)
  local copies, waits for them, and re-layouts  2.64 us (4%)
  between operations  0.91 us (1%)
    pallas_call x4, Pallas kernels, pairs(): pl.pallas_call(functools.partial(pairs_kernel, scale=2.0 / (fields * (fie...  18.4 us
    ppermute x4, starting transfers between devices, move(): return lax.ppermute(array, ('cores', 'strip'), moves)  11.5 us
    ppermute x9, starting transfers between devices, exchange(): return lax.ppermute(block, 'cores', moves)  10.8 us
    pallas_call x3, Pallas kernels, on_tile(): pl.pallas_call(body, in_specs=[SMEM] * len(scalars) + specs, out_specs=ja...  10.2 us
    ppermute x9, waiting for transfers between devices, exchange(): return lax.ppermute(block, 'cores', moves)  6.61 us
    ppermute x4, waiting for transfers between devices, move(): return lax.ppermute(array, ('cores', 'strip'), moves)  6.17 us
    unnamed x10, local copies, waits for them, and re-layouts  2.21 us
  transfers between devices with their start and end apart: 14, of which 4 were waited for; matrix products, arithmetic and copies ran while one was open for 1% of the time, Pallas kernels for 41%

profile of v6, /device:TPU:6, one launch (start us, length us, event | category | flops | bytes accessed | tf_op | source)
XLA Modules:
  0.0 71.7 jit_solution(2278563731357889893)
XLA Ops:
  0.6 5.5 %collective-permute-start = (s32[32,512]{1,0:T(8,128)}, s32[32,512]{1,0:T(8,128)S(1)}, u32[]{:S(2)}, u32[]{:S(2)}) collective-permute-start(s32[32,512]{1,0:T(8,128)} %param.7), channel_id=1, source_target_pairs={{0,0},{1,1},{2,8},{3,9},{4,16},{5,17},{6,24},{7,25},{8,10},{9,11},... | collective-permute-start | bytes 196616 | tf_op jit(solution)/shard_map/ppermute | solution.py:364
  6.2 3.7 %down.1 = (bf16[2,16,32,256]{3,2,1,0:T(8,128)(2,1)}, bf16[2,16,32,256]{3,2,1,0:T(8,128)(2,1)}, bf16[2,16,32,256]{3,2,1,0:T(8,128)(2,1)}, bf16[2,16,32,256]{3,2,1,0:T(8,128)(2,1)}, f32[256,128]{1,0:T(8,128)}) custom-call(f32[16,256,256]{2,1,0:T(8,128)} %potentials_ref.3), custom_call_target="tpu_custom_call" | custom-call | flops 8388608 | bytes 12582912 | tf_op jit(solution)/shard_map/down/pallas_call | solution.py:299
  9.9 0.7 collective-permute-done
  10.6 0.1 broadcast_add_fusion
  10.7 0.1 add.34
  10.8 3.5 %collective-permute-start.3 = (bf16[2,16,32,256]{3,2,1,0:T(8,128)(2,1)}, bf16[2,16,32,256]{3,2,1,0:T(8,128)(2,1)S(1)}, u32[]{:S(2)}, u32[]{:S(2)}) collective-permute-start(bf16[2,16,32,256]{3,2,1,0:T(8,128)(2,1)} %get-tuple-element.46), channel_id=1, source_target_pairs={{0,24},{8,16},{16,8},{24,0},{1,25},{9,17},{17,9},{25,1},{2,26},{10... | collective-permute-start | bytes 1572872 | tf_op jit(solution)/shard_map/ppermute | solution.py:373
  14.3 1.3 %collective-permute-start.5 = (f32[256,128]{1,0:T(8,128)}, f32[256,128]{1,0:T(8,128)S(1)}, u32[]{:S(2)}, u32[]{:S(2)}) collective-permute-start(f32[256,128]{1,0:T(8,128)} %get-tuple-element.36), channel_id=1, source_target_pairs={{1,0},{2,1},{3,2},{4,3},{5,4},{6,5},{7,6},{9,8},{10,9},{11,10},{12... | collective-permute-start | bytes 393224 | tf_op jit(solution)/shard_map/ppermute | solution.py:393
  15.6 0.1 pad_add_fusion.1.first_ref
  15.7 0.7 %prepare.1 = (s32[8,640]{1,0:T(8,128)S(1)}, f32[64,128]{1,0:T(8,128)S(1)}) custom-call(s32[64,64]{1,0:T(8,128)S(1)} %copy-done.4), custom_call_target="tpu_custom_call" | custom-call | tf_op jit(solution)/shard_map/prepare/pallas_call | solution.py:85
  16.4 0.2 copy.7
  16.6 0.2 reshape.22.groups_ref
  16.8 1.0 %collective-permute-done.5.beside_ref = f32[256,128]{1,0:T(8,128)S(1)} collective-permute-done((f32[256,128]{1,0:T(8,128)}, f32[256,128]{1,0:T(8,128)S(1)}, u32[]{:S(2)}, u32[]{:S(2)}) %collective-permute-start.5) | collective-permute-done | bytes 131104 | tf_op jit(solution)/shard_map/ppermute | solution.py:393
  17.8 2.2 %copy-done = f32[16,256,256]{2,1,0:T(8,128)S(1)} copy-done((f32[16,256,256]{2,1,0:T(8,128)S(1)}, f32[16,256,256]{2,1,0:T(8,128)}, u32[]{:S(2)}) %copy-start) | copy-done | bytes 4194328
  19.9 2.6 %side.1 = (bf16[1,16,32,256]{3,2,1,0:T(8,128)(2,1)S(1)}, bf16[1,16,32,256]{3,2,1,0:T(8,128)(2,1)S(1)}, bf16[1,16,32,256]{3,2,1,0:T(8,128)(2,1)S(1)}, bf16[1,16,3...) custom-call(s32[9]{0:T(128)S(1)} %pad_add_fusion.1.first_ref, ...), custom_call_target="tpu_custom_call" | custom-call | flops 4325376 | bytes 6488064 | tf_op jit(solution)/shard_map/side/pallas_call | solution.py:299
  22.5 3.9 %factors.1.refs_5_ = bf16[2,64,32,256]{3,2,1,0:T(8,128)(2,1)S(1)} custom-call(s32[64,256]{1,0:T(8,128)S(1)} %pad_add_fusion.labels_ref, f32[64,128]{1,0:T(8,128)S(1)} %get-tuple-element.58.linear_ref), custom_call_target="tpu_custom_call" | custom-call | flops 98304 | bytes 147456 | tf_op jit(solution)/shard_map/factors/pallas_call | solution.py:299
  26.4 0.1 collective-permute-start.6
  26.5 0.6 collective-permute-start.7
  27.1 0.0 collective-permute-done.1.refs_1_
  27.2 2.8 %collective-permute-start.8 = (bf16[1,16,32,256]{3,2,1,0:T(8,128)(2,1)S(1)}, bf16[1,16,32,256]{3,2,1,0:T(8,128)(2,1)S(1)}, u32[]{:S(2)}, u32[]{:S(2)}) collective-permute-start(bf16[1,16,32,256]{3,2,1,0:T(8,128)(2,1)S(1)} %get-tuple-element.63), channel_id=1, source_target_pairs={{0,24},{8,16},{16,8},{24,0},{1,25},{9,17},{17,9},{25,1},{2,26},{10... | collective-permute-start | bytes 786440 | tf_op jit(solution)/shard_map/ppermute | solution.py:373
  30.0 6.6 %collective-permute-done.2.refs_2_ = bf16[2,16,32,256]{3,2,1,0:T(8,128)(2,1)S(1)} collective-permute-done((bf16[2,16,32,256]{3,2,1,0:T(8,128)(2,1)}, bf16[2,16,32,256]{3,2,1,0:T(8,128)(2,1)S(1)}, u32[]{:S(2)}, u32[]{:S(2)}) %collective-permute-start.2) | collective-permute-done | bytes 524320 | tf_op jit(solution)/shard_map/ppermute | solution.py:373
  36.6 4.6 %pairs.4 = f32[32,256]{1,0:T(8,128)S(1)} custom-call(s32[4]{0:T(128)S(1)} %fusion.base_ref, s32[5120]{0:T(1024)S(1)} %reshape.22.groups_ref, bf16[2,16,32,256]{3,2,1,0:T(8,128)(2,1)S(1)} %copy-done.1, bf16[2,16,32,256]{3,2,1,0:T(8,128)(2,1)S(1)} %collective-permute-done.1.refs_1_, bf16[2,16,32,256]{3,2,1,0:T(8,128)(2,1)S(1)} %collective-permute-done.2.refs_2_, ...), custom_call_target="tpu_custom_call" | custom-call | flops 33554432 | bytes 2097152 | tf_op jit(solution)/shard_map/pairs/pallas_call | solution.py:214
  41.2 2.3 %collective-permute-start.10 = (bf16[1,16,32,256]{3,2,1,0:T(8,128)(2,1)S(1)}, bf16[1,16,32,256]{3,2,1,0:T(8,128)(2,1)S(1)}, u32[]{:S(2)}, u32[]{:S(2)}) collective-permute-start(bf16[1,16,32,256]{3,2,1,0:T(8,128)(2,1)S(1)} %get-tuple-element.65), channel_id=1, source_target_pairs={{0,8},{8,0},{16,24},{24,16},{1,9},{9,1},{17,25},{25,17},{2,10},{10... | collective-permute-start | bytes 786440 | tf_op jit(solution)/shard_map/ppermute | solution.py:373
  43.5 1.5 %collective-permute-start.12 = (bf16[1,16,32,256]{3,2,1,0:T(8,128)(2,1)S(1)}, bf16[1,16,32,256]{3,2,1,0:T(8,128)(2,1)S(1)}, u32[]{:S(2)}, u32[]{:S(2)}) collective-permute-start(bf16[1,16,32,256]{3,2,1,0:T(8,128)(2,1)S(1)} %get-tuple-element.67), channel_id=1, source_target_pairs={{0,24},{8,16},{16,8},{24,0},{1,25},{9,17},{17,9},{25,1},{2,26},{10... | collective-permute-start | bytes 786440 | tf_op jit(solution)/shard_map/ppermute | solution.py:373
  45.0 4.6 %pairs.5 = f32[32,256]{1,0:T(8,128)S(1)} custom-call(s32[4]{0:T(128)S(1)} %fusion.base_ref, s32[5120]{0:T(1024)S(1)} %reshape.22.groups_ref, bf16[2,16,32,256]{3,2,1,0:T(8,128)(2,1)S(1)} %copy-done.1, bf16[2,16,32,256]{3,2,1,0:T(8,128)(2,1)S(1)} %collective-permute-done.1.refs_1_, bf16[2,16,32,256]{3,2,1,0:T(8,128)(2,1)S(1)} %collective-permute-done.2.refs_2_, ...), custom_call_target="tpu_custom_call" | custom-call | flops 33554432 | bytes 2097152 | tf_op jit(solution)/shard_map/pairs/pallas_call | solution.py:214
  49.6 0.0 copy-start.2
  49.6 0.0 copy-start.3
  49.6 4.6 %pairs.6 = f32[32,256]{1,0:T(8,128)S(1)} custom-call(s32[4]{0:T(128)S(1)} %fusion.base_ref, s32[5120]{0:T(1024)S(1)} %reshape.22.groups_ref, bf16[1,16,32,256]{3,2,1,0:T(8,128)(2,1)S(1)} %get-tuple-element.61.refs_0_, bf16[1,16,32,256]{3,2,1,0:T(8,128)(2,1)S(1)} %collective-permute-done.6.refs_1_, ...), custom_call_target="tpu_custom_call" | custom-call | flops 33554432 | bytes 2097152 | tf_op jit(solution)/shard_map/pairs/pallas_call | solution.py:214
  54.3 6.0 %collective-permute-start.9 = (f32[64,256]{1,0:T(8,128)S(1)}, f32[64,256]{1,0:T(8,128)S(1)}, u32[]{:S(2)}, u32[]{:S(2)}) collective-permute-start(f32[64,256]{1,0:T(8,128)S(1)} %pad_maximum_fusion), channel_id=1, source_target_pairs={{0,0},{1,1},{2,10},{3,11},{4,20},{5,21},{6,30},{7,31},{8,2},{9,3},... | collective-permute-start | bytes 196616 | tf_op jit(solution)/shard_map/ppermute | solution.py:364
  60.3 4.6 %pairs.7 = f32[32,256]{1,0:T(8,128)S(1)} custom-call(s32[4]{0:T(128)S(1)} %fusion.base_ref, s32[5120]{0:T(1024)S(1)} %reshape.22.groups_ref, bf16[1,16,32,256]{3,2,1,0:T(8,128)(2,1)S(1)} %get-tuple-element.64.refs_0_, bf16[1,16,32,256]{3,2,1,0:T(8,128)(2,1)S(1)} %collective-permute-done.10.refs_1_, ...), custom_call_target="tpu_custom_call" | custom-call | flops 33554432 | bytes 2097152 | tf_op jit(solution)/shard_map/pairs/pallas_call | solution.py:214
  64.9 0.1 collective-permute-start.13
  65.0 5.5 %collective-permute-done.13.refs_1_ = f32[64,256]{1,0:T(8,128)S(1)} collective-permute-done((f32[64,256]{1,0:T(8,128)S(1)}, f32[64,256]{1,0:T(8,128)S(1)}, u32[]{:S(2)}, u32[]{:S(2)}) %collective-permute-start.13) | collective-permute-done | bytes 65568 | tf_op jit(solution)/shard_map/ppermute | solution.py:364
  70.5 1.2 %finish.1 = (f32[32,512]{1,0:T(8,128)}, f32[32,512]{1,0:T(8,128)}) custom-call(s32[2]{0:T(128)S(1)} %iota_xor_fusion.1.halves_ref, f32[64,256]{1,0:T(8,128)S(1)} %collective-permute-done.9.refs_0_, f32[64,256]{1,0:T(8,128)S(1)} %collective-permute-done.13.refs_1_, f32[32,512]{1,0:T(8,128)S(1)} %copy-done.2, f32[32,512]{1,0:T(8,128)S(1)} %copy-done.3), custom_call_target="tpu_custom_call" | custom-call | tf_op jit(solution)/shard_map/finish/pallas_call | solution.py:328
  (27 shorter events, 0.1 us)
Async XLA Ops:
  0.6 15.0 %copy-start.4 = (s32[64,64]{1,0:T(8,128)S(1)}, s32[64,64]{1,0:T(8,128)}, u32[]{:S(2)}) copy-start(s32[64,64]{1,0:T(8,128)} %include_ref) | copy-start | bytes 49156
  0.6 10.0 %collective-permute-start = (s32[32,512]{1,0:T(8,128)}, s32[32,512]{1,0:T(8,128)S(1)}, u32[]{:S(2)}, u32[]{:S(2)}) collective-permute-start(s32[32,512]{1,0:T(8,128)} %param.7), channel_id=1, source_target_pairs={{0,0},{1,1},{2,8},{3,9},{4,16},{5,17},{6,24},{7,25},{8,10},{9,11},... | collective-permute-start | bytes 196616 | tf_op jit(solution)/shard_map/ppermute | solution.py:364
  9.9 26.7 %copy-start.1 = (bf16[2,16,32,256]{3,2,1,0:T(8,128)(2,1)S(1)}, bf16[2,16,32,256]{3,2,1,0:T(8,128)(2,1)}, u32[]{:S(2)}) copy-start(bf16[2,16,32,256]{3,2,1,0:T(8,128)(2,1)} %get-tuple-element.60.refs_0_) | copy-start | bytes 1572868
  10.6 16.5 %collective-permute-start.1 = (bf16[2,16,32,256]{3,2,1,0:T(8,128)(2,1)}, bf16[2,16,32,256]{3,2,1,0:T(8,128)(2,1)S(1)}, u32[]{:S(2)}, u32[]{:S(2)}) collective-permute-start(bf16[2,16,32,256]{3,2,1,0:T(8,128)(2,1)} %get-tuple-element.44), channel_id=1, source_target_pairs={{0,8},{8,0},{16,24},{24,16},{1,9},{9,1},{17,25},{25,17},{2,10},{10... | collective-permute-start | bytes 1572872 | tf_op jit(solution)/shard_map/ppermute | solution.py:373
  10.8 25.8 %collective-permute-start.2 = (bf16[2,16,32,256]{3,2,1,0:T(8,128)(2,1)}, bf16[2,16,32,256]{3,2,1,0:T(8,128)(2,1)S(1)}, u32[]{:S(2)}, u32[]{:S(2)}) collective-permute-start(bf16[2,16,32,256]{3,2,1,0:T(8,128)(2,1)} %get-tuple-element.45), channel_id=1, source_target_pairs={{0,16},{8,24},{16,0},{24,8},{1,17},{9,25},{17,1},{25,9},{2,18},{10... | collective-permute-start | bytes 1572872 | tf_op jit(solution)/shard_map/ppermute | solution.py:373
  10.8 25.8 %collective-permute-start.3 = (bf16[2,16,32,256]{3,2,1,0:T(8,128)(2,1)}, bf16[2,16,32,256]{3,2,1,0:T(8,128)(2,1)S(1)}, u32[]{:S(2)}, u32[]{:S(2)}) collective-permute-start(bf16[2,16,32,256]{3,2,1,0:T(8,128)(2,1)} %get-tuple-element.46), channel_id=1, source_target_pairs={{0,24},{8,16},{16,8},{24,0},{1,25},{9,17},{17,9},{25,1},{2,26},{10... | collective-permute-start | bytes 1572872 | tf_op jit(solution)/shard_map/ppermute | solution.py:373
  14.3 2.5 %collective-permute-start.4 = (s32[32,256]{1,0:T(8,128)S(1)}, s32[32,256]{1,0:T(8,128)S(1)}, u32[]{:S(2)}, u32[]{:S(2)}) collective-permute-start(s32[32,256]{1,0:T(8,128)S(1)} %get-tuple-element.68), channel_id=1, source_target_pairs={{0,1},{1,0},{2,3},{3,2},{4,5},{5,4},{6,7},{7,6},{8,9},{9,8},{10,11... | collective-permute-start | bytes 98312 | tf_op jit(solution)/shard_map/ppermute | solution.py:364
  14.3 3.5 %collective-permute-start.5 = (f32[256,128]{1,0:T(8,128)}, f32[256,128]{1,0:T(8,128)S(1)}, u32[]{:S(2)}, u32[]{:S(2)}) collective-permute-start(f32[256,128]{1,0:T(8,128)} %get-tuple-element.36), channel_id=1, source_target_pairs={{1,0},{2,1},{3,2},{4,3},{5,4},{6,5},{7,6},{9,8},{10,9},{11,10},{12... | collective-permute-start | bytes 393224 | tf_op jit(solution)/shard_map/ppermute | solution.py:393
  17.7 2.2 %copy-start = (f32[16,256,256]{2,1,0:T(8,128)S(1)}, f32[16,256,256]{2,1,0:T(8,128)}, u32[]{:S(2)}) copy-start(f32[16,256,256]{2,1,0:T(8,128)} %potentials_ref.3) | copy-start | bytes 12582916
  26.4 17.0 %collective-permute-start.6 = (bf16[1,16,32,256]{3,2,1,0:T(8,128)(2,1)S(1)}, bf16[1,16,32,256]{3,2,1,0:T(8,128)(2,1)S(1)}, u32[]{:S(2)}, u32[]{:S(2)}) collective-permute-start(bf16[1,16,32,256]{3,2,1,0:T(8,128)(2,1)S(1)} %get-tuple-element.59), channel_id=1, source_target_pairs={{0,8},{8,0},{16,24},{24,16},{1,9},{9,1},{17,25},{25,17},{2,10},{10... | collective-permute-start | bytes 786440 | tf_op jit(solution)/shard_map/ppermute | solution.py:373
  26.5 23.1 %collective-permute-start.7 = (bf16[1,16,32,256]{3,2,1,0:T(8,128)(2,1)S(1)}, bf16[1,16,32,256]{3,2,1,0:T(8,128)(2,1)S(1)}, u32[]{:S(2)}, u32[]{:S(2)}) collective-permute-start(bf16[1,16,32,256]{3,2,1,0:T(8,128)(2,1)S(1)} %get-tuple-element.62), channel_id=1, source_target_pairs={{0,16},{8,24},{16,0},{24,8},{1,17},{9,25},{17,1},{25,9},{2,18},{10... | collective-permute-start | bytes 786440 | tf_op jit(solution)/shard_map/ppermute | solution.py:373
  27.2 22.5 %collective-permute-start.8 = (bf16[1,16,32,256]{3,2,1,0:T(8,128)(2,1)S(1)}, bf16[1,16,32,256]{3,2,1,0:T(8,128)(2,1)S(1)}, u32[]{:S(2)}, u32[]{:S(2)}) collective-permute-start(bf16[1,16,32,256]{3,2,1,0:T(8,128)(2,1)S(1)} %get-tuple-element.63), channel_id=1, source_target_pairs={{0,24},{8,16},{16,8},{24,0},{1,25},{9,17},{17,9},{25,1},{2,26},{10... | collective-permute-start | bytes 786440 | tf_op jit(solution)/shard_map/ppermute | solution.py:373
  41.2 19.0 %collective-permute-start.10 = (bf16[1,16,32,256]{3,2,1,0:T(8,128)(2,1)S(1)}, bf16[1,16,32,256]{3,2,1,0:T(8,128)(2,1)S(1)}, u32[]{:S(2)}, u32[]{:S(2)}) collective-permute-start(bf16[1,16,32,256]{3,2,1,0:T(8,128)(2,1)S(1)} %get-tuple-element.65), channel_id=1, source_target_pairs={{0,8},{8,0},{16,24},{24,16},{1,9},{9,1},{17,25},{25,17},{2,10},{10... | collective-permute-start | bytes 786440 | tf_op jit(solution)/shard_map/ppermute | solution.py:373
  43.5 16.8 %collective-permute-start.11 = (bf16[1,16,32,256]{3,2,1,0:T(8,128)(2,1)S(1)}, bf16[1,16,32,256]{3,2,1,0:T(8,128)(2,1)S(1)}, u32[]{:S(2)}, u32[]{:S(2)}) collective-permute-start(bf16[1,16,32,256]{3,2,1,0:T(8,128)(2,1)S(1)} %get-tuple-element.66), channel_id=1, source_target_pairs={{0,16},{8,24},{16,0},{24,8},{1,17},{9,25},{17,1},{25,9},{2,18},{10... | collective-permute-start | bytes 786440 | tf_op jit(solution)/shard_map/ppermute | solution.py:373
  43.5 16.8 %collective-permute-start.12 = (bf16[1,16,32,256]{3,2,1,0:T(8,128)(2,1)S(1)}, bf16[1,16,32,256]{3,2,1,0:T(8,128)(2,1)S(1)}, u32[]{:S(2)}, u32[]{:S(2)}) collective-permute-start(bf16[1,16,32,256]{3,2,1,0:T(8,128)(2,1)S(1)} %get-tuple-element.67), channel_id=1, source_target_pairs={{0,24},{8,16},{16,8},{24,0},{1,25},{9,17},{17,9},{25,1},{2,26},{10... | collective-permute-start | bytes 786440 | tf_op jit(solution)/shard_map/ppermute | solution.py:373
  49.6 20.9 %copy-start.2 = (f32[32,512]{1,0:T(8,128)S(1)}, f32[32,512]{1,0:T(8,128)}, u32[]{:S(2)}) copy-start(f32[32,512]{1,0:T(8,128)} %refs_2_.1) | copy-start | bytes 196612
  49.6 20.8 %copy-start.3 = (f32[32,512]{1,0:T(8,128)S(1)}, f32[32,512]{1,0:T(8,128)}, u32[]{:S(2)}) copy-start(f32[32,512]{1,0:T(8,128)} %refs_3_.1) | copy-start | bytes 196612
  54.3 10.7 %collective-permute-start.9 = (f32[64,256]{1,0:T(8,128)S(1)}, f32[64,256]{1,0:T(8,128)S(1)}, u32[]{:S(2)}, u32[]{:S(2)}) collective-permute-start(f32[64,256]{1,0:T(8,128)S(1)} %pad_maximum_fusion), channel_id=1, source_target_pairs={{0,0},{1,1},{2,10},{3,11},{4,20},{5,21},{6,30},{7,31},{8,2},{9,3},... | collective-permute-start | bytes 196616 | tf_op jit(solution)/shard_map/ppermute | solution.py:364
  64.9 5.5 %collective-permute-start.13 = (f32[64,256]{1,0:T(8,128)S(1)}, f32[64,256]{1,0:T(8,128)S(1)}, u32[]{:S(2)}, u32[]{:S(2)}) collective-permute-start(f32[64,256]{1,0:T(8,128)S(1)} %pad_maximum_fusion.1), channel_id=1, source_target_pairs={{0,1},{1,0},{2,11},{3,10},{4,21},{5,20},{6,31},{7,30},{8,3},{9,2},... | collective-permute-start | bytes 196616 | tf_op jit(solution)/shard_map/ppermute | solution.py:364

commit v7 on v6

--- a/solution.py
+++ b/solution.py
@@ -232,49 +232,68 @@
     )(base, groups, *parts, labels, factors)
 
 
-def load_fields(potentials_ref, held, sems):
-    each = held.shape[0]
-    step = max(each // LOADS, 1)
-    copies = []
-    for number, at in enumerate(range(0, each, step)):
-        span = pl.ds(at, step)
-        copies.append(
-            pltpu.make_async_copy(potentials_ref.at[span], held.at[span], sems.at[number])
-        )
-        copies[-1].start()
-    for number, copy in enumerate(copies):
-        copy.wait()
-        yield from range(number * step, (number + 1) * step)
+def down_of(potentials_ref, place, first, row, base, height):
+    rows = row.shape[0]
+    following = jnp.minimum(first + rows, height - 8)
+    here = potentials_ref[(*place, pl.ds(pl.multiple_of(first - base, 8), rows))]
+    below = potentials_ref[(*place, pl.ds(pl.multiple_of(following - base, 8), 8))]
+    below = jnp.concatenate([here[1:], below[:1]], axis=0)
+    at_end = first + rows == height
+    return jnp.where((row == rows - 1) & at_end, 0.0, below - here).astype(jnp.bfloat16)
+
+
+def edge_kernel(potentials_ref, out_ref):
+    each, rows, _ = potentials_ref.shape
+    lane = lax.broadcasted_iota(jnp.int32, (rows, LANES), 1)
+    edge = jnp.zeros((rows, LANES), jnp.float32)
+    for i in range(each):
+        edge = jnp.where(lane == i, potentials_ref[i, :, 0:1], edge)
+    out_ref[...] = edge
 
 
 def down_kernel(potentials_ref, *refs):
-    *outs, edge_ref, held, sems = refs
-    parts = len(outs)
+    *outs, held, sems = refs
+    parts = len(outs) + 1
     core, strip = lax.axis_index("cores"), lax.axis_index("strip")
-    _, height, width = held.shape
+    _, each, span, width = held.shape
+    height = potentials_ref.shape[1]
     turns, _, rows, _ = outs[0].shape
     row = lax.broadcasted_iota(jnp.int32, (rows, width), 0)
-    lane = lax.broadcasted_iota(jnp.int32, (height, LANES), 1)
-    for i in load_fields(potentials_ref, held, sems):
+    step = max(each // LOADS, 1)
+    regions, bases = [], []
+    for k in range(len(outs)):
+        region = towards(towards(core, k + 1, parts), lax.div(strip, turns), parts)
+        regions.append(region)
+        bases.append(pl.multiple_of(jnp.minimum(region * (turns * rows), height - span), 8))
+
+    def load(number, k):
+        some = pl.ds(number * step, step)
+        return pltpu.make_async_copy(
+            potentials_ref.at[some, pl.ds(bases[k], span)], held.at[k, some], sems.at[number, k]
+        )
+
+    for number in range(each // step):
+        for k in range(len(outs)):
+            load(number, k).start()
+    for number in range(each // step):
         for k, out in enumerate(outs):
+            load(number, k).wait()
             for t in range(turns):
-                region = towards(towards(core, k, parts), lax.div(strip, turns), parts)
-                band = region * turns + towards(lax.rem(strip, turns), t, turns)
-                first = pl.multiple_of(band * rows, rows)
-                following = pl.multiple_of(jnp.minimum(first + rows, height - 8), 8)
-                at_end = first + rows == height
-                here = held[i, pl.ds(first, rows), :]
-                below = held[i, pl.ds(following, 8), :]
-                below = jnp.concatenate([here[1:], below[:1]], axis=0)
-                change = jnp.where((row == rows - 1) & at_end, 0.0, below - here)
-                out[t, i] = change.astype(jnp.bfloat16)
-        edge_ref[...] = jnp.where(lane == i, held[i, :, 0:1], edge_ref[...] if i else 0.0)
-
-
-def side_kernel(first_ref, potentials_ref, beside_ref, *outs, turns):
+                band = regions[k] * turns + towards(lax.rem(strip, turns), t, turns)
+                first = band * rows
+                for i in range(number * step, (number + 1) * step):
+                    out[t, i] = down_of(held, (k, i), first, row, bases[k], height)
+
+
+def side_kernel(first_ref, potentials_ref, beside_ref, own_down, *outs, turns):
     _, each, rows, width = outs[0].shape
     parts = len(outs) // turns
     lane = lax.broadcasted_iota(jnp.int32, (rows, width), 1)
+    row = lax.broadcasted_iota(jnp.int32, (rows, width), 0)
+    for t in range(turns):
+        first = pl.multiple_of(first_ref[t] * rows, rows)
+        for i in range(each):
+            own_down[t, i] = down_of(potentials_ref, (i,), first, row, 0, potentials_ref.shape[1])
     at_end = first_ref[len(outs)] == 1
     for k in range(parts):
         for t in range(turns):
@@ -294,7 +313,12 @@
     scratch = []
     if fields is not None:
         arrays, specs = (fields, *arrays), [HBM, *specs]
-        scratch = [pltpu.VMEM(fields.shape, fields.dtype), pltpu.SemaphoreType.DMA((LOADS,))]
+        turns, each, rows, width = out_shape[0].shape
+        held = (len(out_shape), each, turns * rows + 8, width)
+        scratch = [
+            pltpu.VMEM(held, fields.dtype),
+            pltpu.SemaphoreType.DMA((LOADS, len(out_shape))),
+        ]
         work = 2 * fields.size
     return pl.pallas_call(
         body,
@@ -384,15 +408,13 @@
 
     block = jax.ShapeDtypeStruct((turns, each, rows, width), jnp.bfloat16)
     column = jax.ShapeDtypeStruct((height, LANES), jnp.float32)
-    *down, edge = on_tile(
-        down_kernel, "down", [block] * parts + [column], [], fields=potentials
-    )
+    sent = on_tile(down_kernel, "down", [block] * (parts - 1), [], fields=potentials)
     far = list(range(parts - 1, 0, -1))
     labels = move(labels, lambda c, g, j: (source(g, c, parts), c, j))
-    edge = after(edge, labels)
+    edge = on_tile(edge_kernel, "edge", column, [], after(potentials, *sent, labels))
     beside = lax.ppermute(edge, "strip", [(i, i - 1) for i in range(1, strips)])
-    down = after(tuple(down), labels)
-    down = [down[0], *[exchange(down[k], k) for k in far][::-1]]
+    sent = after(tuple(sent), labels)
+    sent = [exchange(sent[k - 1], k) for k in far][::-1]
     groups, linear = prepare(after(pair_include, edge))
 
     own_labels = []
@@ -403,11 +425,11 @@
         own_labels.append((back, move(part, lambda c, g, j: (c, g, towards(j, t, turns))) if t else part))
     own_labels = [part for _, part in sorted(own_labels, key=lambda pair: pair[0])]
 
-    block = jax.ShapeDtypeStruct((1, each, rows, width), jnp.bfloat16)
-    side = on_tile(
+    one = jax.ShapeDtypeStruct((1, each, rows, width), jnp.bfloat16)
+    own_down, *side = on_tile(
         functools.partial(side_kernel, turns=turns),
         "side",
-        [block] * (parts * turns),
+        [block] + [one] * (parts * turns),
         [after(first, *own_labels, groups)],
         potentials,
         beside,
@@ -424,7 +446,7 @@
     def band_sums(t, got):
         return pairs(base, groups, got, own_labels[t], factors, t, t)
 
-    down[0] = after(down[0], *down[1:])
+    down = [after(own_down, *sent), *sent]
     down_sums = [band_sums(0, down)]
     arrived = []
     for t in range(turns):

time: 72.1 us -> 71 us (0.985)
  the two profiles are of different devices: /device:TPU:6 before, /device:TPU:5 now
where the time goes in v7:
time: 71 us; the launch traced here: 70.7 us
  Pallas kernels  30.2 us (43%)
  starting transfers between devices  22.8 us (32%)
  waiting for transfers between devices  11.8 us (17%)
  local copies, waits for them, and re-layouts  4.82 us (7%)
  between operations  0.86 us (1%)
    pallas_call x4, Pallas kernels, pairs(): pl.pallas_call(functools.partial(pairs_kernel, scale=2.0 / (fields * (fie...  17.8 us
    ppermute x4, starting transfers between devices, move(): return lax.ppermute(array, ('cores', 'strip'), moves)  11.4 us
    pallas_call x4, Pallas kernels, on_tile(): pl.pallas_call(body, in_specs=[SMEM] * len(scalars) + specs, out_specs=ja...  10.4 us
    ppermute x9, starting transfers between devices, exchange(): return lax.ppermute(block, 'cores', moves)  9.49 us
    ppermute x4, waiting for transfers between devices, move(): return lax.ppermute(array, ('cores', 'strip'), moves)  4.92 us
    unnamed x10, local copies, waits for them, and re-layouts  4.39 us
    ppermute x1, waiting for transfers between devices, local(): beside = lax.ppermute(edge, 'strip', [(i, i - 1) for i in range(1, strips)])  3.46 us
    ppermute x9, waiting for transfers between devices, exchange(): return lax.ppermute(block, 'cores', moves)  3.41 us
  transfers between devices with their start and end apart: 14, of which 4 were waited for; matrix products, arithmetic and copies ran while one was open for 1% of the time, Pallas kernels for 41%

profile of v7, /device:TPU:5, one launch (start us, length us, event | category | flops | bytes accessed | tf_op | source)
XLA Modules:
  0.0 70.7 jit_solution(296717923719345646)
XLA Ops:
  0.6 4.2 %collective-permute-start = (s32[32,512]{1,0:T(8,128)}, s32[32,512]{1,0:T(8,128)S(1)}, u32[]{:S(2)}, u32[]{:S(2)}) collective-permute-start(s32[32,512]{1,0:T(8,128)} %param.7), channel_id=1, source_target_pairs={{0,0},{1,1},{2,8},{3,9},{4,16},{5,17},{6,24},{7,25},{8,10},{9,11},... | collective-permute-start | bytes 196616 | tf_op jit(solution)/shard_map/ppermute | solution.py:388
  4.9 3.2 %down.1 = (bf16[2,16,32,256]{3,2,1,0:T(8,128)(2,1)}, bf16[2,16,32,256]{3,2,1,0:T(8,128)(2,1)}, bf16[2,16,32,256]{3,2,1,0:T(8,128)(2,1)}) custom-call(f32[16,256,256]{2,1,0:T(8,128)} %potentials_ref.4), custom_call_target="tpu_custom_call" | custom-call | flops 8388608 | bytes 12582912 | tf_op jit(solution)/shard_map/down/pallas_call | solution.py:323
  8.2 2.5 %collective-permute-start.3 = (bf16[2,16,32,256]{3,2,1,0:T(8,128)(2,1)}, bf16[2,16,32,256]{3,2,1,0:T(8,128)(2,1)S(1)}, u32[]{:S(2)}, u32[]{:S(2)}) collective-permute-start(bf16[2,16,32,256]{3,2,1,0:T(8,128)(2,1)} %get-tuple-element.41), channel_id=1, source_target_pairs={{0,8},{8,0},{16,24},{24,16},{1,9},{9,1},{17,25},{25,17},{2,10},{10... | collective-permute-start | bytes 1572872 | tf_op jit(solution)/shard_map/ppermute | solution.py:397
  10.7 0.1 broadcast_add_fusion
  10.7 0.1 add.32
  10.8 1.2 %collective-permute-start.5 = (bf16[2,16,32,256]{3,2,1,0:T(8,128)(2,1)}, bf16[2,16,32,256]{3,2,1,0:T(8,128)(2,1)S(1)}, u32[]{:S(2)}, u32[]{:S(2)}) collective-permute-start(bf16[2,16,32,256]{3,2,1,0:T(8,128)(2,1)} %get-tuple-element.43), channel_id=1, source_target_pairs={{0,24},{8,16},{16,8},{24,0},{1,25},{9,17},{17,9},{25,1},{2,26},{10... | collective-permute-start | bytes 1572872 | tf_op jit(solution)/shard_map/ppermute | solution.py:397
  12.0 2.5 %collective-permute-start.1 = (s32[32,256]{1,0:T(8,128)S(1)}, s32[32,256]{1,0:T(8,128)S(1)}, u32[]{:S(2)}, u32[]{:S(2)}) collective-permute-start(s32[32,256]{1,0:T(8,128)S(1)} %get-tuple-element.64), channel_id=1, source_target_pairs={{0,1},{1,0},{2,3},{3,2},{4,5},{5,4},{6,7},{7,6},{8,9},{9,8},{10,11... | collective-permute-start | bytes 98312 | tf_op jit(solution)/shard_map/ppermute | solution.py:388
  14.5 2.2 %copy-done = f32[16,256,256]{2,1,0:T(8,128)S(1)} copy-done((f32[16,256,256]{2,1,0:T(8,128)S(1)}, f32[16,256,256]{2,1,0:T(8,128)}, u32[]{:S(2)}) %copy-start) | copy-done | bytes 4194328
  16.7 0.6 edge.1
  17.3 1.9 %collective-permute-start.2 = (f32[256,128]{1,0:T(8,128)S(1)}, f32[256,128]{1,0:T(8,128)S(1)}, u32[]{:S(2)}, u32[]{:S(2)}) collective-permute-start(f32[256,128]{1,0:T(8,128)S(1)} %edge.1), channel_id=1, source_target_pairs={{1,0},{2,1},{3,2},{4,3},{5,4},{6,5},{7,6},{9,8},{10,9},{11,10},{12... | collective-permute-start | bytes 393224 | tf_op jit(solution)/shard_map/ppermute | solution.py:415
  19.2 0.1 pad_add_fusion.1.first_ref
  19.3 0.7 %prepare.1 = (s32[8,640]{1,0:T(8,128)S(1)}, f32[64,128]{1,0:T(8,128)S(1)}) custom-call(s32[64,64]{1,0:T(8,128)S(1)} %copy-done.4), custom_call_target="tpu_custom_call" | custom-call | tf_op jit(solution)/shard_map/prepare/pallas_call | solution.py:85
  20.1 0.2 copy.7
  20.2 0.2 reshape.22.groups_ref
  20.4 3.5 %collective-permute-done.2.beside_ref = f32[256,128]{1,0:T(8,128)S(1)} collective-permute-done((f32[256,128]{1,0:T(8,128)S(1)}, f32[256,128]{1,0:T(8,128)S(1)}, u32[]{:S(2)}, u32[]{:S(2)}) %collective-permute-start.2) | collective-permute-done | bytes 131104 | tf_op jit(solution)/shard_map/ppermute | solution.py:415
  23.9 2.2 %copy-done.1 = f32[16,256,256]{2,1,0:T(8,128)S(1)} copy-done((f32[16,256,256]{2,1,0:T(8,128)S(1)}, f32[16,256,256]{2,1,0:T(8,128)}, u32[]{:S(2)}) %copy-start.1) | copy-done | bytes 4194328
  26.1 2.6 %side.1 = (bf16[2,16,32,256]{3,2,1,0:T(8,128)(2,1)S(1)}, bf16[1,16,32,256]{3,2,1,0:T(8,128)(2,1)S(1)}, bf16[1,16,32,256]{3,2,1,0:T(8,128)(2,1)S(1)}, bf16[1,16,3...) custom-call(s32[9]{0:T(128)S(1)} %pad_add_fusion.1.first_ref, ...), custom_call_target="tpu_custom_call" | custom-call | flops 4325376 | bytes 6488064 | tf_op jit(solution)/shard_map/side/pallas_call | solution.py:323
  28.7 3.9 %factors.1.refs_5_ = bf16[2,64,32,256]{3,2,1,0:T(8,128)(2,1)S(1)} custom-call(s32[64,256]{1,0:T(8,128)S(1)} %pad_add_fusion.labels_ref, f32[64,128]{1,0:T(8,128)S(1)} %get-tuple-element.54.linear_ref), custom_call_target="tpu_custom_call" | custom-call | flops 98304 | bytes 147456 | tf_op jit(solution)/shard_map/factors/pallas_call | solution.py:323
  32.6 1.8 %collective-permute-start.6 = (bf16[1,16,32,256]{3,2,1,0:T(8,128)(2,1)S(1)}, bf16[1,16,32,256]{3,2,1,0:T(8,128)(2,1)S(1)}, u32[]{:S(2)}, u32[]{:S(2)}) collective-permute-start(bf16[1,16,32,256]{3,2,1,0:T(8,128)(2,1)S(1)} %get-tuple-element.55), channel_id=1, source_target_pairs={{0,8},{8,0},{16,24},{24,16},{1,9},{9,1},{17,25},{25,17},{2,10},{10... | collective-permute-start | bytes 786440 | tf_op jit(solution)/shard_map/ppermute | solution.py:397
  34.5 1.3 %collective-permute-start.8 = (bf16[1,16,32,256]{3,2,1,0:T(8,128)(2,1)S(1)}, bf16[1,16,32,256]{3,2,1,0:T(8,128)(2,1)S(1)}, u32[]{:S(2)}, u32[]{:S(2)}) collective-permute-start(bf16[1,16,32,256]{3,2,1,0:T(8,128)(2,1)S(1)} %get-tuple-element.59), channel_id=1, source_target_pairs={{0,24},{8,16},{16,8},{24,0},{1,25},{9,17},{17,9},{25,1},{2,26},{10... | collective-permute-start | bytes 786440 | tf_op jit(solution)/shard_map/ppermute | solution.py:397
  35.7 4.5 %pairs.4 = f32[32,256]{1,0:T(8,128)S(1)} custom-call(s32[4]{0:T(128)S(1)} %fusion.base_ref, s32[5120]{0:T(1024)S(1)} %reshape.22.groups_ref, bf16[2,16,32,256]{3,2,1,0:T(8,128)(2,1)S(1)} %get-tuple-element.56.refs_0_, bf16[2,16,32,256]{3,2,1,0:T(8,128)(2,1)S(1)} %collective-permute-done.3.refs_1_, ...), custom_call_target="tpu_custom_call" | custom-call | flops 33554432 | bytes 2097152 | tf_op jit(solution)/shard_map/pairs/pallas_call | solution.py:214
  40.2 1.5 %collective-permute-start.10 = (bf16[1,16,32,256]{3,2,1,0:T(8,128)(2,1)S(1)}, bf16[1,16,32,256]{3,2,1,0:T(8,128)(2,1)S(1)}, u32[]{:S(2)}, u32[]{:S(2)}) collective-permute-start(bf16[1,16,32,256]{3,2,1,0:T(8,128)(2,1)S(1)} %get-tuple-element.61), channel_id=1, source_target_pairs={{0,8},{8,0},{16,24},{24,16},{1,9},{9,1},{17,25},{25,17},{2,10},{10... | collective-permute-start | bytes 786440 | tf_op jit(solution)/shard_map/ppermute | solution.py:397
  41.6 1.3 %collective-permute-start.12 = (bf16[1,16,32,256]{3,2,1,0:T(8,128)(2,1)S(1)}, bf16[1,16,32,256]{3,2,1,0:T(8,128)(2,1)S(1)}, u32[]{:S(2)}, u32[]{:S(2)}) collective-permute-start(bf16[1,16,32,256]{3,2,1,0:T(8,128)(2,1)S(1)} %get-tuple-element.63), channel_id=1, source_target_pairs={{0,24},{8,16},{16,8},{24,0},{1,25},{9,17},{17,9},{25,1},{2,26},{10... | collective-permute-start | bytes 786440 | tf_op jit(solution)/shard_map/ppermute | solution.py:397
  42.9 4.4 %pairs.5 = f32[32,256]{1,0:T(8,128)S(1)} custom-call(s32[4]{0:T(128)S(1)} %fusion.base_ref, s32[5120]{0:T(1024)S(1)} %reshape.22.groups_ref, bf16[2,16,32,256]{3,2,1,0:T(8,128)(2,1)S(1)} %get-tuple-element.56.refs_0_, bf16[2,16,32,256]{3,2,1,0:T(8,128)(2,1)S(1)} %collective-permute-done.3.refs_1_, ...), custom_call_target="tpu_custom_call" | custom-call | flops 33554432 | bytes 2097152 | tf_op jit(solution)/shard_map/pairs/pallas_call | solution.py:214
  47.4 0.3 collective-permute-done.7.refs_2_
  47.6 4.5 %pairs.6 = f32[32,256]{1,0:T(8,128)S(1)} custom-call(s32[4]{0:T(128)S(1)} %fusion.base_ref, s32[5120]{0:T(1024)S(1)} %reshape.22.groups_ref, bf16[1,16,32,256]{3,2,1,0:T(8,128)(2,1)S(1)} %get-tuple-element.57.refs_0_, bf16[1,16,32,256]{3,2,1,0:T(8,128)(2,1)S(1)} %collective-permute-done.6.refs_1_, ...), custom_call_target="tpu_custom_call" | custom-call | flops 33554432 | bytes 2097152 | tf_op jit(solution)/shard_map/pairs/pallas_call | solution.py:214
  52.1 3.2 %collective-permute-start.9 = (f32[64,256]{1,0:T(8,128)S(1)}, f32[64,256]{1,0:T(8,128)S(1)}, u32[]{:S(2)}, u32[]{:S(2)}) collective-permute-start(f32[64,256]{1,0:T(8,128)S(1)} %pad_maximum_fusion), channel_id=1, source_target_pairs={{0,0},{1,1},{2,10},{3,11},{4,20},{5,21},{6,30},{7,31},{8,2},{9,3},... | collective-permute-start | bytes 196616 | tf_op jit(solution)/shard_map/ppermute | solution.py:388
  55.4 3.1 %collective-permute-done.11.refs_2_ = bf16[1,16,32,256]{3,2,1,0:T(8,128)(2,1)S(1)} collective-permute-done((bf16[1,16,32,256]{3,2,1,0:T(8,128)(2,1)S(1)}, bf16[1,16,32,256]{3,2,1,0:T(8,128)(2,1)S(1)}, u32[]{:S(2)}, u32[]{:S(2)}) %collective-permute-start.11) | collective-permute-done | bytes 262176 | tf_op jit(solution)/shard_map/ppermute | solution.py:397
  58.5 4.5 %pairs.7 = f32[32,256]{1,0:T(8,128)S(1)} custom-call(s32[4]{0:T(128)S(1)} %fusion.base_ref, s32[5120]{0:T(1024)S(1)} %reshape.22.groups_ref, bf16[1,16,32,256]{3,2,1,0:T(8,128)(2,1)S(1)} %get-tuple-element.60.refs_0_, bf16[1,16,32,256]{3,2,1,0:T(8,128)(2,1)S(1)} %collective-permute-done.10.refs_1_, ...), custom_call_target="tpu_custom_call" | custom-call | flops 33554432 | bytes 2097152 | tf_op jit(solution)/shard_map/pairs/pallas_call | solution.py:214
  63.0 1.5 %collective-permute-start.13 = (f32[64,256]{1,0:T(8,128)S(1)}, f32[64,256]{1,0:T(8,128)S(1)}, u32[]{:S(2)}, u32[]{:S(2)}) collective-permute-start(f32[64,256]{1,0:T(8,128)S(1)} %pad_maximum_fusion.1), channel_id=1, source_target_pairs={{0,1},{1,0},{2,11},{3,10},{4,21},{5,20},{6,31},{7,30},{8,3},{9,2},... | collective-permute-start | bytes 196616 | tf_op jit(solution)/shard_map/ppermute | solution.py:388
  64.5 4.9 %collective-permute-done.13.refs_1_ = f32[64,256]{1,0:T(8,128)S(1)} collective-permute-done((f32[64,256]{1,0:T(8,128)S(1)}, f32[64,256]{1,0:T(8,128)S(1)}, u32[]{:S(2)}, u32[]{:S(2)}) %collective-permute-start.13) | collective-permute-done | bytes 65568 | tf_op jit(solution)/shard_map/ppermute | solution.py:388
  69.4 1.2 %finish.1 = (f32[32,512]{1,0:T(8,128)}, f32[32,512]{1,0:T(8,128)}) custom-call(s32[2]{0:T(128)S(1)} %iota_xor_fusion.1.halves_ref, f32[64,256]{1,0:T(8,128)S(1)} %collective-permute-done.9.refs_0_, f32[64,256]{1,0:T(8,128)S(1)} %collective-permute-done.13.refs_1_, f32[32,512]{1,0:T(8,128)S(1)} %copy-done.2, f32[32,512]{1,0:T(8,128)S(1)} %copy-done.3), custom_call_target="tpu_custom_call" | custom-call | tf_op jit(solution)/shard_map/finish/pallas_call | solution.py:352
  (28 shorter events, 0.1 us)
Async XLA Ops:
  0.6 7.5 %collective-permute-start = (s32[32,512]{1,0:T(8,128)}, s32[32,512]{1,0:T(8,128)S(1)}, u32[]{:S(2)}, u32[]{:S(2)}) collective-permute-start(s32[32,512]{1,0:T(8,128)} %param.7), channel_id=1, source_target_pairs={{0,0},{1,1},{2,8},{3,9},{4,16},{5,17},{6,24},{7,25},{8,10},{9,11},... | collective-permute-start | bytes 196616 | tf_op jit(solution)/shard_map/ppermute | solution.py:388
  4.9 14.4 %copy-start.4 = (s32[64,64]{1,0:T(8,128)S(1)}, s32[64,64]{1,0:T(8,128)}, u32[]{:S(2)}) copy-start(s32[64,64]{1,0:T(8,128)} %include_ref) | copy-start | bytes 49156
  8.2 26.3 %collective-permute-start.3 = (bf16[2,16,32,256]{3,2,1,0:T(8,128)(2,1)}, bf16[2,16,32,256]{3,2,1,0:T(8,128)(2,1)S(1)}, u32[]{:S(2)}, u32[]{:S(2)}) collective-permute-start(bf16[2,16,32,256]{3,2,1,0:T(8,128)(2,1)} %get-tuple-element.41), channel_id=1, source_target_pairs={{0,8},{8,0},{16,24},{24,16},{1,9},{9,1},{17,25},{25,17},{2,10},{10... | collective-permute-start | bytes 1572872 | tf_op jit(solution)/shard_map/ppermute | solution.py:397
  10.8 24.9 %collective-permute-start.4 = (bf16[2,16,32,256]{3,2,1,0:T(8,128)(2,1)}, bf16[2,16,32,256]{3,2,1,0:T(8,128)(2,1)S(1)}, u32[]{:S(2)}, u32[]{:S(2)}) collective-permute-start(bf16[2,16,32,256]{3,2,1,0:T(8,128)(2,1)} %get-tuple-element.42), channel_id=1, source_target_pairs={{0,16},{8,24},{16,0},{24,8},{1,17},{9,25},{17,1},{25,9},{2,18},{10... | collective-permute-start | bytes 1572872 | tf_op jit(solution)/shard_map/ppermute | solution.py:397
  10.8 24.9 %collective-permute-start.5 = (bf16[2,16,32,256]{3,2,1,0:T(8,128)(2,1)}, bf16[2,16,32,256]{3,2,1,0:T(8,128)(2,1)S(1)}, u32[]{:S(2)}, u32[]{:S(2)}) collective-permute-start(bf16[2,16,32,256]{3,2,1,0:T(8,128)(2,1)} %get-tuple-element.43), channel_id=1, source_target_pairs={{0,24},{8,16},{16,8},{24,0},{1,25},{9,17},{17,9},{25,1},{2,26},{10... | collective-permute-start | bytes 1572872 | tf_op jit(solution)/shard_map/ppermute | solution.py:397
  12.0 8.4 %collective-permute-start.1 = (s32[32,256]{1,0:T(8,128)S(1)}, s32[32,256]{1,0:T(8,128)S(1)}, u32[]{:S(2)}, u32[]{:S(2)}) collective-permute-start(s32[32,256]{1,0:T(8,128)S(1)} %get-tuple-element.64), channel_id=1, source_target_pairs={{0,1},{1,0},{2,3},{3,2},{4,5},{5,4},{6,7},{7,6},{8,9},{9,8},{10,11... | collective-permute-start | bytes 98312 | tf_op jit(solution)/shard_map/ppermute | solution.py:388
  14.5 2.2 %copy-start = (f32[16,256,256]{2,1,0:T(8,128)S(1)}, f32[16,256,256]{2,1,0:T(8,128)}, u32[]{:S(2)}) copy-start(f32[16,256,256]{2,1,0:T(8,128)} %potentials_ref.4) | copy-start | bytes 12582916
  17.3 6.6 %collective-permute-start.2 = (f32[256,128]{1,0:T(8,128)S(1)}, f32[256,128]{1,0:T(8,128)S(1)}, u32[]{:S(2)}, u32[]{:S(2)}) collective-permute-start(f32[256,128]{1,0:T(8,128)S(1)} %edge.1), channel_id=1, source_target_pairs={{1,0},{2,1},{3,2},{4,3},{5,4},{6,5},{7,6},{9,8},{10,9},{11,10},{12... | collective-permute-start | bytes 393224 | tf_op jit(solution)/shard_map/ppermute | solution.py:415
  23.9 2.2 %copy-start.1 = (f32[16,256,256]{2,1,0:T(8,128)S(1)}, f32[16,256,256]{2,1,0:T(8,128)}, u32[]{:S(2)}) copy-start(f32[16,256,256]{2,1,0:T(8,128)} %potentials_ref.4) | copy-start | bytes 12582916
  32.6 9.0 %collective-permute-start.6 = (bf16[1,16,32,256]{3,2,1,0:T(8,128)(2,1)S(1)}, bf16[1,16,32,256]{3,2,1,0:T(8,128)(2,1)S(1)}, u32[]{:S(2)}, u32[]{:S(2)}) collective-permute-start(bf16[1,16,32,256]{3,2,1,0:T(8,128)(2,1)S(1)} %get-tuple-element.55), channel_id=1, source_target_pairs={{0,8},{8,0},{16,24},{24,16},{1,9},{9,1},{17,25},{25,17},{2,10},{10... | collective-permute-start | bytes 786440 | tf_op jit(solution)/shard_map/ppermute | solution.py:397
  34.4 13.2 %collective-permute-start.7 = (bf16[1,16,32,256]{3,2,1,0:T(8,128)(2,1)S(1)}, bf16[1,16,32,256]{3,2,1,0:T(8,128)(2,1)S(1)}, u32[]{:S(2)}, u32[]{:S(2)}) collective-permute-start(bf16[1,16,32,256]{3,2,1,0:T(8,128)(2,1)S(1)} %get-tuple-element.58), channel_id=1, source_target_pairs={{0,16},{8,24},{16,0},{24,8},{1,17},{9,25},{17,1},{25,9},{2,18},{10... | collective-permute-start | bytes 786440 | tf_op jit(solution)/shard_map/ppermute | solution.py:397
  34.5 13.2 %collective-permute-start.8 = (bf16[1,16,32,256]{3,2,1,0:T(8,128)(2,1)S(1)}, bf16[1,16,32,256]{3,2,1,0:T(8,128)(2,1)S(1)}, u32[]{:S(2)}, u32[]{:S(2)}) collective-permute-start(bf16[1,16,32,256]{3,2,1,0:T(8,128)(2,1)S(1)} %get-tuple-element.59), channel_id=1, source_target_pairs={{0,24},{8,16},{16,8},{24,0},{1,25},{9,17},{17,9},{25,1},{2,26},{10... | collective-permute-start | bytes 786440 | tf_op jit(solution)/shard_map/ppermute | solution.py:397
  40.2 15.2 %collective-permute-start.10 = (bf16[1,16,32,256]{3,2,1,0:T(8,128)(2,1)S(1)}, bf16[1,16,32,256]{3,2,1,0:T(8,128)(2,1)S(1)}, u32[]{:S(2)}, u32[]{:S(2)}) collective-permute-start(bf16[1,16,32,256]{3,2,1,0:T(8,128)(2,1)S(1)} %get-tuple-element.61), channel_id=1, source_target_pairs={{0,8},{8,0},{16,24},{24,16},{1,9},{9,1},{17,25},{25,17},{2,10},{10... | collective-permute-start | bytes 786440 | tf_op jit(solution)/shard_map/ppermute | solution.py:397
  41.6 16.9 %collective-permute-start.11 = (bf16[1,16,32,256]{3,2,1,0:T(8,128)(2,1)S(1)}, bf16[1,16,32,256]{3,2,1,0:T(8,128)(2,1)S(1)}, u32[]{:S(2)}, u32[]{:S(2)}) collective-permute-start(bf16[1,16,32,256]{3,2,1,0:T(8,128)(2,1)S(1)} %get-tuple-element.62), channel_id=1, source_target_pairs={{0,16},{8,24},{16,0},{24,8},{1,17},{9,25},{17,1},{25,9},{2,18},{10... | collective-permute-start | bytes 786440 | tf_op jit(solution)/shard_map/ppermute | solution.py:397
  41.6 16.9 %collective-permute-start.12 = (bf16[1,16,32,256]{3,2,1,0:T(8,128)(2,1)S(1)}, bf16[1,16,32,256]{3,2,1,0:T(8,128)(2,1)S(1)}, u32[]{:S(2)}, u32[]{:S(2)}) collective-permute-start(bf16[1,16,32,256]{3,2,1,0:T(8,128)(2,1)S(1)} %get-tuple-element.63), channel_id=1, source_target_pairs={{0,24},{8,16},{16,8},{24,0},{1,25},{9,17},{17,9},{25,1},{2,26},{10... | collective-permute-start | bytes 786440 | tf_op jit(solution)/shard_map/ppermute | solution.py:397
  47.4 22.1 %copy-start.2 = (f32[32,512]{1,0:T(8,128)S(1)}, f32[32,512]{1,0:T(8,128)}, u32[]{:S(2)}) copy-start(f32[32,512]{1,0:T(8,128)} %refs_2_.1) | copy-start | bytes 196612
  47.4 22.1 %copy-start.3 = (f32[32,512]{1,0:T(8,128)S(1)}, f32[32,512]{1,0:T(8,128)}, u32[]{:S(2)}) copy-start(f32[32,512]{1,0:T(8,128)} %refs_3_.1) | copy-start | bytes 196612
  52.1 12.4 %collective-permute-start.9 = (f32[64,256]{1,0:T(8,128)S(1)}, f32[64,256]{1,0:T(8,128)S(1)}, u32[]{:S(2)}, u32[]{:S(2)}) collective-permute-start(f32[64,256]{1,0:T(8,128)S(1)} %pad_maximum_fusion), channel_id=1, source_target_pairs={{0,0},{1,1},{2,10},{3,11},{4,20},{5,21},{6,30},{7,31},{8,2},{9,3},... | collective-permute-start | bytes 196616 | tf_op jit(solution)/shard_map/ppermute | solution.py:388
  63.0 6.5 %collective-permute-start.13 = (f32[64,256]{1,0:T(8,128)S(1)}, f32[64,256]{1,0:T(8,128)S(1)}, u32[]{:S(2)}, u32[]{:S(2)}) collective-permute-start(f32[64,256]{1,0:T(8,128)S(1)} %pad_maximum_fusion.1), channel_id=1, source_target_pairs={{0,1},{1,0},{2,11},{3,10},{4,21},{5,20},{6,31},{7,30},{8,3},{9,2},... | collective-permute-start | bytes 196616 | tf_op jit(solution)/shard_map/ppermute | solution.py:388
